TPU v7x, 128 devices: a whole 4x4x4 slice. The times are simulated.
128 devices in a mesh: kern: 8 (over z, x_lo), strip: 16 (over x_hi, y, core).
Axes of the slice: x: 4 (x_hi: 2, x_lo: 2; x = x_hi * 2 + x_lo), y: 4, z: 4, core: 2. Of those that a mesh axis runs over, the one named last changes fastest.
Arguments:
- mask: bfloat16 [512, 1024], P('strip'), may hold values from 0 to 1
- kernels: bfloat16 [72, 2, 33, 33], P('kern'), may hold values from -0.1875 to 0.1875
- eigen: float32 [72], replicated, may hold values from 0.05 to 1
- focus: int32 [72], replicated, may hold values from 0 to 2, as said below
- target: int32 [512, 1024], P('strip'), may hold values 0 or 1
- pixel_weight: float32 [512, 1024], P('strip'), may hold values from 0.3 to 3
- threshold: float32 [3], replicated, may hold values from 0.15 to 0.27
Outputs:
- gradient: float32 [512, 1024], P('strip', 'kern')
- resist: float32 [3, 512, 1024], P(None, 'strip', 'kern')
Inputs may be any that keep to these rules, and one draw needn't show every extreme that they name: Each of the three focus planes is named by exactly 24 systems.
All inputs are finite; a program needn't handle non-finite values. No bound on the sum of `target` on one device may be relied on, other than what follows from the above.
Results may differ from a plain program's by a relative error of at most 0.0019.
Values may be sent and summed in bfloat16 or wider, within the bound.
No kernel may reach another device: no remote copies, remote signals or barrier semaphores. Data moves between devices by JAX's collectives and lax.ppermute only.
A program may use at most 64 MiB of HBM per device.

v0:
```python
import jax
import jax.numpy as jnp
from jax import lax
from jax.sharding import PartitionSpec as P

STEEP = 20.0


def padded_2(cells, sides, width):
    for axis, dim in sides:
        count = lax.axis_size(axis)
        ends = count - 1
        head = lax.slice_in_dim(cells, 0, width, axis=dim)
        tail = lax.slice_in_dim(cells, cells.shape[dim] - width, cells.shape[dim], axis=dim)
        cells = jnp.concatenate(
            [
                lax.ppermute(tail, axis, [(i, (i + 1) % count) for i in range(ends)]),
                cells,
                lax.ppermute(head, axis, [((i + 1) % count, i) for i in range(ends)]),
            ],
            axis=dim,
        )
    return cells


def banded(rows_of_taps):
    extent = rows_of_taps.shape[0]
    padded = jnp.pad(rows_of_taps, ((0, 0), (0, 257 - rows_of_taps.shape[1])))
    repeated = jnp.tile(padded, (1, 128))
    shifted = repeated[:, : 128 * 256].reshape(extent, 128, 256)
    return jnp.transpose(shifted, (0, 2, 1))


def forward_taps(kernel_pair):
    return jnp.concatenate([banded(kernel_pair[0]), banded(kernel_pair[1])], axis=2)


def adjoint_taps(kernel_pair):
    flipped = kernel_pair[:, ::-1, ::-1]
    return jnp.concatenate([banded(flipped[0]), banded(flipped[1])], axis=1)


def windows(source, block_width):
    row_total = source.shape[0]
    out_width = source.shape[1] - block_width
    block_count = out_width // block_width
    leading = source[:, :out_width].reshape(row_total, block_count, block_width)
    trailing = source[:, block_width:].reshape(row_total, block_count, block_width)
    return jnp.concatenate([leading, trailing], axis=2)


def fields(frames, kernel_pair, row_count):
    taps = forward_taps(kernel_pair)
    summed = jnp.zeros((row_count, frames.shape[1], 256), jnp.float32)
    for offset in range(kernel_pair.shape[1]):
        summed = summed + jnp.einsum(
            "rjt,to->rjo",
            frames[offset : offset + row_count],
            taps[offset],
            preferred_element_type=jnp.float32,
        )
    out_cols = frames.shape[1] * 128
    real_part = summed[:, :, :128].reshape(row_count, out_cols)
    imag_part = summed[:, :, 128:].reshape(row_count, out_cols)
    return jnp.stack([real_part, imag_part])


def adjoint_sum(spread, kernel_pair, row_count):
    taps = adjoint_taps(kernel_pair)
    frames = jnp.concatenate([windows(spread[0], 128), windows(spread[1], 128)], axis=2)
    summed = jnp.zeros((row_count, frames.shape[1], 128), jnp.float32)
    for offset in range(kernel_pair.shape[1]):
        summed = summed + jnp.einsum(
            "rjt,to->rjo",
            frames[offset : offset + row_count],
            taps[offset],
            preferred_element_type=jnp.float32,
        )
    return summed.reshape(row_count, frames.shape[1] * 128)


def power_term(field, weight, plane_id):
    one_hot = (jnp.arange(3, dtype=jnp.int32) == plane_id).astype(jnp.float32)
    power = weight * (field[0] * field[0] + field[1] * field[1])
    return one_hot[:, None, None] * power[None]


def adjoint_field(field, slopes, weight, plane_id, norm_scale):
    one_hot = (jnp.arange(3, dtype=jnp.int32) == plane_id).astype(jnp.float32)
    chosen = jnp.sum(one_hot[:, None, None] * slopes, axis=0)
    factor = 2.0 * weight * norm_scale * chosen
    return (factor[None] * field).astype(jnp.bfloat16)


def resist_and_slope(intensity, threshold, target_part, weight_part):
    printed = jax.nn.sigmoid(STEEP * (intensity - threshold[:, None, None]))
    slopes = (
        weight_part[None] * 2.0 * (printed - target_part[None]) * STEEP * printed * (1.0 - printed)
    )
    return (printed, slopes)


def on_device(mask, kernels, eigen, focus, target, pixel_weight, threshold):
    row_count, col_count = mask.shape
    local_sys = kernels.shape[0]
    groups = lax.axis_size("kern")
    norm_scale = 3.0 / (local_sys * groups)
    margin = (kernels.shape[2] - 1) // 2
    col_share = col_count // groups
    col_start = lax.axis_index("kern") * col_share
    rimmed = padded_2(mask, (("strip", 0),), margin)
    extra = margin - margin
    first_sys = lax.axis_index("kern") * local_sys
    own_eigen = lax.dynamic_slice_in_dim(eigen, first_sys, local_sys)
    own_focus = lax.dynamic_slice_in_dim(focus, first_sys, local_sys)
    frames = windows(jnp.pad(rimmed, ((0, 0), (margin, 128 - margin))), 128)
    field_rows = row_count + 2 * extra

    def accumulate(running, record):
        field = fields(frames, record[0], field_rows)
        return (running + power_term(field, record[1], record[2]), field)

    empty_planes = jnp.zeros((3, row_count, col_count), jnp.float32)
    local_planes, stored = lax.scan(accumulate, empty_planes, (kernels, own_eigen, own_focus))
    intensity = norm_scale * lax.psum(local_planes, "kern")
    printed, slopes = resist_and_slope(
        intensity, threshold, target.astype(jnp.float32), pixel_weight
    )
    printed_share = lax.dynamic_slice_in_dim(printed, col_start, col_share, 2)

    def adjoin(running, record):
        adjoint = adjoint_field(record[3], slopes, record[1], record[2], norm_scale)
        spread = padded_2(adjoint, (("strip", 1),), margin)
        spread = jnp.pad(spread, ((0, 0), (0, 0), (margin, 128 - margin)))
        return (running + adjoint_sum(spread, record[0], row_count), None)

    empty_grad = jnp.zeros((row_count, col_count), jnp.float32)
    grad_full, _ = lax.scan(adjoin, empty_grad, (kernels, own_eigen, own_focus, stored))
    gradient = lax.psum_scatter(grad_full, "kern", scatter_dimension=1, tiled=True)
    return (gradient, printed_share)


def solution(mesh):
    placed = (
        P("strip", None),
        P("kern", None, None, None),
        P(),
        P(),
        P("strip", None),
        P("strip", None),
        P(),
    )
    return jax.shard_map(
        on_device,
        mesh=mesh,
        in_specs=placed,
        out_specs=(P("strip", "kern"), P(None, "strip", "kern")),
        check_vma=False,
    )
```

profile of v0, /device:TPU:0, one launch (start us, length us, event | category | flops | bytes accessed | tf_op | source)
XLA Modules:
  0.0 1039.0 jit_solution(14021219423686548054)
XLA Ops:
  15.4 396.9 %while.28 = (s32[]{:T(128)}, f32[3,32,1024]{2,1,0:T(8,128)}, f32[9,2,32,1024]{3,2,1,0:T(8,128)}, s32[9]{0:T(128)S(1)}, f32[9]{0:T(128)S(1)}, /*index=5*/bf16[9,2...) while((s32[]{:T(128)}, f32[3,32,1024]{2,1,0:T(8,128)}, ...), condition=%wide.region_1.2_spmd.clone, body=%wide.region_0.1_spmd.clone.sunk | while | flops 1118535680 | bytes 235013488 | solution.py:124
  16.5 5.9 tile.65
  31.4 7.6 tile.67
  60.6 5.9 tile.65
  75.5 7.6 tile.67
  104.7 5.9 tile.65
  119.5 7.6 tile.67
  148.7 5.9 tile.65
  163.6 7.6 tile.67
  192.8 5.9 tile.65
  207.7 7.6 tile.67
  236.9 5.9 tile.65
  251.8 7.6 tile.67
  281.0 5.9 tile.65
  295.9 7.6 tile.67
  325.2 5.9 tile.65
  340.0 7.6 tile.67
  369.2 5.9 tile.65
  384.1 7.6 tile.67
  414.2 80.0 %all-reduce.8.cloned.1.call-done = f32[3,32,1024]{2,1,0:T(8,128)} async-done(((f32[3,32,1024]{2,1,0:T(8,128)}), f32[3,32,1024]{2,1,0:T(8,128)}) %all-reduce.8.cloned.1.call-update) | async-done | bytes 393232 | tf_op jit(solution)/shard_map/psum | solution.py:125
  496.4 470.1 %while.29 = (s32[]{:T(128)}, f32[32,1024]{1,0:T(8,128)S(1)}, f32[9]{0:T(128)S(1)}, s32[9]{0:T(128)S(1)}, f32[3,32,1024]{2,1,0:T(8,128)}, /*index=5*/f32[9,2,32,1...) while((s32[]{:T(128)}, f32[32,1024]{1,0:T(8,128)S(1)}, ...), condition=%wide.region_5.6_spmd.clone, body=%wide.region_3.5_spmd.clone.sunk | while | flops 1119158272 | bytes 239707552 | solution.py:138
  507.7 5.9 tile.69
  522.6 7.6 tile.71
  534.2 4.2 copy.65
  559.4 5.9 tile.69
  574.3 7.6 tile.71
  606.4 4.3 collective-permute-start.1
  611.8 5.9 tile.69
  626.7 7.6 tile.71
  658.7 4.3 collective-permute-start.1
  664.2 5.9 tile.69
  679.1 7.6 tile.71
  711.1 4.3 collective-permute-start.1
  716.6 5.9 tile.69
  731.5 7.6 tile.71
  763.5 4.3 collective-permute-start.1
  768.9 5.9 tile.69
  783.9 7.6 tile.71
  815.9 4.3 collective-permute-start.1
  821.3 5.9 tile.69
  836.2 7.6 tile.71
  868.3 4.3 collective-permute-start.1
  873.7 5.9 tile.69
  888.6 7.6 tile.71
  920.6 4.3 collective-permute-start.1
  926.1 5.9 tile.69
  941.0 7.6 tile.71
  968.6 63.6 %reduce-scatter.2.cloned.1.call-done = f32[32,128]{1,0:T(8,128)} async-done(((f32[32,1024]{1,0:T(8,128)}), f32[32,128]{1,0:T(8,128)}) %reduce-scatter.2.cloned.1.call-update) | async-done | bytes 16400 | tf_op jit(solution)/shard_map/reduce_scatter | solution.py:139
  (1281 shorter events, 592.3 us)
Async XLA Ops:
  7.2 487.1 %all-reduce.8.cloned.1.call-start = ((), (), s32[]{:S(2)}) async-start(), calls=%async_computation.1 | async-start | bytes 786432 | tf_op jit(solution)/shard_map/psum | solution.py:125
  8.0 5.7 collective-permute-start.2
  9.3 5.0 collective-permute-start.3
  15.4 478.8 %copy-start.5 = (f32[3]{0:T(128)S(1)}, f32[3]{0:T(128)}, u32[]{:S(2)}) copy-start(f32[3]{0:T(128)} %param.17) | copy-start | bytes 40
  22.4 1.7 slice-start
  39.0 1.7 slice-start.1
  55.1 3.5 copy-start.2
  66.5 1.7 slice-start
  83.1 1.7 slice-start.1
  99.2 3.5 copy-start.2
  110.6 1.7 slice-start
  127.2 1.7 slice-start.1
  143.3 3.5 copy-start.2
  154.7 1.7 slice-start
  171.3 1.7 slice-start.1
  187.4 3.5 copy-start.2
  198.8 1.7 slice-start
  215.3 1.7 slice-start.1
  231.5 3.5 copy-start.2
  242.9 1.7 slice-start
  259.5 1.7 slice-start.1
  275.6 3.5 copy-start.2
  287.0 1.7 slice-start
  303.5 1.7 slice-start.1
  319.7 3.5 copy-start.2
  331.1 1.7 slice-start
  347.7 1.7 slice-start.1
  363.8 3.5 copy-start.2
  407.9 3.5 copy-start.2
  412.3 619.8 %reduce-scatter.2.cloned.1.call-start = ((), (), s32[]{:S(2)}) async-start(), calls=%async_computation.2 | async-start | bytes 147456 | tf_op jit(solution)/shard_map/reduce_scatter | solution.py:139
  501.6 36.7 %collective-permute-start = (bf16[2,16,1024]{2,1,0:T(8,128)(2,1)}, bf16[2,16,1024]{2,1,0:T(8,128)(2,1)}, u32[]{:S(2)}, u32[]{:S(2)}) collective-permute-start(bf16[2,16,1024]{2,1,0:T(8,128)(2,1)} %get-tuple-element.404), channel_id=1, source_target_pairs={{1,0},{2,1},{3,2},{4,3},{5,4},{6,5},{7,6},{8,7},{9,8},{10,9},{11,1... | collective-permute-start | bytes 196616 | tf_op jit(solution)/shard_map/while/body/eval_jaxpr/ppermute | solution.py:19
  502.9 35.4 %collective-permute-start.1 = (bf16[2,16,1024]{2,1,0:T(8,128)(2,1)}, bf16[2,16,1024]{2,1,0:T(8,128)(2,1)}, u32[]{:S(2)}, u32[]{:S(2)}) collective-permute-start(bf16[2,16,1024]{2,1,0:T(8,128)(2,1)} %get-tuple-element.405), channel_id=1, source_target_pairs={{0,1},{1,2},{2,3},{3,4},{4,5},{5,6},{6,7},{7,8},{8,9},{9,10},{10,1... | collective-permute-start | bytes 196616 | tf_op jit(solution)/shard_map/while/body/eval_jaxpr/ppermute | solution.py:17
  553.3 36.7 %collective-permute-start = (bf16[2,16,1024]{2,1,0:T(8,128)(2,1)}, bf16[2,16,1024]{2,1,0:T(8,128)(2,1)}, u32[]{:S(2)}, u32[]{:S(2)}) collective-permute-start(bf16[2,16,1024]{2,1,0:T(8,128)(2,1)} %get-tuple-element.404), channel_id=1, source_target_pairs={{1,0},{2,1},{3,2},{4,3},{5,4},{6,5},{7,6},{8,7},{9,8},{10,9},{11,1... | collective-permute-start | bytes 196616 | tf_op jit(solution)/shard_map/while/body/eval_jaxpr/ppermute | solution.py:19
  554.6 35.4 %collective-permute-start.1 = (bf16[2,16,1024]{2,1,0:T(8,128)(2,1)}, bf16[2,16,1024]{2,1,0:T(8,128)(2,1)}, u32[]{:S(2)}, u32[]{:S(2)}) collective-permute-start(bf16[2,16,1024]{2,1,0:T(8,128)(2,1)} %get-tuple-element.405), channel_id=1, source_target_pairs={{0,1},{1,2},{2,3},{3,4},{4,5},{5,6},{6,7},{7,8},{8,9},{9,10},{10,1... | collective-permute-start | bytes 196616 | tf_op jit(solution)/shard_map/while/body/eval_jaxpr/ppermute | solution.py:17
  605.1 37.4 %collective-permute-start = (bf16[2,16,1024]{2,1,0:T(8,128)(2,1)}, bf16[2,16,1024]{2,1,0:T(8,128)(2,1)}, u32[]{:S(2)}, u32[]{:S(2)}) collective-permute-start(bf16[2,16,1024]{2,1,0:T(8,128)(2,1)} %get-tuple-element.404), channel_id=1, source_target_pairs={{1,0},{2,1},{3,2},{4,3},{5,4},{6,5},{7,6},{8,7},{9,8},{10,9},{11,1... | collective-permute-start | bytes 196616 | tf_op jit(solution)/shard_map/while/body/eval_jaxpr/ppermute | solution.py:19
  606.4 36.1 %collective-permute-start.1 = (bf16[2,16,1024]{2,1,0:T(8,128)(2,1)}, bf16[2,16,1024]{2,1,0:T(8,128)(2,1)}, u32[]{:S(2)}, u32[]{:S(2)}) collective-permute-start(bf16[2,16,1024]{2,1,0:T(8,128)(2,1)} %get-tuple-element.405), channel_id=1, source_target_pairs={{0,1},{1,2},{2,3},{3,4},{4,5},{5,6},{6,7},{7,8},{8,9},{9,10},{10,1... | collective-permute-start | bytes 196616 | tf_op jit(solution)/shard_map/while/body/eval_jaxpr/ppermute | solution.py:17
  657.5 37.4 %collective-permute-start = (bf16[2,16,1024]{2,1,0:T(8,128)(2,1)}, bf16[2,16,1024]{2,1,0:T(8,128)(2,1)}, u32[]{:S(2)}, u32[]{:S(2)}) collective-permute-start(bf16[2,16,1024]{2,1,0:T(8,128)(2,1)} %get-tuple-element.404), channel_id=1, source_target_pairs={{1,0},{2,1},{3,2},{4,3},{5,4},{6,5},{7,6},{8,7},{9,8},{10,9},{11,1... | collective-permute-start | bytes 196616 | tf_op jit(solution)/shard_map/while/body/eval_jaxpr/ppermute | solution.py:19
  658.7 36.1 %collective-permute-start.1 = (bf16[2,16,1024]{2,1,0:T(8,128)(2,1)}, bf16[2,16,1024]{2,1,0:T(8,128)(2,1)}, u32[]{:S(2)}, u32[]{:S(2)}) collective-permute-start(bf16[2,16,1024]{2,1,0:T(8,128)(2,1)} %get-tuple-element.405), channel_id=1, source_target_pairs={{0,1},{1,2},{2,3},{3,4},{4,5},{5,6},{6,7},{7,8},{8,9},{9,10},{10,1... | collective-permute-start | bytes 196616 | tf_op jit(solution)/shard_map/while/body/eval_jaxpr/ppermute | solution.py:17
  709.8 37.4 %collective-permute-start = (bf16[2,16,1024]{2,1,0:T(8,128)(2,1)}, bf16[2,16,1024]{2,1,0:T(8,128)(2,1)}, u32[]{:S(2)}, u32[]{:S(2)}) collective-permute-start(bf16[2,16,1024]{2,1,0:T(8,128)(2,1)} %get-tuple-element.404), channel_id=1, source_target_pairs={{1,0},{2,1},{3,2},{4,3},{5,4},{6,5},{7,6},{8,7},{9,8},{10,9},{11,1... | collective-permute-start | bytes 196616 | tf_op jit(solution)/shard_map/while/body/eval_jaxpr/ppermute | solution.py:19
  711.1 36.1 %collective-permute-start.1 = (bf16[2,16,1024]{2,1,0:T(8,128)(2,1)}, bf16[2,16,1024]{2,1,0:T(8,128)(2,1)}, u32[]{:S(2)}, u32[]{:S(2)}) collective-permute-start(bf16[2,16,1024]{2,1,0:T(8,128)(2,1)} %get-tuple-element.405), channel_id=1, source_target_pairs={{0,1},{1,2},{2,3},{3,4},{4,5},{5,6},{6,7},{7,8},{8,9},{9,10},{10,1... | collective-permute-start | bytes 196616 | tf_op jit(solution)/shard_map/while/body/eval_jaxpr/ppermute | solution.py:17
  762.2 37.4 %collective-permute-start = (bf16[2,16,1024]{2,1,0:T(8,128)(2,1)}, bf16[2,16,1024]{2,1,0:T(8,128)(2,1)}, u32[]{:S(2)}, u32[]{:S(2)}) collective-permute-start(bf16[2,16,1024]{2,1,0:T(8,128)(2,1)} %get-tuple-element.404), channel_id=1, source_target_pairs={{1,0},{2,1},{3,2},{4,3},{5,4},{6,5},{7,6},{8,7},{9,8},{10,9},{11,1... | collective-permute-start | bytes 196616 | tf_op jit(solution)/shard_map/while/body/eval_jaxpr/ppermute | solution.py:19
  763.5 36.1 %collective-permute-start.1 = (bf16[2,16,1024]{2,1,0:T(8,128)(2,1)}, bf16[2,16,1024]{2,1,0:T(8,128)(2,1)}, u32[]{:S(2)}, u32[]{:S(2)}) collective-permute-start(bf16[2,16,1024]{2,1,0:T(8,128)(2,1)} %get-tuple-element.405), channel_id=1, source_target_pairs={{0,1},{1,2},{2,3},{3,4},{4,5},{5,6},{6,7},{7,8},{8,9},{9,10},{10,1... | collective-permute-start | bytes 196616 | tf_op jit(solution)/shard_map/while/body/eval_jaxpr/ppermute | solution.py:17
  814.6 37.4 %collective-permute-start = (bf16[2,16,1024]{2,1,0:T(8,128)(2,1)}, bf16[2,16,1024]{2,1,0:T(8,128)(2,1)}, u32[]{:S(2)}, u32[]{:S(2)}) collective-permute-start(bf16[2,16,1024]{2,1,0:T(8,128)(2,1)} %get-tuple-element.404), channel_id=1, source_target_pairs={{1,0},{2,1},{3,2},{4,3},{5,4},{6,5},{7,6},{8,7},{9,8},{10,9},{11,1... | collective-permute-start | bytes 196616 | tf_op jit(solution)/shard_map/while/body/eval_jaxpr/ppermute | solution.py:19
  815.9 36.1 %collective-permute-start.1 = (bf16[2,16,1024]{2,1,0:T(8,128)(2,1)}, bf16[2,16,1024]{2,1,0:T(8,128)(2,1)}, u32[]{:S(2)}, u32[]{:S(2)}) collective-permute-start(bf16[2,16,1024]{2,1,0:T(8,128)(2,1)} %get-tuple-element.405), channel_id=1, source_target_pairs={{0,1},{1,2},{2,3},{3,4},{4,5},{5,6},{6,7},{7,8},{8,9},{9,10},{10,1... | collective-permute-start | bytes 196616 | tf_op jit(solution)/shard_map/while/body/eval_jaxpr/ppermute | solution.py:17
  867.0 37.4 %collective-permute-start = (bf16[2,16,1024]{2,1,0:T(8,128)(2,1)}, bf16[2,16,1024]{2,1,0:T(8,128)(2,1)}, u32[]{:S(2)}, u32[]{:S(2)}) collective-permute-start(bf16[2,16,1024]{2,1,0:T(8,128)(2,1)} %get-tuple-element.404), channel_id=1, source_target_pairs={{1,0},{2,1},{3,2},{4,3},{5,4},{6,5},{7,6},{8,7},{9,8},{10,9},{11,1... | collective-permute-start | bytes 196616 | tf_op jit(solution)/shard_map/while/body/eval_jaxpr/ppermute | solution.py:19
  868.3 36.1 %collective-permute-start.1 = (bf16[2,16,1024]{2,1,0:T(8,128)(2,1)}, bf16[2,16,1024]{2,1,0:T(8,128)(2,1)}, u32[]{:S(2)}, u32[]{:S(2)}) collective-permute-start(bf16[2,16,1024]{2,1,0:T(8,128)(2,1)} %get-tuple-element.405), channel_id=1, source_target_pairs={{0,1},{1,2},{2,3},{3,4},{4,5},{5,6},{6,7},{7,8},{8,9},{9,10},{10,1... | collective-permute-start | bytes 196616 | tf_op jit(solution)/shard_map/while/body/eval_jaxpr/ppermute | solution.py:17
  919.3 37.4 %collective-permute-start = (bf16[2,16,1024]{2,1,0:T(8,128)(2,1)}, bf16[2,16,1024]{2,1,0:T(8,128)(2,1)}, u32[]{:S(2)}, u32[]{:S(2)}) collective-permute-start(bf16[2,16,1024]{2,1,0:T(8,128)(2,1)} %get-tuple-element.404), channel_id=1, source_target_pairs={{1,0},{2,1},{3,2},{4,3},{5,4},{6,5},{7,6},{8,7},{9,8},{10,9},{11,1... | collective-permute-start | bytes 196616 | tf_op jit(solution)/shard_map/while/body/eval_jaxpr/ppermute | solution.py:19
  920.6 36.1 %collective-permute-start.1 = (bf16[2,16,1024]{2,1,0:T(8,128)(2,1)}, bf16[2,16,1024]{2,1,0:T(8,128)(2,1)}, u32[]{:S(2)}, u32[]{:S(2)}) collective-permute-start(bf16[2,16,1024]{2,1,0:T(8,128)(2,1)} %get-tuple-element.405), channel_id=1, source_target_pairs={{0,1},{1,2},{2,3},{3,4},{4,5},{5,6},{6,7},{7,8},{8,9},{9,10},{10,1... | collective-permute-start | bytes 196616 | tf_op jit(solution)/shard_map/while/body/eval_jaxpr/ppermute | solution.py:17
  (48 other events, 72.1 us)
Sparse Core Ops, SparseCore 0:
  412.5 81.7 all-reduce.7
  967.3 64.8 reduce-scatter.1
where the time goes:
time: 1050 us; the launch traced here: 1040 us
  local copies, waits for them, and re-layouts  620 us (59%)
  waiting for transfers between devices  144 us (14%)
  matrix products  137 us (13%)
  other arithmetic  60.1 us (6%)
  starting transfers between devices  51.6 us (5%)
  between operations  14.2 us (1%)
  loops' own time  11.7 us (1%)
    another operation x72, local copies, waits for them, and re-layouts, banded(): repeated = jnp.tile(padded, (1, 128))  284 us
    reshape x72, local copies, waits for them, and re-layouts, banded(): shifted = repeated[:, :128 * 256].reshape(extent, 128, 256)  186 us
    psum x1, waiting for transfers between devices, on_device(): intensity = norm_scale * lax.psum(local_planes, 'kern')  80 us
    dot_general x297, matrix products, adjoint_sum(): jnp.einsum('rjt,to->rjo', frames[offset:offset + row_count], taps[offset]...  71.6 us
    dot_general x297, matrix products, fields(): jnp.einsum('rjt,to->rjo', frames[offset:offset + row_count], taps[offset]...  65.8 us
    reduce_scatter x1, waiting for transfers between devices, on_device(): lax.psum_scatter(grad_full, 'kern', scatter_dimension=1, tiled=True)  63.6 us
    slice x72, local copies, waits for them, and re-layouts, banded(): shifted = repeated[:, :128 * 256].reshape(extent, 128, 256)  62.6 us
    ppermute x10, starting transfers between devices, padded_2(): lax.ppermute(tail, axis, [(i, (i + 1) % count) for i in range(ends)])  38.7 us
  transfers between devices with their start and end apart: 22, of which 3 were waited for; matrix products, arithmetic and copies ran while one was open for 25% of the time, Pallas kernels for 0%

commit v1 on v0

v1 whole, which is shorter than its diff:
```python
import jax
import jax.numpy as jnp
from jax import lax
from jax.experimental import pallas as pl
from jax.experimental.pallas import tpu as pltpu
from jax.sharding import PartitionSpec as P

STEEP = 20.0
F32 = jnp.float32
BF16 = jnp.bfloat16


def iota(shape, dim):
    return lax.broadcasted_iota(jnp.int32, shape, dim)


def step_kernel(
    place_ref, thr_ref, fe_ref, own_ref, up_ref, down_ref, *rest
):
    blocks = rest[:8]
    grad_ref, resist_ref = rest[8:10]
    (rows_ref, lo_ref, hi_ref, main_t, side_t, e_ref, raw_ref, wf_ref, wt_ref, main_a, side_a,
     h_main, h_side, d_ref, tgt_main, tgt_side, res_main, res_side) = rest[10:]
    strip = place_ref[0]
    last = place_ref[1]
    norm_scale = 3.0 / 72

    has_up = (strip > 0).astype(F32)
    has_down = (strip < last).astype(F32)
    rows_ref[96:, :] = jnp.zeros((16, 256), F32)
    rows_ref[:, 128:] = jnp.zeros((112, 128), F32)
    rows_ref[0:32, 0:192] = up_ref[0:32, :] * has_up
    rows_ref[32:64, 0:192] = own_ref[0:32, :]
    rows_ref[64:96, 0:192] = down_ref[0:32, :] * has_down

    for kind in range(2):
        above = up_ref[pl.ds(32 + 16 * kind, 16), 0:160]
        below = down_ref[pl.ds(32 + 16 * kind, 16), 0:160]
        if kind == 1:
            above = above * has_up
            below = below * has_down
        mine = own_ref[pl.ds(32 + 32 * kind, 32), 0:160]
        area = jnp.concatenate([above, mine, below], axis=0)
        tgt_main[kind] = area[:, 0:128]
        tgt_side[kind] = jnp.concatenate(
            [area[8 * g : 8 * g + 8, 128:160] for g in range(8)], axis=1
        )

    lo_ref[...] = jnp.concatenate([rows_ref[8 * g : 8 * g + 56, 128:160] for g in range(8)], axis=1)
    hi_ref[...] = jnp.concatenate([rows_ref[8 * g : 8 * g + 56, 160:192] for g in range(8)], axis=1)

    tap = iota((32, 128), 0)
    lane = iota((32, 128), 1)

    def spread_main(block, _):
        eight = rows_ref[pl.ds(pl.multiple_of(block * 8, 8), 8), :]
        for j in range(8):
            r = block * 8 + j
            left = jnp.broadcast_to(eight[j : j + 1, 0:128], (32, 128))
            right = jnp.broadcast_to(eight[j : j + 1, 128:256], (32, 128))
            left = pltpu.roll(left, 97, 1, stride=1, stride_axis=0)
            right = pltpu.roll(right, 97, 1, stride=1, stride_axis=0)
            both = jnp.where(lane + 31 - tap < 128, left, right).astype(BF16)
            main_t[pl.ds(pl.multiple_of(r * 32 + 1024, 32), 32), 0:128] = both
            main_t[pl.ds(pl.multiple_of(r * 32, 32), 32), 128:256] = both
        return 0

    lax.fori_loop(0, 12, spread_main, 0)

    def spread_side(block, _):
        start = pl.multiple_of(block * 8, 8)
        lows, highs = lo_ref[pl.ds(start, 8), :], hi_ref[pl.ds(start, 8), :]
        for j in range(8):
            for half in range(2):
                cols = slice(128 * half, 128 * half + 128)
                low = jnp.broadcast_to(lows[j : j + 1, cols], (32, 128))
                high = jnp.broadcast_to(highs[j : j + 1, cols], (32, 128))
                low = pltpu.roll(low, 97, 1, stride=1, stride_axis=0)
                high = pltpu.roll(high, 1, 1, stride=1, stride_axis=0)
                both = jnp.where((lane & 31) <= tap, low, high).astype(BF16)
                side_t[pl.ds(pl.multiple_of((block * 8 + j) * 32, 32), 32), cols] = both
        return 0

    lax.fori_loop(0, 5, spread_side, 0)

    for w in range(32):
        e_ref[48 * w : 48 * w + 48, :] = jnp.concatenate(
            [rows_ref[w : w + 48, 32:160], rows_ref[w + 32 : w + 80, 32:160]], axis=1
        ).astype(BF16)
    for w in range(8):
        e_ref[48 * (32 + w) : 48 * (33 + w), :] = hi_ref[w : w + 48, :].astype(BF16)

    fe = fe_ref[...]
    fcol = jnp.transpose(fe)[:, 0:1]
    frow = fe[0:1, :]
    before = (fcol == frow) & (iota((256, 256), 0) < iota((256, 256), 1))
    rank = jnp.sum(jnp.where(before, 1.0, 0.0), axis=0, keepdims=True)
    pos = jnp.where(frow >= 0.0, frow * 48.0 + rank, -1.0)
    pick = jnp.where(iota((256, 256), 0).astype(F32) == pos, 1.0, 0.0)
    eig = jnp.sum(pick * fe[1:2, :], axis=1, keepdims=True)[0:144]
    scale = 2.0 * eig * norm_scale

    raw_ref[...] = jnp.zeros_like(raw_ref)
    for s in range(8):
        raw_ref[32 * s : 32 * s + 18, :] = blocks[s][...]
    taps_f = jnp.dot(pick.astype(BF16), raw_ref[...], preferred_element_type=F32)
    wt_ref[...] = jnp.transpose(taps_f).astype(BF16)
    x = iota((128, 128), 0)
    y = iota((128, 128), 1)
    turn = jnp.where(((x >> 5) == (y >> 5)) & ((x & 31) + (y & 31) == 31), 1.0, 0.0).astype(BF16)
    turn_last = jnp.where(
        ((x < 32) & (x + y == 31)) | ((x >= 32) & (x == y)), 1.0, 0.0
    ).astype(BF16)
    for c in range(9):
        piece = taps_f[0:144, 128 * c : 128 * c + 128].astype(BF16)
        wf_ref[:, 128 * c : 128 * c + 128] = jnp.dot(
            piece, turn_last if c == 8 else turn, preferred_element_type=F32
        ).astype(BF16)

    thr = jnp.concatenate([jnp.full((1, 256), thr_ref[f], F32) for f in range(3)], axis=0)

    def imaged(head, tail, tgt, wgt):
        field = jnp.dot(wf_ref[:, 0:1024], head, preferred_element_type=F32)
        field += jnp.dot(wf_ref[:, 1024:1104], tail, preferred_element_type=F32)
        power = eig * (field * field)
        planes = [
            jnp.sum(power[48 * f : 48 * f + 48], axis=0, keepdims=True) for f in range(3)
        ]
        intensity = norm_scale * jnp.concatenate(planes, axis=0)
        printed = 1.0 / (1.0 + jnp.exp(-STEEP * (intensity - thr)))
        slopes = wgt * 2.0 * (printed - tgt) * STEEP * printed * (1.0 - printed)
        adjoint = jnp.concatenate(
            [
                (scale[48 * f : 48 * f + 48] * slopes[f : f + 1]) * field[48 * f : 48 * f + 48]
                for f in range(3)
            ],
            axis=0,
        ).astype(BF16)
        return printed, adjoint

    def main_window(w, _):
        start = pl.multiple_of(w * 32 + 1024, 32)
        head = main_t[pl.ds(start, 1024), :]
        ones = e_ref[pl.ds(pl.multiple_of(w * 48, 16), 48), :]
        tail = jnp.concatenate([main_t[pl.ds(start + 1024, 32), :], ones], axis=0)
        tgt = jnp.concatenate(
            [tgt_main[0, pl.ds(w, 1), :], tgt_main[0, pl.ds(w + 32, 1), :]], axis=1
        )
        wgt = jnp.concatenate(
            [tgt_main[1, pl.ds(w, 1), :], tgt_main[1, pl.ds(w + 32, 1), :]], axis=1
        )
        printed, adjoint = imaged(head, tail, tgt, wgt)
        main_a[w] = adjoint[:, 0:128]
        main_a[w + 32] = adjoint[:, 128:256]
        for f in range(3):
            res_main[f, pl.ds(w, 1), :] = printed[f : f + 1, 0:128]
            res_main[f, pl.ds(w + 32, 1), :] = printed[f : f + 1, 128:256]
        return 0

    lax.fori_loop(0, 32, main_window, 0, unroll=2)

    for w in range(8):
        head = side_t[32 * w : 32 * w + 1024, :]
        ones = e_ref[1536 + 48 * w : 1584 + 48 * w, :]
        tail = jnp.concatenate([side_t[32 * w + 1024 : 32 * w + 1056, :], ones], axis=0)
        printed, adjoint = imaged(
            head, tail, tgt_side[0, w : w + 1, :], tgt_side[1, w : w + 1, :]
        )
        side_a[w] = adjoint
        for f in range(3):
            res_side[f, w : w + 1, :] = printed[f : f + 1, :]

    for f in range(3):
        edge = jnp.concatenate(
            [res_side[f, :, 32 * g : 32 * g + 16] for g in range(2, 6)], axis=0
        )
        resist_ref[f] = jnp.concatenate([res_main[f, 16:48, 16:128], edge], axis=1)

    h_main[...] = jnp.zeros_like(h_main)
    h_side[...] = jnp.zeros_like(h_side)
    d_ref[...] = jnp.zeros_like(d_ref)
    for p in range(32):
        i = 2 * p
        first, final = max(0, 31 - i), min(32, 63 - i)
        pair = jnp.concatenate([main_a[i], main_a[i + 1]], axis=1)
        spot = 32 * (i + first - 31)
        size = 32 * (final + 1 - first)
        h_main[spot : spot + size, :] += jnp.dot(
            wt_ref[32 * first : 32 * first + size, 0:144], pair, preferred_element_type=F32
        )
        d_ref[i : i + 48, :] += jnp.dot(
            wt_ref[1056:1104, 0:144], pair, preferred_element_type=F32
        )
    for w in range(8):
        h_side[32 * w : 32 * w + 1056, :] += jnp.dot(
            wt_ref[0:1056, 0:144], side_a[w], preferred_element_type=F32
        )

    group = lane >> 5
    for r in range(32):
        body = h_main[32 * r + 32 : 32 * r + 64, 0:128] + h_main[32 * r : 32 * r + 32, 128:256]
        edge = jnp.zeros((32, 128), F32)
        for g in range(8):
            u = r + 32 - 8 * g
            if 0 <= u <= 39:
                cols = slice(128 * (g // 4), 128 * (g // 4) + 128)
                edge += jnp.where(group == g % 4, h_side[32 * u : 32 * u + 32, cols], 0.0)
        edge = edge + pltpu.roll(edge, 64, 1)
        edge = edge + pltpu.roll(edge, 32, 1)
        body = pltpu.roll(body, 96, 1, stride=1, stride_axis=0)
        edge = pltpu.roll(edge, 96, 1, stride=1, stride_axis=0)
        both = jnp.where(lane + 32 - tap < 128, body, edge)
        grad_ref[r : r + 1, :] = (
            jnp.sum(both, axis=0, keepdims=True)
            + d_ref[r + 32 : r + 33, 0:128]
            + d_ref[r + 31 : r + 32, 128:256]
        )


def step_call(place, thr, fe, own, up, down, blocks):
    vmem = pl.BlockSpec(memory_space=pltpu.VMEM)
    smem = pl.BlockSpec(memory_space=pltpu.SMEM)
    return pl.pallas_call(
        step_kernel,
        out_shape=(
            jax.ShapeDtypeStruct((32, 128), F32),
            jax.ShapeDtypeStruct((3, 32, 128), F32),
        ),
        in_specs=[smem, smem] + [vmem] * 12,
        out_specs=(vmem, vmem),
        scratch_shapes=[
            pltpu.VMEM((112, 256), F32),
            pltpu.VMEM((56, 256), F32),
            pltpu.VMEM((56, 256), F32),
            pltpu.VMEM((4096, 256), BF16),
            pltpu.VMEM((1280, 256), BF16),
            pltpu.VMEM((1920, 256), BF16),
            pltpu.VMEM((256, 1152), BF16),
            pltpu.VMEM((144, 1152), BF16),
            pltpu.VMEM((1152, 256), BF16),
            pltpu.VMEM((64, 144, 128), BF16),
            pltpu.VMEM((8, 144, 256), BF16),
            pltpu.VMEM((1056, 256), F32),
            pltpu.VMEM((1280, 256), F32),
            pltpu.VMEM((112, 256), F32),
            pltpu.VMEM((2, 64, 128), F32),
            pltpu.VMEM((2, 8, 256), F32),
            pltpu.VMEM((3, 64, 128), F32),
            pltpu.VMEM((3, 8, 256), F32),
        ],
        compiler_params=pltpu.CompilerParams(vmem_limit_bytes=48 * 1024 * 1024),
    )(place, thr, fe, own, up, down, *blocks)


def flat_taps(kernels):
    count = kernels.shape[0] * 2
    pairs = kernels.reshape(count, 33, 33)
    return jnp.concatenate(
        [
            pairs[:, :, :32].reshape(count, 1056),
            pairs[:, :, 32],
            jnp.zeros((count, 63), BF16),
        ],
        axis=1,
    )


def on_device(mask, kernels, eigen, focus, target, pixel_weight, threshold):
    strips = lax.axis_size("strip")
    strip = lax.axis_index("strip")
    me = lax.axis_index("kern")
    taps = flat_taps(kernels)

    def columns(array, rim):
        wide = jnp.pad(array.astype(F32), ((0, 0), (rim, rim)))
        return lax.dynamic_slice_in_dim(wide, me * 128, 128 + 2 * rim, 1)

    mask_cols = columns(mask, 32)
    target_cols = jnp.pad(columns(target, 16), ((0, 0), (0, 32)))
    weight_cols = jnp.pad(columns(pixel_weight, 16), ((0, 0), (0, 32)))
    own = jnp.concatenate([mask_cols, target_cols, weight_cols], axis=0)
    to_next = jnp.concatenate([mask_cols, target_cols[16:], weight_cols[16:]], axis=0)
    to_prev = jnp.concatenate([mask_cols, target_cols[:16], weight_cols[:16]], axis=0)
    up = lax.ppermute(to_next, "strip", [(i, (i + 1) % strips) for i in range(strips)])
    down = lax.ppermute(to_prev, "strip", [((i + 1) % strips, i) for i in range(strips)])
    blocks = [taps] + [
        lax.ppermute(taps, "kern", [(i, i ^ s) for i in range(8)]) for s in range(1, 8)
    ]

    def reorder(values, fill):
        cube = values.reshape(2, 2, 2, 9)
        for axis, bit in ((0, 4), (1, 2), (2, 1)):
            cube = jnp.where((me & bit) > 0, jnp.flip(cube, axis), cube)
        both = jnp.repeat(cube.reshape(8, 9), 2, axis=1)
        return jnp.pad(both, ((0, 0), (0, 14)), constant_values=fill).reshape(1, 256)

    fe = jnp.concatenate(
        [reorder(focus.astype(F32), -1.0), reorder(eigen, 0.0), jnp.zeros((6, 256), F32)], axis=0
    )
    place = jnp.stack([strip, strip * 0 + strips - 1]).astype(jnp.int32)
    return step_call(place, threshold, fe, own, up, down, blocks)


def solution(mesh):
    placed = (
        P("strip", None),
        P("kern", None, None, None),
        P(),
        P(),
        P("strip", None),
        P("strip", None),
        P(),
    )
    return jax.shard_map(
        on_device,
        mesh=mesh,
        in_specs=placed,
        out_specs=(P("strip", "kern"), P(None, "strip", "kern")),
        check_vma=False,
    )
```

time: 1050 us -> 44.8 us (0.04); the launches traced: 1040 us -> 44.6 us
  local copies, waits for them, and re-layouts: 620 us -> 5.07 us
  matrix products: 137 us -> 0 us
  waiting for transfers between devices: 144 us -> 7.23 us
  other arithmetic: 60.1 us -> 0.3 us
  starting transfers between devices: 51.6 us -> 15.4 us
  Pallas kernels: 0 us -> 15.9 us
  between operations: 14.2 us -> 0.76 us
  loops' own time: 11.7 us -> 0 us
    another operation x72 -> x0, local copies, waits for them, and re-layouts: 284 us -> none  [banded(): repeated = jnp.tile(padded, (1, 128))]
    reshape x90 -> x9, local copies, waits for them, and re-layouts: 186 us -> 0.68 us  [the longest x4 0.2 us: reorder(): both = jnp.repeat(cube.reshape(8, 9), 2, axis=1)]
    dot_general x594 -> x0, matrix products: 137 us -> none  [the longest x297 71.6 us: adjoint_sum(): jnp.einsum('rjt,to->rjo', frames[offset:offset + row_count], taps[offset]...]
    psum x1 -> x0, waiting for transfers between devices: 80 us -> none  [on_device(): intensity = norm_scale * lax.psum(local_planes, 'kern')]
    slice x127 -> x2, local copies, waits for them, and re-layouts: 79.2 us -> 0.12 us  [the longest x1 0.11 us: flat_taps(): pairs[:, :, 32]]
    reduce_scatter x1 -> x0, waiting for transfers between devices: 63.6 us -> none  [on_device(): lax.psum_scatter(grad_full, 'kern', scatter_dimension=1, tiled=True)]
    while x180 -> x0, local copies, waits for them, and re-layouts: 36.4 us -> none
    ppermute x20 -> x9, starting transfers between devices: 51.5 us -> 15.4 us  [the longest x7 12.3 us: on_device(): lax.ppermute(taps, 'kern', [(i, i ^ s) for i in range(8)])]
  transfers between devices with their start and end apart: 22 -> 9, of which waited for: 3 -> 3; matrix products, arithmetic and copies ran while one was open for 25% -> 3% of each run, Pallas kernels for 0% -> 0%
where the time goes in v1:
time: 44.8 us; the launch traced here: 44.6 us
  Pallas kernels  15.9 us (35%)
  starting transfers between devices  15.4 us (34%)
  waiting for transfers between devices  7.23 us (16%)
  local copies, waits for them, and re-layouts  5.07 us (11%)
  between operations  0.76 us (2%)
    pallas_call x1, Pallas kernels, step_call(): pl.pallas_call(step_kernel, out_shape=(jax.ShapeDtypeStruct((32, 128), F3...  15.9 us
    ppermute x7, starting transfers between devices, on_device(): lax.ppermute(taps, 'kern', [(i, i ^ s) for i in range(8)])  12.3 us
    ppermute x1, waiting for transfers between devices, on_device(): lax.ppermute(to_next, 'strip', [(i, (i + 1) % strips) for i in range(stri...  5.4 us
    unnamed x16, local copies, waits for them, and re-layouts  3.84 us
    ppermute x1, starting transfers between devices, on_device(): lax.ppermute(to_prev, 'strip', [((i + 1) % strips, i) for i in range(stri...  3.12 us
    ppermute x1, waiting for transfers between devices, on_device(): lax.ppermute(to_prev, 'strip', [((i + 1) % strips, i) for i in range(stri...  1.52 us
  transfers between devices with their start and end apart: 9, of which 3 were waited for; matrix products, arithmetic and copies ran while one was open for 3% of the time, Pallas kernels for 0%

profile of v1, /device:TPU:0, one launch (start us, length us, event | category | flops | bytes accessed | tf_op | source)
XLA Modules:
  0.0 44.6 jit_solution(17585669948414740918)
XLA Ops:
  0.6 0.9 %copy.14 = bf16[9,2,33,33]{3,2,1,0:T(8,128)(2,1)S(1)} copy(bf16[9,2,33,33]{3,1,2,0:T(2,128)(2,1)} %param.8) | data formatting | bytes 78408 | tf_op args[1]
  1.6 0.1 slice.25
  1.7 0.2 reshape.43
  1.8 0.0 copy-start.2
  1.9 0.3 copy.16
  2.1 0.1 concatenate.19.rest_0_
  2.2 5.1 %collective-permute-start.8 = (bf16[18,1152]{1,0:T(8,128)(2,1)S(1)}, bf16[18,1152]{1,0:T(8,128)(2,1)S(1)}, u32[]{:S(2)}, u32[]{:S(2)}) collective-permute-start(bf16[18,1152]{1,0:T(8,128)(2,1)S(1)} %concatenate.19.rest_0_), channel_id=1, source_target_pairs={{0,112},{16,96},{32,80},{48,64},{64,48},{80,32},{96,16},{112,0},{1... | collective-permute-start | bytes 124424 | tf_op jit(solution)/shard_map/ppermute | solution.py:287
  7.3 0.0 collective-permute-start.7
  7.3 1.8 %collective-permute-start.6 = (bf16[18,1152]{1,0:T(8,128)(2,1)S(1)}, bf16[18,1152]{1,0:T(8,128)(2,1)S(1)}, u32[]{:S(2)}, u32[]{:S(2)}) collective-permute-start(bf16[18,1152]{1,0:T(8,128)(2,1)S(1)} %concatenate.19.rest_0_), channel_id=1, source_target_pairs={{0,80},{16,64},{32,112},{48,96},{64,16},{80,0},{96,48},{112,32},{1... | collective-permute-start | bytes 124424 | tf_op jit(solution)/shard_map/ppermute | solution.py:287
  9.2 1.8 %collective-permute-start.5 = (bf16[18,1152]{1,0:T(8,128)(2,1)S(1)}, bf16[18,1152]{1,0:T(8,128)(2,1)S(1)}, u32[]{:S(2)}, u32[]{:S(2)}) collective-permute-start(bf16[18,1152]{1,0:T(8,128)(2,1)S(1)} %concatenate.19.rest_0_), channel_id=1, source_target_pairs={{0,64},{16,80},{32,96},{48,112},{64,0},{80,16},{96,32},{112,48},{1... | collective-permute-start | bytes 124424 | tf_op jit(solution)/shard_map/ppermute | solution.py:287
  10.9 1.4 %collective-permute-start.4 = (bf16[18,1152]{1,0:T(8,128)(2,1)S(1)}, bf16[18,1152]{1,0:T(8,128)(2,1)S(1)}, u32[]{:S(2)}, u32[]{:S(2)}) collective-permute-start(bf16[18,1152]{1,0:T(8,128)(2,1)S(1)} %concatenate.19.rest_0_), channel_id=1, source_target_pairs={{0,48},{16,32},{32,16},{48,0},{64,112},{80,96},{96,80},{112,64},{1... | collective-permute-start | bytes 124424 | tf_op jit(solution)/shard_map/ppermute | solution.py:287
  12.3 0.0 copy-done.2
  12.3 0.0 copy-start.1
  12.3 0.9 %copy-done.1 = f32[32,1024]{1,0:T(8,128)S(1)} copy-done((f32[32,1024]{1,0:T(8,128)S(1)}, f32[32,1024]{1,0:T(8,128)}, u32[]{:S(2)}) %copy-start.1) | copy-done | bytes 131096
  13.2 0.1 pad_dynamic-slice_fusion
  13.3 0.1 pad_dynamic-slice_fusion.1
  13.4 0.0 copy-start.5
  13.4 0.6 %copy-done.5 = s32[72]{0:T(128)S(1)} copy-done((s32[72]{0:T(128)S(1)}, s32[72]{0:T(128)}, u32[]{:S(2)}) %copy-start.5) | copy-done | bytes 312
  14.1 0.0 copy-start.4
  14.1 0.1 reshape.34
  14.2 0.6 %copy-done.4 = f32[72]{0:T(128)S(1)} copy-done((f32[72]{0:T(128)S(1)}, f32[72]{0:T(128)}, u32[]{:S(2)}) %copy-start.4) | copy-done | bytes 312
  14.8 0.1 reshape.38
  14.9 0.1 copy.12
  15.0 0.1 copy.18
  15.1 0.1 reshape.41
  15.2 0.1 copy.10
  15.3 0.1 copy.17
  15.4 0.1 reshape.37
  15.5 0.1 pad.47.clone
  15.6 0.4 copy-done.3
  15.9 0.1 fusion.2
  16.0 0.1 maximum_maximum_fusion.fe_ref
  16.1 0.0 collective-permute-done.8.rest_7_
  16.1 1.5 %collective-permute-start.3 = (bf16[18,1152]{1,0:T(8,128)(2,1)S(1)}, bf16[18,1152]{1,0:T(8,128)(2,1)S(1)}, u32[]{:S(2)}, u32[]{:S(2)}) collective-permute-start(bf16[18,1152]{1,0:T(8,128)(2,1)S(1)} %concatenate.19.rest_0_), channel_id=1, source_target_pairs={{0,32},{16,48},{32,0},{48,16},{64,96},{80,112},{96,64},{112,80},{1... | collective-permute-start | bytes 124424 | tf_op jit(solution)/shard_map/ppermute | solution.py:287
  17.7 0.0 collective-permute-done.7.rest_6_
  17.7 0.7 %collective-permute-start.2 = (bf16[18,1152]{1,0:T(8,128)(2,1)S(1)}, bf16[18,1152]{1,0:T(8,128)(2,1)S(1)}, u32[]{:S(2)}, u32[]{:S(2)}) collective-permute-start(bf16[18,1152]{1,0:T(8,128)(2,1)S(1)} %concatenate.19.rest_0_), channel_id=1, source_target_pairs={{0,16},{16,0},{32,48},{48,32},{64,80},{80,64},{96,112},{112,96},{1... | collective-permute-start | bytes 124424 | tf_op jit(solution)/shard_map/ppermute | solution.py:287
  18.3 0.0 collective-permute-done.6.rest_5_
  18.3 3.1 %collective-permute-start.1 = (f32[64,192]{1,0:T(8,128)S(1)}, f32[64,192]{1,0:T(8,128)S(1)}, u32[]{:S(2)}, u32[]{:S(2)}) collective-permute-start(f32[64,192]{1,0:T(8,128)S(1)} %get-tuple-element.2), channel_id=1, source_target_pairs={{1,0},{2,1},{3,2},{4,3},{5,4},{6,5},{7,6},{8,7},{9,8},{10,9},{11,1... | collective-permute-start | bytes 147464 | tf_op jit(solution)/shard_map/ppermute | solution.py:285
  21.4 0.0 collective-permute-done.5.rest_4_
  21.5 0.0 collective-permute-start
  21.5 0.1 pad_add_fusion.place_ref
  21.5 0.0 collective-permute-done.4.rest_3_
  21.5 0.0 collective-permute-done.3.rest_2_
  21.5 0.3 collective-permute-done.2.rest_1_
  21.8 1.5 %collective-permute-done.1.down_ref = f32[64,192]{1,0:T(8,128)S(1)} collective-permute-done((f32[64,192]{1,0:T(8,128)S(1)}, f32[64,192]{1,0:T(8,128)S(1)}, u32[]{:S(2)}, u32[]{:S(2)}) %collective-permute-start.1) | collective-permute-done | bytes 49184 | tf_op jit(solution)/shard_map/ppermute | solution.py:285
  23.4 5.4 %collective-permute-done.up_ref = f32[64,192]{1,0:T(8,128)S(1)} collective-permute-done((f32[64,192]{1,0:T(8,128)S(1)}, f32[64,192]{1,0:T(8,128)S(1)}, u32[]{:S(2)}, u32[]{:S(2)}) %collective-permute-start) | collective-permute-done | bytes 49184 | tf_op jit(solution)/shard_map/ppermute | solution.py:284
  28.8 0.0 copy-done
  28.8 15.9 %shard_map.86 = (f32[32,128]{1,0:T(8,128)}, f32[3,32,128]{2,1,0:T(8,128)}) custom-call(s32[2]{0:T(128)S(1)} %pad_add_fusion.place_ref, f32[3]{0:T(128)S(1)} %copy-done, f32[8,256]{1,0:T(8,128)S(1)} %maximum_maximum_fusion.fe_ref, f32[96,192]{1,0:T(8,128)S(1)} %pad_maximum_fusion.own_ref, f32[64,192]{1,0:T(8,128)S(1)} %collective-permute-done.up_ref, ...), custom_call_target="tpu_custom_call" | custom-call | tf_op jit(solution)/shard_map/pallas_call | solution.py:223
  (24 shorter events, 0.2 us)
Async XLA Ops:
  1.8 10.5 %copy-start.2 = (s32[32,1024]{1,0:T(8,128)S(1)}, s32[32,1024]{1,0:T(8,128)}, u32[]{:S(2)}) copy-start(s32[32,1024]{1,0:T(8,128)} %param.11) | copy-start | bytes 393220
  2.2 13.9 %collective-permute-start.8 = (bf16[18,1152]{1,0:T(8,128)(2,1)S(1)}, bf16[18,1152]{1,0:T(8,128)(2,1)S(1)}, u32[]{:S(2)}, u32[]{:S(2)}) collective-permute-start(bf16[18,1152]{1,0:T(8,128)(2,1)S(1)} %concatenate.19.rest_0_), channel_id=1, source_target_pairs={{0,112},{16,96},{32,80},{48,64},{64,48},{80,32},{96,16},{112,0},{1... | collective-permute-start | bytes 124424 | tf_op jit(solution)/shard_map/ppermute | solution.py:287
  7.3 10.4 %collective-permute-start.7 = (bf16[18,1152]{1,0:T(8,128)(2,1)S(1)}, bf16[18,1152]{1,0:T(8,128)(2,1)S(1)}, u32[]{:S(2)}, u32[]{:S(2)}) collective-permute-start(bf16[18,1152]{1,0:T(8,128)(2,1)S(1)} %concatenate.19.rest_0_), channel_id=1, source_target_pairs={{0,96},{16,112},{32,64},{48,80},{64,32},{80,48},{96,0},{112,16},{1... | collective-permute-start | bytes 124424 | tf_op jit(solution)/shard_map/ppermute | solution.py:287
  7.3 11.0 %collective-permute-start.6 = (bf16[18,1152]{1,0:T(8,128)(2,1)S(1)}, bf16[18,1152]{1,0:T(8,128)(2,1)S(1)}, u32[]{:S(2)}, u32[]{:S(2)}) collective-permute-start(bf16[18,1152]{1,0:T(8,128)(2,1)S(1)} %concatenate.19.rest_0_), channel_id=1, source_target_pairs={{0,80},{16,64},{32,112},{48,96},{64,16},{80,0},{96,48},{112,32},{1... | collective-permute-start | bytes 124424 | tf_op jit(solution)/shard_map/ppermute | solution.py:287
  9.2 12.3 %collective-permute-start.5 = (bf16[18,1152]{1,0:T(8,128)(2,1)S(1)}, bf16[18,1152]{1,0:T(8,128)(2,1)S(1)}, u32[]{:S(2)}, u32[]{:S(2)}) collective-permute-start(bf16[18,1152]{1,0:T(8,128)(2,1)S(1)} %concatenate.19.rest_0_), channel_id=1, source_target_pairs={{0,64},{16,80},{32,96},{48,112},{64,0},{80,16},{96,32},{112,48},{1... | collective-permute-start | bytes 124424 | tf_op jit(solution)/shard_map/ppermute | solution.py:287
  10.9 10.6 %collective-permute-start.4 = (bf16[18,1152]{1,0:T(8,128)(2,1)S(1)}, bf16[18,1152]{1,0:T(8,128)(2,1)S(1)}, u32[]{:S(2)}, u32[]{:S(2)}) collective-permute-start(bf16[18,1152]{1,0:T(8,128)(2,1)S(1)} %concatenate.19.rest_0_), channel_id=1, source_target_pairs={{0,48},{16,32},{32,16},{48,0},{64,112},{80,96},{96,80},{112,64},{1... | collective-permute-start | bytes 124424 | tf_op jit(solution)/shard_map/ppermute | solution.py:287
  12.3 0.9 %copy-start.1 = (f32[32,1024]{1,0:T(8,128)S(1)}, f32[32,1024]{1,0:T(8,128)}, u32[]{:S(2)}) copy-start(f32[32,1024]{1,0:T(8,128)} %param.12) | copy-start | bytes 393220
  13.4 0.7 %copy-start.5 = (s32[72]{0:T(128)S(1)}, s32[72]{0:T(128)}, u32[]{:S(2)}) copy-start(s32[72]{0:T(128)} %param.10) | copy-start | bytes 868
  14.1 0.7 %copy-start.4 = (f32[72]{0:T(128)S(1)}, f32[72]{0:T(128)}, u32[]{:S(2)}) copy-start(f32[72]{0:T(128)} %param.9) | copy-start | bytes 868
  15.1 0.8 %copy-start.3 = (bf16[32,1024]{1,0:T(8,128)(2,1)S(1)}, bf16[32,1024]{1,0:T(8,128)(2,1)}, u32[]{:S(2)}) copy-start(bf16[32,1024]{1,0:T(8,128)(2,1)} %param.7) | copy-start | bytes 196612
  16.1 5.4 %collective-permute-start.3 = (bf16[18,1152]{1,0:T(8,128)(2,1)S(1)}, bf16[18,1152]{1,0:T(8,128)(2,1)S(1)}, u32[]{:S(2)}, u32[]{:S(2)}) collective-permute-start(bf16[18,1152]{1,0:T(8,128)(2,1)S(1)} %concatenate.19.rest_0_), channel_id=1, source_target_pairs={{0,32},{16,48},{32,0},{48,16},{64,96},{80,112},{96,64},{112,80},{1... | collective-permute-start | bytes 124424 | tf_op jit(solution)/shard_map/ppermute | solution.py:287
  17.7 4.2 %collective-permute-start.2 = (bf16[18,1152]{1,0:T(8,128)(2,1)S(1)}, bf16[18,1152]{1,0:T(8,128)(2,1)S(1)}, u32[]{:S(2)}, u32[]{:S(2)}) collective-permute-start(bf16[18,1152]{1,0:T(8,128)(2,1)S(1)} %concatenate.19.rest_0_), channel_id=1, source_target_pairs={{0,16},{16,0},{32,48},{48,32},{64,80},{80,64},{96,112},{112,96},{1... | collective-permute-start | bytes 124424 | tf_op jit(solution)/shard_map/ppermute | solution.py:287
  18.3 5.0 %collective-permute-start.1 = (f32[64,192]{1,0:T(8,128)S(1)}, f32[64,192]{1,0:T(8,128)S(1)}, u32[]{:S(2)}, u32[]{:S(2)}) collective-permute-start(f32[64,192]{1,0:T(8,128)S(1)} %get-tuple-element.2), channel_id=1, source_target_pairs={{1,0},{2,1},{3,2},{4,3},{5,4},{6,5},{7,6},{8,7},{9,8},{10,9},{11,1... | collective-permute-start | bytes 147464 | tf_op jit(solution)/shard_map/ppermute | solution.py:285
  21.5 7.3 %collective-permute-start = (f32[64,192]{1,0:T(8,128)S(1)}, f32[64,192]{1,0:T(8,128)S(1)}, u32[]{:S(2)}, u32[]{:S(2)}) collective-permute-start(f32[64,192]{1,0:T(8,128)S(1)} %get-tuple-element.3), channel_id=1, source_target_pairs={{0,1},{1,2},{2,3},{3,4},{4,5},{5,6},{6,7},{7,8},{8,9},{9,10},{10,1... | collective-permute-start | bytes 147464 | tf_op jit(solution)/shard_map/ppermute | solution.py:284
  21.5 7.3 %copy-start = (f32[3]{0:T(128)S(1)}, f32[3]{0:T(128)}, u32[]{:S(2)}) copy-start(f32[3]{0:T(128)} %thr_ref.1) | copy-start | bytes 40

commit v2 on v1

v2 whole, which is shorter than its diff:
```python
import jax
import jax.numpy as jnp
from jax import lax
from jax.experimental import pallas as pl
from jax.experimental.pallas import tpu as pltpu
from jax.sharding import PartitionSpec as P

STEEP = 20.0
F32 = jnp.float32
BF16 = jnp.bfloat16


def iota(shape, dim):
    return lax.broadcasted_iota(jnp.int32, shape, dim)


def spread_kernel(
    place_ref, fe_ref, own_ref, up_ref, down_ref,
    main_t, side_t, e_ref, tgt_main, tgt_side, pick_ref, eig_ref, rows_ref, lo_ref, hi_ref,
):
    strip = place_ref[0]
    last = place_ref[1]

    has_up = (strip > 0).astype(F32)
    has_down = (strip < last).astype(F32)
    rows_ref[96:, :] = jnp.zeros((16, 256), F32)
    rows_ref[:, 128:] = jnp.zeros((112, 128), F32)
    rows_ref[0:32, 0:192] = up_ref[:, 0:192] * has_up
    rows_ref[32:64, 0:192] = own_ref[0:32, :]
    rows_ref[64:96, 0:192] = down_ref[:, 0:192] * has_down

    for kind in range(2):
        above = up_ref[16 * kind : 16 * kind + 16, 192:352]
        below = down_ref[16 * kind : 16 * kind + 16, 192:352]
        if kind == 1:
            above = above * has_up
            below = below * has_down
        mine = own_ref[32 + 32 * kind : 64 + 32 * kind, 0:160]
        area = jnp.concatenate([above, mine, below], axis=0)
        tgt_main[kind] = area[:, 0:128]
        tgt_side[kind] = jnp.concatenate(
            [area[8 * g : 8 * g + 8, 128:160] for g in range(8)], axis=1
        )

    lo_ref[...] = jnp.concatenate([rows_ref[8 * g : 8 * g + 56, 128:160] for g in range(8)], axis=1)
    hi_ref[...] = jnp.concatenate([rows_ref[8 * g : 8 * g + 56, 160:192] for g in range(8)], axis=1)

    tap = iota((32, 128), 0)
    lane = iota((32, 128), 1)

    def spread_main(block, _, to_left, to_right):
        eight = rows_ref[pl.ds(pl.multiple_of(block * 8, 8), 8), :]
        for j in range(8):
            r = block * 8 + j
            left = jnp.broadcast_to(eight[j : j + 1, 0:128], (32, 128))
            right = jnp.broadcast_to(eight[j : j + 1, 128:256], (32, 128))
            left = pltpu.roll(left, 97, 1, stride=1, stride_axis=0)
            right = pltpu.roll(right, 97, 1, stride=1, stride_axis=0)
            both = jnp.where(lane + 31 - tap < 128, left, right).astype(BF16)
            if to_left:
                main_t[pl.ds(pl.multiple_of(r * 32, 32), 32), 0:128] = both
            if to_right:
                main_t[pl.ds(pl.multiple_of(r * 32 - 1024, 32), 32), 128:256] = both
        return 0

    for span in range(3):
        lax.fori_loop(
            4 * span,
            4 * span + 4,
            lambda block, c: spread_main(block, c, span < 2, span > 0),
            0,
        )

    def spread_side(block, _):
        start = pl.multiple_of(block * 8, 8)
        lows, highs = lo_ref[pl.ds(start, 8), :], hi_ref[pl.ds(start, 8), :]
        for j in range(8):
            for half in range(2):
                cols = slice(128 * half, 128 * half + 128)
                low = jnp.broadcast_to(lows[j : j + 1, cols], (32, 128))
                high = jnp.broadcast_to(highs[j : j + 1, cols], (32, 128))
                low = pltpu.roll(low, 97, 1, stride=1, stride_axis=0)
                high = pltpu.roll(high, 1, 1, stride=1, stride_axis=0)
                both = jnp.where((lane & 31) <= tap, low, high).astype(BF16)
                side_t[pl.ds(pl.multiple_of((block * 8 + j) * 32, 32), 32), cols] = both
        return 0

    lax.fori_loop(0, 5, spread_side, 0)

    for m in range(8):
        e_ref[48 * m : 48 * m + 48, :] = jnp.concatenate(
            [rows_ref[4 * m : 4 * m + 48, 32:160], rows_ref[4 * m + 32 : 4 * m + 80, 32:160]], axis=1
        ).astype(BF16)
    for m in range(2):
        e_ref[48 * (8 + m) : 48 * (9 + m), :] = hi_ref[4 * m : 4 * m + 48, :].astype(BF16)

    fe = fe_ref[...]
    fcol = jnp.transpose(fe)[:, 0:1]
    frow = fe[0:1, :]
    before = (fcol == frow) & (iota((256, 256), 0) < iota((256, 256), 1))
    rank = jnp.sum(jnp.where(before, 1.0, 0.0), axis=0, keepdims=True)
    pos = jnp.where(frow >= 0.0, frow * 48.0 + rank, -1.0)
    pick = jnp.where(iota((256, 256), 0).astype(F32) == pos, 1.0, 0.0)
    pick_ref[...] = pick.astype(BF16)
    eig = jnp.sum(pick * fe[1:2, :], axis=1, keepdims=True)[0:144]
    eig_ref[...] = jnp.broadcast_to(eig, (144, 128))


def step_kernel(
    thr_ref, main_t, side_t, e_ref, tgt_main, tgt_side, pick_ref, eig_ref, four_ref, other_ref,
    grad_ref, resist_ref,
    raw_ref, wf_ref, wt_ref, main_a, side_a, h_main, h_side, d_ref, res_main, res_side,
):
    norm_scale = 3.0 / 72
    tap = iota((32, 128), 0)
    lane = iota((32, 128), 1)
    eig = eig_ref[:, 0:1]

    raw_ref[...] = jnp.zeros_like(raw_ref)
    for s in range(4):
        raw_ref[32 * s : 32 * s + 18, :] = four_ref[s]
        raw_ref[32 * s + 128 : 32 * s + 146, :] = other_ref[s]
    taps_f = jnp.dot(pick_ref[...], raw_ref[...], preferred_element_type=F32)
    wt_ref[...] = jnp.transpose(taps_f).astype(BF16)
    x = iota((128, 128), 0)
    y = iota((128, 128), 1)
    turn = jnp.where(((x >> 5) == (y >> 5)) & ((x & 31) + (y & 31) == 31), 1.0, 0.0).astype(BF16)
    turn_last = jnp.where(
        ((x < 32) & (x + y == 31)) | ((x >= 32) & (x == y)), 1.0, 0.0
    ).astype(BF16)
    turned = [
        jnp.dot(
            taps_f[0:144, 128 * c : 128 * c + 128].astype(BF16),
            turn_last if c == 8 else turn,
            preferred_element_type=F32,
        )
        for c in range(9)
    ]
    lane_w = iota((144, 128), 1)
    final = pltpu.roll(turned[8], 96, 1)
    final = jnp.where(lane_w < 33, final, 0.0)
    turned[8] = jnp.where(lane_w < 32, turned[8], 0.0)
    base = jnp.concatenate(turned, axis=1)
    for w in range(4):
        wf_ref[144 * w : 144 * w + 144, 0:1152] = (
            pltpu.roll(base, 32 * w, 1) if w else base
        ).astype(BF16)
        wf_ref[144 * w : 144 * w + 144, 1152:1280] = (
            pltpu.roll(final, w, 1) if w else final
        ).astype(BF16)

    thr = jnp.concatenate([jnp.full((1, 256), thr_ref[f], F32) for f in range(3)] * 4, axis=0)
    eigs = jnp.concatenate([eig] * 4, axis=0)
    scales = 2.0 * eigs * norm_scale

    def imaged(source, start, ones, tgt, wgt):
        field = jnp.dot(
            wf_ref[:, 0:1024], source[start : start + 1024, :], preferred_element_type=F32
        )
        tail = jnp.concatenate([source[start + 1024 : start + 1152, :], ones], axis=0)
        field += jnp.dot(wf_ref[:, 1024:1200], tail, preferred_element_type=F32)
        power = eigs * (field * field)
        planes = jnp.sum(power.reshape(12, 48, 256), axis=1)
        printed = 1.0 / (1.0 + jnp.exp(-STEEP * (norm_scale * planes - thr)))
        tgt = jnp.concatenate([tgt[v // 3 : v // 3 + 1] for v in range(12)], axis=0)
        wgt = jnp.concatenate([wgt[v // 3 : v // 3 + 1] for v in range(12)], axis=0)
        slopes = wgt * 2.0 * (printed - tgt) * STEEP * printed * (1.0 - printed)
        adjoint = (scales.reshape(12, 48, 1) * slopes[:, None, :]) * field.reshape(12, 48, 256)
        return printed, adjoint.reshape(4, 144, 256).astype(BF16)

    for m in range(8):
        both = [
            jnp.concatenate(
                [tgt_main[kind, 4 * m : 4 * m + 4, :], tgt_main[kind, 4 * m + 32 : 4 * m + 36, :]],
                axis=1,
            )
            for kind in range(2)
        ]
        ones = e_ref[48 * m : 48 * m + 48, :]
        printed, adjoint = imaged(main_t, 128 * m, ones, *both)
        main_a[4 * m : 4 * m + 4] = adjoint[:, :, 0:128]
        main_a[4 * m + 32 : 4 * m + 36] = adjoint[:, :, 128:256]
        for v in range(12):
            w = 4 * m + v // 3
            res_main[v % 3, w : w + 1, :] = printed[v : v + 1, 0:128]
            res_main[v % 3, w + 32 : w + 33, :] = printed[v : v + 1, 128:256]

    for m in range(2):
        both = [tgt_side[kind, 4 * m : 4 * m + 4, :] for kind in range(2)]
        ones = e_ref[48 * (8 + m) : 48 * (9 + m), :]
        printed, adjoint = imaged(side_t, 128 * m, ones, *both)
        side_a[4 * m : 4 * m + 4] = adjoint
        for v in range(12):
            w = 4 * m + v // 3
            res_side[v % 3, w : w + 1, :] = printed[v : v + 1, :]

    for f in range(3):
        edge = jnp.concatenate(
            [res_side[f, :, 32 * g : 32 * g + 16] for g in range(2, 6)], axis=0
        )
        resist_ref[f] = jnp.concatenate([res_main[f, 16:48, 16:128], edge], axis=1)

    h_main[...] = jnp.zeros_like(h_main)
    h_side[...] = jnp.zeros_like(h_side)
    d_ref[...] = jnp.zeros_like(d_ref)
    for p in range(32):
        i = 2 * p
        first, final = max(0, 31 - i), min(32, 63 - i)
        pair = jnp.concatenate([main_a[i], main_a[i + 1]], axis=1)
        spot = 32 * (i + first - 31)
        size = 32 * (final + 1 - first)
        h_main[spot : spot + size, :] += jnp.dot(
            wt_ref[32 * first : 32 * first + size, 0:144], pair, preferred_element_type=F32
        )
        d_ref[i : i + 48, :] += jnp.dot(
            wt_ref[1056:1104, 0:144], pair, preferred_element_type=F32
        )
    for w in range(8):
        h_side[32 * w : 32 * w + 1056, :] += jnp.dot(
            wt_ref[0:1056, 0:144], side_a[w], preferred_element_type=F32
        )

    group = lane >> 5
    for r in range(32):
        body = h_main[32 * r + 32 : 32 * r + 64, 0:128] + h_main[32 * r : 32 * r + 32, 128:256]
        edge = jnp.zeros((32, 128), F32)
        for g in range(8):
            u = r + 32 - 8 * g
            if 0 <= u <= 39:
                cols = slice(128 * (g // 4), 128 * (g // 4) + 128)
                edge += jnp.where(group == g % 4, h_side[32 * u : 32 * u + 32, cols], 0.0)
        edge = edge + pltpu.roll(edge, 64, 1)
        edge = edge + pltpu.roll(edge, 32, 1)
        body = pltpu.roll(body, 96, 1, stride=1, stride_axis=0)
        edge = pltpu.roll(edge, 96, 1, stride=1, stride_axis=0)
        both = jnp.where(lane + 32 - tap < 128, body, edge)
        grad_ref[r : r + 1, :] = (
            jnp.sum(both, axis=0, keepdims=True)
            + d_ref[r + 32 : r + 33, 0:128]
            + d_ref[r + 31 : r + 32, 128:256]
        )


VMEM_SPEC = pl.BlockSpec(memory_space=pltpu.VMEM)
SMEM_SPEC = pl.BlockSpec(memory_space=pltpu.SMEM)
BIG = 40 * 1024 * 1024


def spread_call(place, fe, own, up, down):
    return pl.pallas_call(
        spread_kernel,
        out_shape=(
            jax.ShapeDtypeStruct((2048, 256), BF16),
            jax.ShapeDtypeStruct((1280, 256), BF16),
            jax.ShapeDtypeStruct((480, 256), BF16),
            jax.ShapeDtypeStruct((2, 64, 128), F32),
            jax.ShapeDtypeStruct((2, 8, 256), F32),
            jax.ShapeDtypeStruct((256, 256), BF16),
            jax.ShapeDtypeStruct((144, 128), F32),
        ),
        in_specs=[SMEM_SPEC] + [VMEM_SPEC] * 4,
        out_specs=(VMEM_SPEC,) * 7,
        scratch_shapes=[
            pltpu.VMEM((112, 256), F32),
            pltpu.VMEM((56, 256), F32),
            pltpu.VMEM((56, 256), F32),
        ],
        cost_estimate=pl.CostEstimate(flops=2**31, bytes_accessed=2**21, transcendentals=0),
        compiler_params=pltpu.CompilerParams(vmem_limit_bytes=16 * 1024 * 1024),
    )(place, fe, own, up, down)


def step_call(thr, spread, four, other):
    return pl.pallas_call(
        step_kernel,
        out_shape=(
            jax.ShapeDtypeStruct((32, 128), F32),
            jax.ShapeDtypeStruct((3, 32, 128), F32),
        ),
        in_specs=[SMEM_SPEC] + [VMEM_SPEC] * 9,
        out_specs=(VMEM_SPEC, VMEM_SPEC),
        scratch_shapes=[
            pltpu.VMEM((256, 1152), BF16),
            pltpu.VMEM((576, 1280), BF16),
            pltpu.VMEM((1152, 256), BF16),
            pltpu.VMEM((64, 144, 128), BF16),
            pltpu.VMEM((8, 144, 256), BF16),
            pltpu.VMEM((1056, 256), F32),
            pltpu.VMEM((1280, 256), F32),
            pltpu.VMEM((112, 256), F32),
            pltpu.VMEM((3, 64, 128), F32),
            pltpu.VMEM((3, 8, 256), F32),
        ],
        compiler_params=pltpu.CompilerParams(vmem_limit_bytes=32 * 1024 * 1024),
    )(thr, *spread, four, other)


def flat_taps(kernels):
    count = kernels.shape[0] * 2
    pairs = kernels.reshape(count, 33, 33)
    return jnp.concatenate(
        [
            pairs[:, :, :32].reshape(count, 1056),
            pairs[:, :, 32],
            jnp.zeros((count, 63), BF16),
        ],
        axis=1,
    )


def on_device(mask, kernels, eigen, focus, target, pixel_weight, threshold):
    strips = lax.axis_size("strip")
    strip = lax.axis_index("strip")
    me = lax.axis_index("kern")

    def columns(array, rim):
        wide = jnp.pad(array.astype(F32), ((0, 0), (rim, rim)))
        return lax.dynamic_slice_in_dim(wide, me * 128, 128 + 2 * rim, 1)

    mask_cols = columns(mask, 32)
    target_cols = columns(target, 16)
    weight_cols = columns(pixel_weight, 16)

    def rim_rows(start):
        rows = slice(start, start + 16)
        return jnp.concatenate(
            [mask_cols, jnp.concatenate([target_cols[rows], weight_cols[rows]], axis=0)], axis=1
        )

    up = lax.ppermute(rim_rows(16), "strip", [(i, (i + 1) % strips) for i in range(strips)])
    down = lax.ppermute(rim_rows(0), "strip", [((i + 1) % strips, i) for i in range(strips)])
    own = jnp.concatenate(
        [
            mask_cols,
            jnp.pad(jnp.concatenate([target_cols, weight_cols], axis=0), ((0, 0), (0, 32))),
        ],
        axis=0,
    )

    taps = flat_taps(kernels)
    four = jnp.stack(
        [taps]
        + [lax.ppermute(taps, "kern", [(i, i ^ (2 * s)) for i in range(8)]) for s in range(1, 4)]
    )
    other = lax.ppermute(four, "kern", [(i, i ^ 1) for i in range(8)])

    def reorder(values, fill):
        cube = values.reshape(2, 2, 2, 9)
        for axis, bit in ((0, 4), (1, 2), (2, 1)):
            cube = jnp.where((me & bit) > 0, jnp.flip(cube, axis), cube)
        cube = jnp.moveaxis(cube, 2, 0)
        both = jnp.repeat(cube.reshape(8, 9), 2, axis=1)
        return jnp.pad(both, ((0, 0), (0, 14)), constant_values=fill).reshape(1, 256)

    fe = jnp.concatenate(
        [reorder(focus.astype(F32), -1.0), reorder(eigen, 0.0), jnp.zeros((6, 256), F32)], axis=0
    )
    place = jnp.stack([strip, strip * 0 + strips - 1]).astype(jnp.int32)
    spread = spread_call(place, fe, own, up, down)
    return step_call(threshold, spread, four, other)


def solution(mesh):
    placed = (
        P("strip", None),
        P("kern", None, None, None),
        P(),
        P(),
        P("strip", None),
        P("strip", None),
        P(),
    )
    return jax.shard_map(
        on_device,
        mesh=mesh,
        in_specs=placed,
        out_specs=(P("strip", "kern"), P(None, "strip", "kern")),
        check_vma=False,
    )
```

time: 44.8 us -> 33.9 us (0.76)
  waiting for transfers between devices: 7.23 us -> 1.41 us
  Pallas kernels: 15.9 us -> 13.1 us
  starting transfers between devices: 15.4 us -> 12.7 us
    pallas_call x1, Pallas kernels: 15.9 us -> 10 us  [step_call(): pl.pallas_call(step_kernel, out_shape=(jax.ShapeDtypeStruct((32, 128), F3...]
    ppermute x9 -> x6, waiting for transfers between devices: 7.23 us -> 1.41 us  [the longest x1 1.4 us: on_device(): other = lax.ppermute(four, 'kern', [(i, i ^ 1) for i in range(8)])]
    pallas_call x0 -> x1, Pallas kernels: none -> 3.03 us  [spread_call(): pl.pallas_call(spread_kernel, out_shape=(jax.ShapeDtypeStruct((2048, 256)...]
    ppermute x9 -> x6, starting transfers between devices: 15.4 us -> 12.7 us  [the longest x3 5.71 us: on_device(): lax.ppermute(taps, 'kern', [(i, i ^ 2 * s) for i in range(8)])]
  transfers between devices with their start and end apart: 9 -> 6, of which waited for: 3 -> 1; matrix products, arithmetic and copies ran while one was open for 3% -> 4% of each run, Pallas kernels for 0% -> 9%
where the time goes in v2:
time: 33.9 us; the launch traced here: 33.7 us
  Pallas kernels  13.1 us (39%)
  starting transfers between devices  12.7 us (37%)
  local copies, waits for them, and re-layouts  5.32 us (16%)
  waiting for transfers between devices  1.41 us (4%)
  between operations  0.78 us (2%)
  other arithmetic  0.43 us (1%)
    pallas_call x1, Pallas kernels, step_call(): pl.pallas_call(step_kernel, out_shape=(jax.ShapeDtypeStruct((32, 128), F3...  10 us
    ppermute x3, starting transfers between devices, on_device(): lax.ppermute(taps, 'kern', [(i, i ^ 2 * s) for i in range(8)])  5.71 us
    ppermute x1, starting transfers between devices, on_device(): lax.ppermute(rim_rows(0), 'strip', [((i + 1) % strips, i) for i in range(...  5.35 us
    unnamed x16, local copies, waits for them, and re-layouts  4.09 us
    pallas_call x1, Pallas kernels, spread_call(): pl.pallas_call(spread_kernel, out_shape=(jax.ShapeDtypeStruct((2048, 256)...  3.03 us
    ppermute x1, starting transfers between devices, on_device(): other = lax.ppermute(four, 'kern', [(i, i ^ 1) for i in range(8)])  1.57 us
    ppermute x1, waiting for transfers between devices, on_device(): other = lax.ppermute(four, 'kern', [(i, i ^ 1) for i in range(8)])  1.4 us
  transfers between devices with their start and end apart: 6, of which 1 were waited for; matrix products, arithmetic and copies ran while one was open for 4% of the time, Pallas kernels for 9%

profile of v2, /device:TPU:0, one launch (start us, length us, event | category | flops | bytes accessed | tf_op | source)
XLA Modules:
  0.0 33.7 jit_solution(16208852844030789332)
XLA Ops:
  0.6 0.9 %copy.18 = bf16[9,2,33,33]{3,2,1,0:T(8,128)(2,1)S(1)} copy(bf16[9,2,33,33]{3,1,2,0:T(2,128)(2,1)} %param.8) | data formatting | bytes 78408 | tf_op args[1]
  1.6 0.1 slice.25
  1.7 0.3 copy.20
  2.0 0.2 reshape.43
  2.1 0.0 copy-start.2
  2.1 0.1 concatenate.31
  2.2 4.2 %collective-permute-start.4 = (bf16[18,1152]{1,0:T(8,128)(2,1)S(1)}, bf16[18,1152]{1,0:T(8,128)(2,1)S(1)}, u32[]{:S(2)}, u32[]{:S(2)}) collective-permute-start(bf16[18,1152]{1,0:T(8,128)(2,1)S(1)} %concatenate.31), channel_id=1, source_target_pairs={{0,96},{16,112},{32,64},{48,80},{64,32},{80,48},{96,0},{112,16},{1... | collective-permute-start | bytes 124424 | tf_op jit(solution)/shard_map/ppermute | solution.py:343
  6.4 0.0 collective-permute-start.2
  6.4 1.6 %collective-permute-start.3 = (bf16[18,1152]{1,0:T(8,128)(2,1)S(1)}, bf16[18,1152]{1,0:T(8,128)(2,1)S(1)}, u32[]{:S(2)}, u32[]{:S(2)}) collective-permute-start(bf16[18,1152]{1,0:T(8,128)(2,1)S(1)} %concatenate.31), channel_id=1, source_target_pairs={{0,64},{16,80},{32,96},{48,112},{64,0},{80,16},{96,32},{112,48},{1... | collective-permute-start | bytes 124424 | tf_op jit(solution)/shard_map/ppermute | solution.py:343
  8.0 0.0 copy-done.2
  8.0 0.0 copy-start.3
  8.0 0.0 copy-start.1
  8.0 0.8 %copy-done.3 = bf16[32,1024]{1,0:T(8,128)(2,1)S(1)} copy-done((bf16[32,1024]{1,0:T(8,128)(2,1)S(1)}, bf16[32,1024]{1,0:T(8,128)(2,1)}, u32[]{:S(2)}) %copy-start.3) | copy-done | bytes 65560
  8.8 0.1 fusion
  8.9 0.0 copy-done.1
  8.9 0.1 pad_dynamic-slice_fusion
  9.0 0.1 pad_maximum_fusion.2
  9.1 0.1 collective-permute-start
  9.2 5.3 %collective-permute-start.1 = (f32[32,352]{1,0:T(8,128)S(1)}, f32[32,352]{1,0:T(8,128)S(1)}, u32[]{:S(2)}, u32[]{:S(2)}) collective-permute-start(f32[32,352]{1,0:T(8,128)S(1)} %get-tuple-element.20), channel_id=1, source_target_pairs={{1,0},{2,1},{3,2},{4,3},{5,4},{6,5},{7,6},{8,7},{9,8},{10,9},{11,1... | collective-permute-start | bytes 135176 | tf_op jit(solution)/shard_map/ppermute | solution.py:331
  14.5 0.1 pad_dynamic-slice_fusion.2
  14.6 0.0 copy-start.5
  14.6 0.6 %copy-done.5 = s32[72]{0:T(128)S(1)} copy-done((s32[72]{0:T(128)S(1)}, s32[72]{0:T(128)}, u32[]{:S(2)}) %copy-start.5) | copy-done | bytes 312
  15.3 0.0 copy-start.4
  15.3 0.1 reshape.34
  15.4 0.6 %copy-done.4 = f32[72]{0:T(128)S(1)} copy-done((f32[72]{0:T(128)S(1)}, f32[72]{0:T(128)}, u32[]{:S(2)}) %copy-start.4) | copy-done | bytes 312
  16.0 0.1 reshape.38
  16.1 0.1 copy.13
  16.2 0.1 copy.21
  16.3 0.1 reshape.37
  16.4 0.1 copy.16
  16.5 0.1 copy.22
  16.6 0.1 reshape.41
  16.7 0.1 pad.48.clone
  16.8 0.1 maximum_maximum_fusion.fe_ref
  16.9 0.1 pad_add_fusion.place_ref
  16.9 0.0 collective-permute-done.4
  16.9 0.0 collective-permute-done.2
  17.0 0.0 collective-permute-done.3
  17.0 0.1 pad_maximum_fusion.four_ref
  17.0 1.6 %collective-permute-start.5 = (bf16[4,18,1152]{2,1,0:T(8,128)(2,1)S(1)}, bf16[4,18,1152]{2,1,0:T(8,128)(2,1)S(1)}, u32[]{:S(2)}, u32[]{:S(2)}) collective-permute-start(bf16[4,18,1152]{2,1,0:T(8,128)(2,1)S(1)} %pad_maximum_fusion.four_ref), channel_id=1, source_target_pairs={{0,16},{16,0},{32,48},{48,32},{64,80},{80,64},{96,112},{112,96},{1... | collective-permute-start | bytes 497672 | tf_op jit(solution)/shard_map/ppermute | solution.py:345
  18.6 0.0 collective-permute-done.up_ref
  18.6 0.0 collective-permute-done.1.down_ref
  18.6 3.0 %shard_map.86 = (bf16[2048,256]{1,0:T(8,128)(2,1)S(1)}, bf16[1280,256]{1,0:T(8,128)(2,1)S(1)}, bf16[480,256]{1,0:T(8,128)(2,1)S(1)}, f32[2,64,128]{2,1,0:T(8,128...) custom-call(s32[2]{0:T(128)S(1)} %pad_add_fusion.place_ref, ...), custom_call_target="tpu_custom_call" | custom-call | flops 2147483648 | bytes 2097152 | tf_op jit(solution)/shard_map/pallas_call | solution.py:250
  21.6 1.4 %collective-permute-done.5.other_ref = bf16[4,18,1152]{2,1,0:T(8,128)(2,1)S(1)} collective-permute-done((bf16[4,18,1152]{2,1,0:T(8,128)(2,1)S(1)}, bf16[4,18,1152]{2,1,0:T(8,128)(2,1)S(1)}, u32[]{:S(2)}, u32[]{:S(2)}) %collective-permute-start.5) | collective-permute-done | bytes 165920 | tf_op jit(solution)/shard_map/ppermute | solution.py:345
  23.0 0.0 copy-start
  23.0 0.7 %copy-done = f32[3]{0:T(128)S(1)} copy-done((f32[3]{0:T(128)S(1)}, f32[3]{0:T(128)}, u32[]{:S(2)}) %copy-start) | copy-done | bytes 36
  23.7 10.0 %shard_map.87 = (f32[32,128]{1,0:T(8,128)}, f32[3,32,128]{2,1,0:T(8,128)}) custom-call(f32[3]{0:T(128)S(1)} %copy-done, bf16[2048,256]{1,0:T(8,128)(2,1)S(1)} %get-tuple-element.9.main_t, bf16[1280,256]{1,0:T(8,128)(2,1)S(1)} %get-tuple-element.10.side_t, bf16[480,256]{1,0:T(8,128)(2,1)S(1)} %get-tuple-element.11.e_ref, ...), custom_call_target="tpu_custom_call" | custom-call | tf_op jit(solution)/shard_map/pallas_call | solution.py:274
  (21 shorter events, 0.2 us)
Async XLA Ops:
  2.1 5.8 %copy-start.2 = (s32[32,1024]{1,0:T(8,128)S(1)}, s32[32,1024]{1,0:T(8,128)}, u32[]{:S(2)}) copy-start(s32[32,1024]{1,0:T(8,128)} %param.11) | copy-start | bytes 393220
  2.2 14.7 %collective-permute-start.4 = (bf16[18,1152]{1,0:T(8,128)(2,1)S(1)}, bf16[18,1152]{1,0:T(8,128)(2,1)S(1)}, u32[]{:S(2)}, u32[]{:S(2)}) collective-permute-start(bf16[18,1152]{1,0:T(8,128)(2,1)S(1)} %concatenate.31), channel_id=1, source_target_pairs={{0,96},{16,112},{32,64},{48,80},{64,32},{80,48},{96,0},{112,16},{1... | collective-permute-start | bytes 124424 | tf_op jit(solution)/shard_map/ppermute | solution.py:343
  6.4 10.6 %collective-permute-start.2 = (bf16[18,1152]{1,0:T(8,128)(2,1)S(1)}, bf16[18,1152]{1,0:T(8,128)(2,1)S(1)}, u32[]{:S(2)}, u32[]{:S(2)}) collective-permute-start(bf16[18,1152]{1,0:T(8,128)(2,1)S(1)} %concatenate.31), channel_id=1, source_target_pairs={{0,32},{16,48},{32,0},{48,16},{64,96},{80,112},{96,64},{112,80},{1... | collective-permute-start | bytes 124424 | tf_op jit(solution)/shard_map/ppermute | solution.py:343
  6.4 10.6 %collective-permute-start.3 = (bf16[18,1152]{1,0:T(8,128)(2,1)S(1)}, bf16[18,1152]{1,0:T(8,128)(2,1)S(1)}, u32[]{:S(2)}, u32[]{:S(2)}) collective-permute-start(bf16[18,1152]{1,0:T(8,128)(2,1)S(1)} %concatenate.31), channel_id=1, source_target_pairs={{0,64},{16,80},{32,96},{48,112},{64,0},{80,16},{96,32},{112,48},{1... | collective-permute-start | bytes 124424 | tf_op jit(solution)/shard_map/ppermute | solution.py:343
  8.0 0.8 %copy-start.3 = (bf16[32,1024]{1,0:T(8,128)(2,1)S(1)}, bf16[32,1024]{1,0:T(8,128)(2,1)}, u32[]{:S(2)}) copy-start(bf16[32,1024]{1,0:T(8,128)(2,1)} %param.7) | copy-start | bytes 196612
  8.0 0.9 %copy-start.1 = (f32[32,1024]{1,0:T(8,128)S(1)}, f32[32,1024]{1,0:T(8,128)}, u32[]{:S(2)}) copy-start(f32[32,1024]{1,0:T(8,128)} %param.12) | copy-start | bytes 393220
  9.1 9.5 %collective-permute-start = (f32[32,352]{1,0:T(8,128)S(1)}, f32[32,352]{1,0:T(8,128)S(1)}, u32[]{:S(2)}, u32[]{:S(2)}) collective-permute-start(f32[32,352]{1,0:T(8,128)S(1)} %get-tuple-element.21), channel_id=1, source_target_pairs={{0,1},{1,2},{2,3},{3,4},{4,5},{5,6},{6,7},{7,8},{8,9},{9,10},{10,1... | collective-permute-start | bytes 135176 | tf_op jit(solution)/shard_map/ppermute | solution.py:330
  9.2 9.4 %collective-permute-start.1 = (f32[32,352]{1,0:T(8,128)S(1)}, f32[32,352]{1,0:T(8,128)S(1)}, u32[]{:S(2)}, u32[]{:S(2)}) collective-permute-start(f32[32,352]{1,0:T(8,128)S(1)} %get-tuple-element.20), channel_id=1, source_target_pairs={{1,0},{2,1},{3,2},{4,3},{5,4},{6,5},{7,6},{8,7},{9,8},{10,9},{11,1... | collective-permute-start | bytes 135176 | tf_op jit(solution)/shard_map/ppermute | solution.py:331
  14.6 0.7 %copy-start.5 = (s32[72]{0:T(128)S(1)}, s32[72]{0:T(128)}, u32[]{:S(2)}) copy-start(s32[72]{0:T(128)} %param.10) | copy-start | bytes 868
  15.3 0.7 %copy-start.4 = (f32[72]{0:T(128)S(1)}, f32[72]{0:T(128)}, u32[]{:S(2)}) copy-start(f32[72]{0:T(128)} %param.9) | copy-start | bytes 868
  17.0 6.0 %collective-permute-start.5 = (bf16[4,18,1152]{2,1,0:T(8,128)(2,1)S(1)}, bf16[4,18,1152]{2,1,0:T(8,128)(2,1)S(1)}, u32[]{:S(2)}, u32[]{:S(2)}) collective-permute-start(bf16[4,18,1152]{2,1,0:T(8,128)(2,1)S(1)} %pad_maximum_fusion.four_ref), channel_id=1, source_target_pairs={{0,16},{16,0},{32,48},{48,32},{64,80},{80,64},{96,112},{112,96},{1... | collective-permute-start | bytes 497672 | tf_op jit(solution)/shard_map/ppermute | solution.py:345
  23.0 0.7 %copy-start = (f32[3]{0:T(128)S(1)}, f32[3]{0:T(128)}, u32[]{:S(2)}) copy-start(f32[3]{0:T(128)} %thr_ref.1) | copy-start | bytes 40

commit v3 on v2

--- a/solution.py
+++ b/solution.py
@@ -14,19 +14,83 @@
     return lax.broadcasted_iota(jnp.int32, shape, dim)
 
 
+def skewed(eight, j, tap, lane):
+    left = jnp.broadcast_to(eight[j : j + 1, 0:128], (32, 128))
+    right = jnp.broadcast_to(eight[j : j + 1, 128:256], (32, 128))
+    left = pltpu.roll(left, 97, 1, stride=1, stride_axis=0)
+    right = pltpu.roll(right, 97, 1, stride=1, stride_axis=0)
+    return jnp.where(lane + 31 - tap < 128, left, right).astype(BF16)
+
+
+def own_kernel(
+    thr_ref, focus_ref, eigen_ref, mask_ref,
+    center, pick_ref, eig_ref, thrs_ref,
+    both_ref, rows_ref, thr_vm, focus_vm, eigen_vm, sems,
+):
+    me = lax.axis_index("kern")
+    copies = [
+        pltpu.make_async_copy(src, dst, sems.at[n])
+        for n, (src, dst) in enumerate(
+            ((thr_ref, thr_vm), (focus_ref, focus_vm), (eigen_ref, eigen_vm))
+        )
+    ]
+    for copy in copies:
+        copy.start()
+    rows_ref[:, 128:256] = jnp.zeros((32, 128), F32)
+    rows_ref[:, 0:192] = mask_ref[...]
+    tap = iota((32, 128), 0)
+    lane = iota((32, 128), 1)
+
+    def spread_own(block, _):
+        eight = rows_ref[pl.ds(pl.multiple_of(block * 8, 8), 8), :]
+        for j in range(8):
+            spot = pl.multiple_of((block * 8 + j) * 32, 32)
+            center[pl.ds(spot, 32), :] = skewed(eight, j, tap, lane)
+        return 0
+
+    lax.fori_loop(0, 4, spread_own, 0)
+
+    for copy in copies:
+        copy.wait()
+    both_ref[...] = jnp.zeros((8, 128), F32)
+    both_ref[0:1, 0:72] = focus_vm[...].astype(F32)
+    both_ref[1:2, 0:72] = eigen_vm[...]
+    listed = jnp.transpose(both_ref[...])
+    slot = iota((1, 256), 1)
+    block = slot >> 5
+    holder = me ^ (2 * (block & 3) + (block >> 2))
+    inside = (slot & 31) < 18
+    system = jnp.where(inside, 9 * holder + ((slot & 31) >> 1), -1)
+    here = iota((128, 256), 0) == system
+    frow = jnp.sum(jnp.where(here, listed[:, 0:1], 0.0), axis=0, keepdims=True)
+    frow = jnp.where(inside, frow, -1.0)
+    erow = jnp.sum(jnp.where(here, listed[:, 1:2], 0.0), axis=0, keepdims=True)
+    fcol = jnp.transpose(jnp.broadcast_to(frow, (8, 256)))[:, 0:1]
+    before = (fcol == frow) & (iota((256, 256), 0) < iota((256, 256), 1))
+    rank = jnp.sum(jnp.where(before, 1.0, 0.0), axis=0, keepdims=True)
+    pos = jnp.where(frow >= 0.0, frow * 48.0 + rank, -1.0)
+    pick = jnp.where(iota((256, 256), 0).astype(F32) == pos, 1.0, 0.0)
+    pick_ref[...] = pick.astype(BF16)
+    eig = jnp.sum(pick * erow, axis=1, keepdims=True)[0:144]
+    eig_ref[...] = jnp.broadcast_to(eig, (144, 128))
+    for v in range(12):
+        thrs_ref[v : v + 1, :] = jnp.broadcast_to(thr_vm[0:1, v % 3 : v % 3 + 1], (1, 256))
+
+
 def spread_kernel(
-    place_ref, fe_ref, own_ref, up_ref, down_ref,
-    main_t, side_t, e_ref, tgt_main, tgt_side, pick_ref, eig_ref, rows_ref, lo_ref, hi_ref,
+    center, mask_ref, target_ref, weight_ref, up_ref, down_ref,
+    main_t, side_t, e_ref, tgt_main, tgt_side,
+    rows_ref, lo_ref, hi_ref,
 ):
-    strip = place_ref[0]
-    last = place_ref[1]
+    strip = lax.axis_index("strip")
+    last = lax.axis_size("strip") - 1
 
     has_up = (strip > 0).astype(F32)
     has_down = (strip < last).astype(F32)
     rows_ref[96:, :] = jnp.zeros((16, 256), F32)
     rows_ref[:, 128:] = jnp.zeros((112, 128), F32)
     rows_ref[0:32, 0:192] = up_ref[:, 0:192] * has_up
-    rows_ref[32:64, 0:192] = own_ref[0:32, :]
+    rows_ref[32:64, 0:192] = mask_ref[...]
     rows_ref[64:96, 0:192] = down_ref[:, 0:192] * has_down
 
     for kind in range(2):
@@ -35,7 +99,7 @@
         if kind == 1:
             above = above * has_up
             below = below * has_down
-        mine = own_ref[32 + 32 * kind : 64 + 32 * kind, 0:160]
+        mine = (weight_ref if kind else target_ref)[...]
         area = jnp.concatenate([above, mine, below], axis=0)
         tgt_main[kind] = area[:, 0:128]
         tgt_side[kind] = jnp.concatenate(
@@ -48,28 +112,19 @@
     tap = iota((32, 128), 0)
     lane = iota((32, 128), 1)
 
-    def spread_main(block, _, to_left, to_right):
-        eight = rows_ref[pl.ds(pl.multiple_of(block * 8, 8), 8), :]
+    main_t[1024:2048, 0:128] = center[...]
+    main_t[0:1024, 128:256] = center[...]
+
+    def spread_rim(block, _):
+        start = pl.multiple_of(block * 8, 8)
+        above, below = rows_ref[pl.ds(start, 8), :], rows_ref[pl.ds(start + 64, 8), :]
         for j in range(8):
-            r = block * 8 + j
-            left = jnp.broadcast_to(eight[j : j + 1, 0:128], (32, 128))
-            right = jnp.broadcast_to(eight[j : j + 1, 128:256], (32, 128))
-            left = pltpu.roll(left, 97, 1, stride=1, stride_axis=0)
-            right = pltpu.roll(right, 97, 1, stride=1, stride_axis=0)
-            both = jnp.where(lane + 31 - tap < 128, left, right).astype(BF16)
-            if to_left:
-                main_t[pl.ds(pl.multiple_of(r * 32, 32), 32), 0:128] = both
-            if to_right:
-                main_t[pl.ds(pl.multiple_of(r * 32 - 1024, 32), 32), 128:256] = both
+            spot = pl.multiple_of((block * 8 + j) * 32, 32)
+            main_t[pl.ds(spot, 32), 0:128] = skewed(above, j, tap, lane)
+            main_t[pl.ds(spot + 1024, 32), 128:256] = skewed(below, j, tap, lane)
         return 0
 
-    for span in range(3):
-        lax.fori_loop(
-            4 * span,
-            4 * span + 4,
-            lambda block, c: spread_main(block, c, span < 2, span > 0),
-            0,
-        )
+    lax.fori_loop(0, 4, spread_rim, 0)
 
     def spread_side(block, _):
         start = pl.multiple_of(block * 8, 8)
@@ -94,20 +149,9 @@
     for m in range(2):
         e_ref[48 * (8 + m) : 48 * (9 + m), :] = hi_ref[4 * m : 4 * m + 48, :].astype(BF16)
 
-    fe = fe_ref[...]
-    fcol = jnp.transpose(fe)[:, 0:1]
-    frow = fe[0:1, :]
-    before = (fcol == frow) & (iota((256, 256), 0) < iota((256, 256), 1))
-    rank = jnp.sum(jnp.where(before, 1.0, 0.0), axis=0, keepdims=True)
-    pos = jnp.where(frow >= 0.0, frow * 48.0 + rank, -1.0)
-    pick = jnp.where(iota((256, 256), 0).astype(F32) == pos, 1.0, 0.0)
-    pick_ref[...] = pick.astype(BF16)
-    eig = jnp.sum(pick * fe[1:2, :], axis=1, keepdims=True)[0:144]
-    eig_ref[...] = jnp.broadcast_to(eig, (144, 128))
-
 
 def step_kernel(
-    thr_ref, main_t, side_t, e_ref, tgt_main, tgt_side, pick_ref, eig_ref, four_ref, other_ref,
+    main_t, side_t, e_ref, tgt_main, tgt_side, pick_ref, eig_ref, thrs_ref, four_ref, other_ref,
     grad_ref, resist_ref,
     raw_ref, wf_ref, wt_ref, main_a, side_a, h_main, h_side, d_ref, res_main, res_side,
 ):
@@ -149,7 +193,7 @@
             pltpu.roll(final, w, 1) if w else final
         ).astype(BF16)
 
-    thr = jnp.concatenate([jnp.full((1, 256), thr_ref[f], F32) for f in range(3)] * 4, axis=0)
+    thr = thrs_ref[...]
     eigs = jnp.concatenate([eig] * 4, axis=0)
     scales = 2.0 * eigs * norm_scale
 
@@ -242,11 +286,33 @@
 
 
 VMEM_SPEC = pl.BlockSpec(memory_space=pltpu.VMEM)
-SMEM_SPEC = pl.BlockSpec(memory_space=pltpu.SMEM)
-BIG = 40 * 1024 * 1024
-
-
-def spread_call(place, fe, own, up, down):
+
+
+def own_call(*given):
+    return pl.pallas_call(
+        own_kernel,
+        out_shape=(
+            jax.ShapeDtypeStruct((1024, 128), BF16),
+            jax.ShapeDtypeStruct((256, 256), BF16),
+            jax.ShapeDtypeStruct((144, 128), F32),
+            jax.ShapeDtypeStruct((12, 256), F32),
+        ),
+        in_specs=[pl.BlockSpec(memory_space=pl.ANY)] * 3 + [VMEM_SPEC],
+        out_specs=(VMEM_SPEC,) * 4,
+        scratch_shapes=[
+            pltpu.VMEM((8, 128), F32),
+            pltpu.VMEM((32, 256), F32),
+            pltpu.VMEM((1, 3), F32),
+            pltpu.VMEM((1, 72), jnp.int32),
+            pltpu.VMEM((1, 72), F32),
+            pltpu.SemaphoreType.DMA((3,)),
+        ],
+        cost_estimate=pl.CostEstimate(flops=2**31, bytes_accessed=2**18, transcendentals=0),
+        compiler_params=pltpu.CompilerParams(vmem_limit_bytes=16 * 1024 * 1024),
+    )(*given)
+
+
+def spread_call(*given):
     return pl.pallas_call(
         spread_kernel,
         out_shape=(
@@ -255,29 +321,27 @@
             jax.ShapeDtypeStruct((480, 256), BF16),
             jax.ShapeDtypeStruct((2, 64, 128), F32),
             jax.ShapeDtypeStruct((2, 8, 256), F32),
-            jax.ShapeDtypeStruct((256, 256), BF16),
-            jax.ShapeDtypeStruct((144, 128), F32),
         ),
-        in_specs=[SMEM_SPEC] + [VMEM_SPEC] * 4,
-        out_specs=(VMEM_SPEC,) * 7,
+        in_specs=[VMEM_SPEC] * 6,
+        out_specs=(VMEM_SPEC,) * 5,
         scratch_shapes=[
             pltpu.VMEM((112, 256), F32),
             pltpu.VMEM((56, 256), F32),
             pltpu.VMEM((56, 256), F32),
         ],
-        cost_estimate=pl.CostEstimate(flops=2**31, bytes_accessed=2**21, transcendentals=0),
+        cost_estimate=pl.CostEstimate(flops=2**29, bytes_accessed=2**21, transcendentals=0),
         compiler_params=pltpu.CompilerParams(vmem_limit_bytes=16 * 1024 * 1024),
-    )(place, fe, own, up, down)
-
-
-def step_call(thr, spread, four, other):
+    )(*given)
+
+
+def step_call(spread, order, four, other):
     return pl.pallas_call(
         step_kernel,
         out_shape=(
             jax.ShapeDtypeStruct((32, 128), F32),
             jax.ShapeDtypeStruct((3, 32, 128), F32),
         ),
-        in_specs=[SMEM_SPEC] + [VMEM_SPEC] * 9,
+        in_specs=[VMEM_SPEC] * 10,
         out_specs=(VMEM_SPEC, VMEM_SPEC),
         scratch_shapes=[
             pltpu.VMEM((256, 1152), BF16),
@@ -292,7 +356,7 @@
             pltpu.VMEM((3, 8, 256), F32),
         ],
         compiler_params=pltpu.CompilerParams(vmem_limit_bytes=32 * 1024 * 1024),
-    )(thr, *spread, four, other)
+    )(*spread, *order, four, other)
 
 
 def flat_taps(kernels):
@@ -310,32 +374,27 @@
 
 def on_device(mask, kernels, eigen, focus, target, pixel_weight, threshold):
     strips = lax.axis_size("strip")
-    strip = lax.axis_index("strip")
     me = lax.axis_index("kern")
 
-    def columns(array, rim):
+    def columns(array, rim, place):
         wide = jnp.pad(array.astype(F32), ((0, 0), (rim, rim)))
-        return lax.dynamic_slice_in_dim(wide, me * 128, 128 + 2 * rim, 1)
-
-    mask_cols = columns(mask, 32)
-    target_cols = columns(target, 16)
-    weight_cols = columns(pixel_weight, 16)
+        return lax.dynamic_slice_in_dim(wide, place * 128, 128 + 2 * rim, 1)
 
     def rim_rows(start):
         rows = slice(start, start + 16)
         return jnp.concatenate(
-            [mask_cols, jnp.concatenate([target_cols[rows], weight_cols[rows]], axis=0)], axis=1
-        )
-
-    up = lax.ppermute(rim_rows(16), "strip", [(i, (i + 1) % strips) for i in range(strips)])
-    down = lax.ppermute(rim_rows(0), "strip", [((i + 1) % strips, i) for i in range(strips)])
-    own = jnp.concatenate(
-        [
-            mask_cols,
-            jnp.pad(jnp.concatenate([target_cols, weight_cols], axis=0), ((0, 0), (0, 32))),
-        ],
-        axis=0,
-    )
+            [
+                columns(mask, 32, me),
+                jnp.concatenate(
+                    [columns(target[rows], 16, me), columns(pixel_weight[rows], 16, me)], axis=0
+                ),
+            ],
+            axis=1,
+        )
+
+    ahead = [(i, (i + 1) % strips) for i in range(strips)]
+    up = lax.ppermute(rim_rows(16), "strip", ahead)
+    down = lax.ppermute(rim_rows(0), "strip", [(b, a) for a, b in ahead])
 
     taps = flat_taps(kernels)
     four = jnp.stack(
@@ -344,20 +403,14 @@
     )
     other = lax.ppermute(four, "kern", [(i, i ^ 1) for i in range(8)])
 
-    def reorder(values, fill):
-        cube = values.reshape(2, 2, 2, 9)
-        for axis, bit in ((0, 4), (1, 2), (2, 1)):
-            cube = jnp.where((me & bit) > 0, jnp.flip(cube, axis), cube)
-        cube = jnp.moveaxis(cube, 2, 0)
-        both = jnp.repeat(cube.reshape(8, 9), 2, axis=1)
-        return jnp.pad(both, ((0, 0), (0, 14)), constant_values=fill).reshape(1, 256)
-
-    fe = jnp.concatenate(
-        [reorder(focus.astype(F32), -1.0), reorder(eigen, 0.0), jnp.zeros((6, 256), F32)], axis=0
-    )
-    place = jnp.stack([strip, strip * 0 + strips - 1]).astype(jnp.int32)
-    spread = spread_call(place, fe, own, up, down)
-    return step_call(threshold, spread, four, other)
+    own_mask = columns(mask, 32, me)
+    center, *order = own_call(
+        threshold.reshape(1, 3), focus.reshape(1, 72), eigen.reshape(1, 72), own_mask
+    )
+    spread = spread_call(
+        center, own_mask, columns(target, 16, me), columns(pixel_weight, 16, me), up, down
+    )
+    return step_call(spread, order, four, other)
 
 
 def solution(mesh):

time: 33.9 us -> 31.4 us (0.926)
  local copies, waits for them, and re-layouts: 5.32 us -> 4.18 us
  Pallas kernels: 13.1 us -> 12.2 us
  waiting for transfers between devices: 1.41 us -> 0.98 us
    pallas_call x1, Pallas kernels: 3.03 us -> 1.65 us  [spread_call(): pl.pallas_call(spread_kernel, out_shape=(jax.ShapeDtypeStruct((2048, 256)...]
    pallas_call x0 -> x1, Pallas kernels: none -> 1 us  [own_call(): pl.pallas_call(own_kernel, out_shape=(jax.ShapeDtypeStruct((1024, 128), B...]
    unnamed x16 -> x14, local copies, waits for them, and re-layouts: 4.09 us -> 3.54 us
    reshape x8 -> x0, local copies, waits for them, and re-layouts: 0.53 us -> none  [the longest x4 0.19 us: reorder(): both = jnp.repeat(cube.reshape(8, 9), 2, axis=1)]
    pallas_call x1, Pallas kernels: 10 us -> 9.56 us  [step_call(): pl.pallas_call(step_kernel, out_shape=(jax.ShapeDtypeStruct((32, 128), F3...]
    ppermute x1, waiting for transfers between devices: 1.4 us -> 0.96 us  [on_device(): other = lax.ppermute(four, 'kern', [(i, i ^ 1) for i in range(8)])]
  transfers between devices with their start and end apart: 6 -> 6, of which waited for: 1 -> 1; matrix products, arithmetic and copies ran while one was open for 4% -> 2% of each run, Pallas kernels for 9% -> 9%
where the time goes in v3:
time: 31.4 us; the launch traced here: 31 us
  starting transfers between devices  12.6 us (40%)
  Pallas kernels  12.2 us (39%)
  local copies, waits for them, and re-layouts  4.18 us (13%)
  waiting for transfers between devices  0.98 us (3%)
  between operations  0.74 us (2%)
    pallas_call x1, Pallas kernels, step_call(): pl.pallas_call(step_kernel, out_shape=(jax.ShapeDtypeStruct((32, 128), F3...  9.56 us
    ppermute x3, starting transfers between devices, on_device(): lax.ppermute(taps, 'kern', [(i, i ^ 2 * s) for i in range(8)])  5.62 us
    ppermute x1, starting transfers between devices, on_device(): down = lax.ppermute(rim_rows(0), 'strip', [(b, a) for a, b in ahead])  5.35 us
    unnamed x14, local copies, waits for them, and re-layouts  3.54 us
    pallas_call x1, Pallas kernels, spread_call(): pl.pallas_call(spread_kernel, out_shape=(jax.ShapeDtypeStruct((2048, 256)...  1.65 us
    ppermute x1, starting transfers between devices, on_device(): other = lax.ppermute(four, 'kern', [(i, i ^ 1) for i in range(8)])  1.57 us
    pallas_call x1, Pallas kernels, own_call(): pl.pallas_call(own_kernel, out_shape=(jax.ShapeDtypeStruct((1024, 128), B...  1 us
    ppermute x1, waiting for transfers between devices, on_device(): other = lax.ppermute(four, 'kern', [(i, i ^ 1) for i in range(8)])  0.96 us
  transfers between devices with their start and end apart: 6, of which 1 were waited for; matrix products, arithmetic and copies ran while one was open for 2% of the time, Pallas kernels for 9%

profile of v3, /device:TPU:0, one launch (start us, length us, event | category | flops | bytes accessed | tf_op | source)
XLA Modules:
  0.0 31.0 jit_solution(4593090435522016448)
XLA Ops:
  0.6 0.9 %copy.10 = bf16[9,2,33,33]{3,2,1,0:T(8,128)(2,1)S(1)} copy(bf16[9,2,33,33]{3,1,2,0:T(2,128)(2,1)} %param.8) | data formatting | bytes 78408 | tf_op args[1]
  1.6 0.1 slice.25
  1.7 0.3 copy.12
  2.0 0.2 reshape.23
  2.1 0.0 copy-start.4
  2.1 0.1 concatenate.19
  2.2 2.0 %collective-permute-start.2 = (bf16[18,1152]{1,0:T(8,128)(2,1)S(1)}, bf16[18,1152]{1,0:T(8,128)(2,1)S(1)}, u32[]{:S(2)}, u32[]{:S(2)}) collective-permute-start(bf16[18,1152]{1,0:T(8,128)(2,1)S(1)} %concatenate.19), channel_id=1, source_target_pairs={{0,32},{16,48},{32,0},{48,16},{64,96},{80,112},{96,64},{112,80},{1... | collective-permute-start | bytes 124424 | tf_op jit(solution)/shard_map/ppermute | solution.py:402
  4.3 3.6 %collective-permute-start.3 = (bf16[18,1152]{1,0:T(8,128)(2,1)S(1)}, bf16[18,1152]{1,0:T(8,128)(2,1)S(1)}, u32[]{:S(2)}, u32[]{:S(2)}) collective-permute-start(bf16[18,1152]{1,0:T(8,128)(2,1)S(1)} %concatenate.19), channel_id=1, source_target_pairs={{0,64},{16,80},{32,96},{48,112},{64,0},{80,16},{96,32},{112,48},{1... | collective-permute-start | bytes 124424 | tf_op jit(solution)/shard_map/ppermute | solution.py:402
  7.9 0.0 collective-permute-start.4
  7.9 0.0 copy-done.4
  7.9 0.0 copy-start.3
  7.9 0.9 %copy-done.3 = f32[32,1024]{1,0:T(8,128)S(1)} copy-done((f32[32,1024]{1,0:T(8,128)S(1)}, f32[32,1024]{1,0:T(8,128)}, u32[]{:S(2)}) %copy-start.3) | copy-done | bytes 131096
  8.8 0.1 pad_dynamic-slice_fusion.2
  8.9 0.0 copy-start.5
  8.9 0.1 pad_dynamic-slice_fusion.4
  9.0 0.8 %copy-done.5 = bf16[32,1024]{1,0:T(8,128)(2,1)S(1)} copy-done((bf16[32,1024]{1,0:T(8,128)(2,1)S(1)}, bf16[32,1024]{1,0:T(8,128)(2,1)}, u32[]{:S(2)}) %copy-start.5) | copy-done | bytes 65560
  9.7 0.1 fusion.mask_ref
  9.8 0.1 pad_maximum_fusion.1
  9.9 0.1 collective-permute-start
  10.0 5.3 %collective-permute-start.1 = (f32[32,352]{1,0:T(8,128)S(1)}, f32[32,352]{1,0:T(8,128)S(1)}, u32[]{:S(2)}, u32[]{:S(2)}) collective-permute-start(f32[32,352]{1,0:T(8,128)S(1)} %get-tuple-element.24), channel_id=1, source_target_pairs={{1,0},{2,1},{3,2},{4,3},{5,4},{6,5},{7,6},{8,7},{9,8},{10,9},{11,1... | collective-permute-start | bytes 135176 | tf_op jit(solution)/shard_map/ppermute | solution.py:397
  15.3 0.0 collective-permute-done.2
  15.3 0.0 collective-permute-done.3
  15.3 0.0 collective-permute-done.4
  15.3 0.1 pad_maximum_fusion.four_ref
  15.4 1.6 %collective-permute-start.5 = (bf16[4,18,1152]{2,1,0:T(8,128)(2,1)S(1)}, bf16[4,18,1152]{2,1,0:T(8,128)(2,1)S(1)}, u32[]{:S(2)}, u32[]{:S(2)}) collective-permute-start(bf16[4,18,1152]{2,1,0:T(8,128)(2,1)S(1)} %pad_maximum_fusion.four_ref), channel_id=1, source_target_pairs={{0,16},{16,0},{32,48},{48,32},{64,80},{80,64},{96,112},{112,96},{1... | collective-permute-start | bytes 497672 | tf_op jit(solution)/shard_map/ppermute | solution.py:404
  17.0 0.0 copy-start
  17.0 0.0 copy-start.1
  17.0 0.0 copy-start.2
  17.0 0.6 %copy-done = f32[3]{0:T(128)S(1)} copy-done((f32[3]{0:T(128)S(1)}, f32[3]{0:T(128)}, u32[]{:S(2)}) %copy-start) | copy-done | bytes 36
  17.6 0.0 copy-done.1
  17.6 0.0 copy-done.2
  17.6 1.0 %shard_map.86 = (bf16[1024,128]{1,0:T(8,128)(2,1)S(1)}, bf16[256,256]{1,0:T(8,128)(2,1)S(1)}, f32[144,128]{1,0:T(8,128)S(1)}, f32[12,256]{1,0:T(8,128)S(1)}) custom-call(f32[1,3]{1,0:T(1,128)S(1)} %bitcast.10, s32[1,72]{1,0:T(1,128)S(1)} %bitcast.11, f32[1,72]{1,0:T(1,128)S(1)} %bitcast.12, f32[32,192]{1,0:T(8,128)S(1)} %fusion.mask_ref), custom_call_target="tpu_custom_call" | custom-call | flops 2147483648 | bytes 262144 | tf_op jit(solution)/shard_map/pallas_call | solution.py:292
  18.7 0.1 pad_dynamic-slice_fusion
  18.8 0.0 collective-permute-done.up_ref
  18.8 0.0 collective-permute-done.1.down_ref
  18.8 1.6 %shard_map.87 = (bf16[2048,256]{1,0:T(8,128)(2,1)S(1)}, bf16[1280,256]{1,0:T(8,128)(2,1)S(1)}, bf16[480,256]{1,0:T(8,128)(2,1)S(1)}, f32[2,64,128]{2,1,0:T(8,128)S(1)}, f32[2,8,256]{2,1,0:T(8,128)S(1)}) custom-call(bf16[1024,128]{1,0:T(8,128)(2,1)S(1)} %get-tuple-element.11.center, f32[32,192]{1,0:T(8,128)S(1)} %fusion.mask_ref, ...), custom_call_target="tpu_custom_call" | custom-call | flops 536870912 | bytes 2097152 | tf_op jit(solution)/shard_map/pallas_call | solution.py:316
  20.4 1.0 %collective-permute-done.5.other_ref = bf16[4,18,1152]{2,1,0:T(8,128)(2,1)S(1)} collective-permute-done((bf16[4,18,1152]{2,1,0:T(8,128)(2,1)S(1)}, bf16[4,18,1152]{2,1,0:T(8,128)(2,1)S(1)}, u32[]{:S(2)}, u32[]{:S(2)}) %collective-permute-start.5) | collective-permute-done | bytes 165920 | tf_op jit(solution)/shard_map/ppermute | solution.py:404
  21.4 9.6 %shard_map.88 = (f32[32,128]{1,0:T(8,128)}, f32[3,32,128]{2,1,0:T(8,128)}) custom-call(bf16[2048,256]{1,0:T(8,128)(2,1)S(1)} %get-tuple-element.12.main_t, bf16[1280,256]{1,0:T(8,128)(2,1)S(1)} %get-tuple-element.13.side_t, bf16[480,256]{1,0:T(8,128)(2,1)S(1)} %get-tuple-element.14.e_ref, f32[2,64,128]{2,1,0:T(8,128)S(1)} %get-tuple-element.15.tgt_main, ...), custom_call_target="tpu_custom_call" | custom-call | tf_op jit(solution)/shard_map/pallas_call | solution.py:338
  (4 shorter events, 0.0 us)
Async XLA Ops:
  2.1 5.7 %copy-start.4 = (s32[32,1024]{1,0:T(8,128)S(1)}, s32[32,1024]{1,0:T(8,128)}, u32[]{:S(2)}) copy-start(s32[32,1024]{1,0:T(8,128)} %param.11) | copy-start | bytes 393220
  2.2 13.1 %collective-permute-start.2 = (bf16[18,1152]{1,0:T(8,128)(2,1)S(1)}, bf16[18,1152]{1,0:T(8,128)(2,1)S(1)}, u32[]{:S(2)}, u32[]{:S(2)}) collective-permute-start(bf16[18,1152]{1,0:T(8,128)(2,1)S(1)} %concatenate.19), channel_id=1, source_target_pairs={{0,32},{16,48},{32,0},{48,16},{64,96},{80,112},{96,64},{112,80},{1... | collective-permute-start | bytes 124424 | tf_op jit(solution)/shard_map/ppermute | solution.py:402
  4.3 11.0 %collective-permute-start.3 = (bf16[18,1152]{1,0:T(8,128)(2,1)S(1)}, bf16[18,1152]{1,0:T(8,128)(2,1)S(1)}, u32[]{:S(2)}, u32[]{:S(2)}) collective-permute-start(bf16[18,1152]{1,0:T(8,128)(2,1)S(1)} %concatenate.19), channel_id=1, source_target_pairs={{0,64},{16,80},{32,96},{48,112},{64,0},{80,16},{96,32},{112,48},{1... | collective-permute-start | bytes 124424 | tf_op jit(solution)/shard_map/ppermute | solution.py:402
  7.9 7.5 %collective-permute-start.4 = (bf16[18,1152]{1,0:T(8,128)(2,1)S(1)}, bf16[18,1152]{1,0:T(8,128)(2,1)S(1)}, u32[]{:S(2)}, u32[]{:S(2)}) collective-permute-start(bf16[18,1152]{1,0:T(8,128)(2,1)S(1)} %concatenate.19), channel_id=1, source_target_pairs={{0,96},{16,112},{32,64},{48,80},{64,32},{80,48},{96,0},{112,16},{1... | collective-permute-start | bytes 124424 | tf_op jit(solution)/shard_map/ppermute | solution.py:402
  7.9 0.9 %copy-start.3 = (f32[32,1024]{1,0:T(8,128)S(1)}, f32[32,1024]{1,0:T(8,128)}, u32[]{:S(2)}) copy-start(f32[32,1024]{1,0:T(8,128)} %param.12) | copy-start | bytes 393220
  8.9 0.8 %copy-start.5 = (bf16[32,1024]{1,0:T(8,128)(2,1)S(1)}, bf16[32,1024]{1,0:T(8,128)(2,1)}, u32[]{:S(2)}) copy-start(bf16[32,1024]{1,0:T(8,128)(2,1)} %param.7) | copy-start | bytes 196612
  9.9 8.9 %collective-permute-start = (f32[32,352]{1,0:T(8,128)S(1)}, f32[32,352]{1,0:T(8,128)S(1)}, u32[]{:S(2)}, u32[]{:S(2)}) collective-permute-start(f32[32,352]{1,0:T(8,128)S(1)} %get-tuple-element.25), channel_id=1, source_target_pairs={{0,1},{1,2},{2,3},{3,4},{4,5},{5,6},{6,7},{7,8},{8,9},{9,10},{10,1... | collective-permute-start | bytes 135176 | tf_op jit(solution)/shard_map/ppermute | solution.py:396
  10.0 8.8 %collective-permute-start.1 = (f32[32,352]{1,0:T(8,128)S(1)}, f32[32,352]{1,0:T(8,128)S(1)}, u32[]{:S(2)}, u32[]{:S(2)}) collective-permute-start(f32[32,352]{1,0:T(8,128)S(1)} %get-tuple-element.24), channel_id=1, source_target_pairs={{1,0},{2,1},{3,2},{4,3},{5,4},{6,5},{7,6},{8,7},{9,8},{10,9},{11,1... | collective-permute-start | bytes 135176 | tf_op jit(solution)/shard_map/ppermute | solution.py:397
  15.4 6.0 %collective-permute-start.5 = (bf16[4,18,1152]{2,1,0:T(8,128)(2,1)S(1)}, bf16[4,18,1152]{2,1,0:T(8,128)(2,1)S(1)}, u32[]{:S(2)}, u32[]{:S(2)}) collective-permute-start(bf16[4,18,1152]{2,1,0:T(8,128)(2,1)S(1)} %pad_maximum_fusion.four_ref), channel_id=1, source_target_pairs={{0,16},{16,0},{32,48},{48,32},{64,80},{80,64},{96,112},{112,96},{1... | collective-permute-start | bytes 497672 | tf_op jit(solution)/shard_map/ppermute | solution.py:404
  17.0 0.7 %copy-start = (f32[3]{0:T(128)S(1)}, f32[3]{0:T(128)}, u32[]{:S(2)}) copy-start(f32[3]{0:T(128)} %param.13) | copy-start | bytes 40
  17.0 0.7 %copy-start.1 = (s32[72]{0:T(128)S(1)}, s32[72]{0:T(128)}, u32[]{:S(2)}) copy-start(s32[72]{0:T(128)} %param.10) | copy-start | bytes 868
  17.0 0.7 %copy-start.2 = (f32[72]{0:T(128)S(1)}, f32[72]{0:T(128)}, u32[]{:S(2)}) copy-start(f32[72]{0:T(128)} %param.9) | copy-start | bytes 868

commit v4 on v3

--- a/solution.py
+++ b/solution.py
@@ -69,7 +69,9 @@
     before = (fcol == frow) & (iota((256, 256), 0) < iota((256, 256), 1))
     rank = jnp.sum(jnp.where(before, 1.0, 0.0), axis=0, keepdims=True)
     pos = jnp.where(frow >= 0.0, frow * 48.0 + rank, -1.0)
-    pick = jnp.where(iota((256, 256), 0).astype(F32) == pos, 1.0, 0.0)
+    spot = iota((256, 256), 0)
+    spot = jnp.where(spot < 128, spot, 128 + (spot & 15))
+    pick = jnp.where(spot.astype(F32) == pos, 1.0, 0.0)
     pick_ref[...] = pick.astype(BF16)
     eig = jnp.sum(pick * erow, axis=1, keepdims=True)[0:144]
     eig_ref[...] = jnp.broadcast_to(eig, (144, 128))
@@ -78,12 +80,16 @@
 
 
 def spread_kernel(
-    center, mask_ref, target_ref, weight_ref, up_ref, down_ref,
+    center, mask_ref, target_ref, weight_ref, near_ref, far_ref,
     main_t, side_t, e_ref, tgt_main, tgt_side,
-    rows_ref, lo_ref, hi_ref,
+    rows_ref, lo_ref, hi_ref, up_ref, down_ref,
 ):
     strip = lax.axis_index("strip")
     last = lax.axis_size("strip") - 1
+
+    odd = jnp.full((32, 352), strip & 1, jnp.int32) > 0
+    up_ref[...] = jnp.where(odd, near_ref[...], far_ref[...])
+    down_ref[...] = jnp.where(odd, far_ref[...], near_ref[...])
 
     has_up = (strip > 0).astype(F32)
     has_down = (strip < last).astype(F32)
@@ -153,7 +159,8 @@
 def step_kernel(
     main_t, side_t, e_ref, tgt_main, tgt_side, pick_ref, eig_ref, thrs_ref, four_ref, other_ref,
     grad_ref, resist_ref,
-    raw_ref, wf_ref, wt_ref, main_a, side_a, h_main, h_side, d_ref, res_main, res_side,
+    raw_ref, wf_ref, wt_ref, wc_ref, ws_ref, wcs_ref, main_a, side_a,
+    h_main, h_last, h_side, d_ref, d_last, res_main, res_side,
 ):
     norm_scale = 3.0 / 72
     tap = iota((32, 128), 0)
@@ -165,7 +172,32 @@
         raw_ref[32 * s : 32 * s + 18, :] = four_ref[s]
         raw_ref[32 * s + 128 : 32 * s + 146, :] = other_ref[s]
     taps_f = jnp.dot(pick_ref[...], raw_ref[...], preferred_element_type=F32)
-    wt_ref[...] = jnp.transpose(taps_f).astype(BF16)
+    taps_t = jnp.transpose(taps_f)
+    blank = jnp.zeros((32, 128), BF16)
+    wt_ref[0:32, :] = blank
+    wt_ref[32:1088, :] = taps_t[0:1056, 0:128].astype(BF16)
+    wt_ref[1088:1120, :] = blank
+    edge_taps = taps_t[1056:1104, 0:128]
+    wc_ref[...] = jnp.concatenate([edge_taps, pltpu.roll(edge_taps, 1, 0)], axis=1).astype(BF16)
+    step = lane >> 4
+    stack = [taps_t[32 * a : 32 * a + 32, 128:256] for a in range(33)]
+    column = jnp.concatenate([taps_t[1056:1104, 128:256], jnp.zeros((16, 128), F32)], axis=0)
+    step_c = iota((64, 128), 1) >> 4
+    none = jnp.zeros((32, 128), F32)
+    for shift in (1, 2, 4):
+        stack = [
+            jnp.where(
+                (step & shift) > 0,
+                stack[a - shift] if 0 <= a - shift else none,
+                stack[a] if a < len(stack) else none,
+            )
+            for a in range(len(stack) + shift)
+        ]
+        column = jnp.where((step_c & shift) > 0, pltpu.roll(column, shift, 0), column)
+    for a in range(56):
+        inside = 8 <= a < 8 + len(stack)
+        ws_ref[32 * a : 32 * a + 32, :] = stack[a - 8].astype(BF16) if inside else blank
+    wcs_ref[...] = jnp.concatenate([column, pltpu.roll(column, 8, 0)], axis=1).astype(BF16)
     x = iota((128, 128), 0)
     y = iota((128, 128), 1)
     turn = jnp.where(((x >> 5) == (y >> 5)) & ((x & 31) + (y & 31) == 31), 1.0, 0.0).astype(BF16)
@@ -244,35 +276,96 @@
         )
         resist_ref[f] = jnp.concatenate([res_main[f, 16:48, 16:128], edge], axis=1)
 
-    h_main[...] = jnp.zeros_like(h_main)
-    h_side[...] = jnp.zeros_like(h_side)
     d_ref[...] = jnp.zeros_like(d_ref)
-    for p in range(32):
-        i = 2 * p
-        first, final = max(0, 31 - i), min(32, 63 - i)
-        pair = jnp.concatenate([main_a[i], main_a[i + 1]], axis=1)
-        spot = 32 * (i + first - 31)
+    d_last[...] = jnp.zeros_like(d_last)
+    for i in (28, 32, *range(0, 28, 4), *range(36, 64, 4)):
+        quad = jnp.concatenate(
+            [
+                jnp.concatenate([main_a[i, 0:128], main_a[i + 2, 0:128]], axis=1),
+                jnp.concatenate([main_a[i + 1, 0:128], main_a[i + 3, 0:128]], axis=1),
+            ],
+            axis=0,
+        )
+        first, final = max(0, 30 - i), min(33, 63 - i)
         size = 32 * (final + 1 - first)
-        h_main[spot : spot + size, :] += jnp.dot(
-            wt_ref[32 * first : 32 * first + size, 0:144], pair, preferred_element_type=F32
-        )
-        d_ref[i : i + 48, :] += jnp.dot(
-            wt_ref[1056:1104, 0:144], pair, preferred_element_type=F32
-        )
-    for w in range(8):
-        h_side[32 * w : 32 * w + 1056, :] += jnp.dot(
-            wt_ref[0:1056, 0:144], side_a[w], preferred_element_type=F32
-        )
+        left = jnp.concatenate(
+            [
+                jnp.concatenate(
+                    [
+                        wt_ref[32 * first + 32 : 32 * first + 32 + size, :],
+                        wt_ref[32 * first : 32 * first + size, :],
+                    ],
+                    axis=1,
+                ),
+                wc_ref[...],
+            ],
+            axis=0,
+        )
+        part = jnp.dot(left, quad, preferred_element_type=F32)
+        spot = 32 * (i + first - 30)
+        if i == 28:
+            h_main[0:1024, :] = part[0:size]
+        elif i == 32:
+            h_main[64:1024, :] += part[0:960]
+            h_main[1024:1088, :] = part[960:1024]
+        else:
+            h_main[spot : spot + size, :] += part[0:size]
+        d_ref[i : i + 48, :] += part[size:]
+    for t in range(2):
+        rest = jnp.concatenate(
+            [
+                jnp.concatenate(
+                    [main_a[32 * t + r, 128:144], main_a[32 * t + 16 + r, 128:144]], axis=1
+                )
+                for r in range(16)
+            ],
+            axis=0,
+        )
+        first = 16 - 16 * t
+        left = jnp.concatenate(
+            [
+                jnp.concatenate(
+                    [
+                        ws_ref[32 * first + 256 : 32 * first + 1280, :],
+                        ws_ref[32 * first : 32 * first + 1024, :],
+                    ],
+                    axis=1,
+                ),
+                wcs_ref[...],
+            ],
+            axis=0,
+        )
+        part = jnp.dot(left, rest, preferred_element_type=F32)
+        if t == 0:
+            h_last[0:1024, :] = part[0:1024]
+        else:
+            h_last[512:1024, :] += part[0:512]
+            h_last[1024:1536, :] = part[512:1024]
+        d_last[32 * t : 32 * t + 64, :] += part[1024:]
+    rest = jnp.concatenate([side_a[w, 128:144] for w in range(8)], axis=0)
+    h_side[...] = jnp.dot(ws_ref[256:1536, :], rest, preferred_element_type=F32)
+    for w in range(0, 8, 2):
+        pair = jnp.concatenate([side_a[w, 0:128], side_a[w + 1, 0:128]], axis=0)
+        left = jnp.concatenate([wt_ref[32:1120, :], wt_ref[0:1088, :]], axis=1)
+        h_side[32 * w : 32 * w + 1088, :] += jnp.dot(left, pair, preferred_element_type=F32)
 
     group = lane >> 5
     for r in range(32):
-        body = h_main[32 * r + 32 : 32 * r + 64, 0:128] + h_main[32 * r : 32 * r + 32, 128:256]
-        edge = jnp.zeros((32, 128), F32)
-        for g in range(8):
-            u = r + 32 - 8 * g
-            if 0 <= u <= 39:
-                cols = slice(128 * (g // 4), 128 * (g // 4) + 128)
-                edge += jnp.where(group == g % 4, h_side[32 * u : 32 * u + 32, cols], 0.0)
+        body = (
+            h_main[32 * r + 64 : 32 * r + 96, 0:128]
+            + h_main[32 * r : 32 * r + 32, 128:256]
+            + h_last[32 * r + 512 : 32 * r + 544, 0:128]
+            + h_last[32 * r : 32 * r + 32, 128:256]
+        )
+        edge = None
+        for half in range(2):
+            chosen = None
+            for g in range(4 * half, 4 * half + 4):
+                u = r + 32 - 8 * g
+                if 0 <= u <= 39:
+                    term = h_side[32 * u : 32 * u + 32, 128 * half : 128 * half + 128]
+                    chosen = jnp.where(group == g % 4, term, 0.0 if chosen is None else chosen)
+            edge = chosen if edge is None else edge + chosen
         edge = edge + pltpu.roll(edge, 64, 1)
         edge = edge + pltpu.roll(edge, 32, 1)
         body = pltpu.roll(body, 96, 1, stride=1, stride_axis=0)
@@ -281,7 +374,9 @@
         grad_ref[r : r + 1, :] = (
             jnp.sum(both, axis=0, keepdims=True)
             + d_ref[r + 32 : r + 33, 0:128]
-            + d_ref[r + 31 : r + 32, 128:256]
+            + d_ref[r + 30 : r + 31, 128:256]
+            + d_last[r + 32 : r + 33, 0:128]
+            + d_last[r + 16 : r + 17, 128:256]
         )
 
 
@@ -328,6 +423,8 @@
             pltpu.VMEM((112, 256), F32),
             pltpu.VMEM((56, 256), F32),
             pltpu.VMEM((56, 256), F32),
+            pltpu.VMEM((32, 352), F32),
+            pltpu.VMEM((32, 352), F32),
         ],
         cost_estimate=pl.CostEstimate(flops=2**29, bytes_accessed=2**21, transcendentals=0),
         compiler_params=pltpu.CompilerParams(vmem_limit_bytes=16 * 1024 * 1024),
@@ -346,12 +443,17 @@
         scratch_shapes=[
             pltpu.VMEM((256, 1152), BF16),
             pltpu.VMEM((576, 1280), BF16),
-            pltpu.VMEM((1152, 256), BF16),
+            pltpu.VMEM((1120, 128), BF16),
+            pltpu.VMEM((48, 256), BF16),
+            pltpu.VMEM((1792, 128), BF16),
+            pltpu.VMEM((64, 256), BF16),
             pltpu.VMEM((64, 144, 128), BF16),
             pltpu.VMEM((8, 144, 256), BF16),
-            pltpu.VMEM((1056, 256), F32),
+            pltpu.VMEM((1088, 256), F32),
+            pltpu.VMEM((1536, 256), F32),
             pltpu.VMEM((1280, 256), F32),
             pltpu.VMEM((112, 256), F32),
+            pltpu.VMEM((96, 256), F32),
             pltpu.VMEM((3, 64, 128), F32),
             pltpu.VMEM((3, 8, 256), F32),
         ],
@@ -376,25 +478,20 @@
     strips = lax.axis_size("strip")
     me = lax.axis_index("kern")
 
-    def columns(array, rim, place):
+    odd = lax.axis_index("strip") % 2
+
+    def columns(array, rim, row=0, count=32):
         wide = jnp.pad(array.astype(F32), ((0, 0), (rim, rim)))
-        return lax.dynamic_slice_in_dim(wide, place * 128, 128 + 2 * rim, 1)
-
-    def rim_rows(start):
-        rows = slice(start, start + 16)
-        return jnp.concatenate(
-            [
-                columns(mask, 32, me),
-                jnp.concatenate(
-                    [columns(target[rows], 16, me), columns(pixel_weight[rows], 16, me)], axis=0
-                ),
-            ],
-            axis=1,
-        )
-
-    ahead = [(i, (i + 1) % strips) for i in range(strips)]
-    up = lax.ppermute(rim_rows(16), "strip", ahead)
-    down = lax.ppermute(rim_rows(0), "strip", [(b, a) for a, b in ahead])
+        return lax.dynamic_slice(wide, (row, me * 128), (count, 128 + 2 * rim))
+
+    def rim_rows(row):
+        edges = [columns(target, 16, row, 16), columns(pixel_weight, 16, row, 16)]
+        return jnp.concatenate([columns(mask, 32), jnp.concatenate(edges, axis=0)], axis=1)
+
+    near_pairs = [(i, i ^ 1) for i in range(strips)]
+    far_pairs = [((i + 1) % strips, ((i ^ 1) + 1) % strips) for i in range(strips)]
+    near = lax.ppermute(rim_rows(16 - 16 * odd), "strip", near_pairs)
+    far = lax.ppermute(rim_rows(16 * odd), "strip", far_pairs)
 
     taps = flat_taps(kernels)
     four = jnp.stack(
@@ -403,12 +500,12 @@
     )
     other = lax.ppermute(four, "kern", [(i, i ^ 1) for i in range(8)])
 
-    own_mask = columns(mask, 32, me)
+    own_mask = columns(mask, 32)
     center, *order = own_call(
         threshold.reshape(1, 3), focus.reshape(1, 72), eigen.reshape(1, 72), own_mask
     )
     spread = spread_call(
-        center, own_mask, columns(target, 16, me), columns(pixel_weight, 16, me), up, down
+        center, own_mask, columns(target, 16), columns(pixel_weight, 16), near, far
     )
     return step_call(spread, order, four, other)
 

time: 31.4 us -> 29.1 us (0.927); the launches traced: 31 us -> 29 us
  Pallas kernels: 12.2 us -> 10.9 us
  local copies, waits for them, and re-layouts: 4.18 us -> 3.26 us
  waiting for transfers between devices: 0.98 us -> 1.89 us
  starting transfers between devices: 12.6 us -> 12 us
    pallas_call x1, Pallas kernels: 9.56 us -> 8.23 us  [step_call(): pl.pallas_call(step_kernel, out_shape=(jax.ShapeDtypeStruct((32, 128), F3...]
    ppermute x1, waiting for transfers between devices: 0.96 us -> 1.88 us  [on_device(): other = lax.ppermute(four, 'kern', [(i, i ^ 1) for i in range(8)])]
    ppermute x1, starting transfers between devices: 1.57 us -> 0.67 us  [on_device(): other = lax.ppermute(four, 'kern', [(i, i ^ 1) for i in range(8)])]
    unnamed x14, local copies, waits for them, and re-layouts: 3.54 us -> 2.72 us
  transfers between devices with their start and end apart: 6 -> 6, of which waited for: 1 -> 1; matrix products, arithmetic and copies ran while one was open for 2% -> 1% of each run, Pallas kernels for 9% -> 9%
where the time goes in v4:
time: 29.1 us; the launch traced here: 29 us
  starting transfers between devices  12 us (41%)
  Pallas kernels  10.9 us (37%)
  local copies, waits for them, and re-layouts  3.26 us (11%)
  waiting for transfers between devices  1.89 us (6%)
  between operations  0.75 us (3%)
    pallas_call x1, Pallas kernels, step_call(): pl.pallas_call(step_kernel, out_shape=(jax.ShapeDtypeStruct((32, 128), F3...  8.23 us
    ppermute x3, starting transfers between devices, on_device(): lax.ppermute(taps, 'kern', [(i, i ^ 2 * s) for i in range(8)])  5.62 us
    ppermute x1, starting transfers between devices, on_device(): far = lax.ppermute(rim_rows(16 * odd), 'strip', far_pairs)  5.58 us
    unnamed x14, local copies, waits for them, and re-layouts  2.72 us
    ppermute x1, waiting for transfers between devices, on_device(): other = lax.ppermute(four, 'kern', [(i, i ^ 1) for i in range(8)])  1.88 us
    pallas_call x1, Pallas kernels, spread_call(): pl.pallas_call(spread_kernel, out_shape=(jax.ShapeDtypeStruct((2048, 256)...  1.65 us
    pallas_call x1, Pallas kernels, own_call(): pl.pallas_call(own_kernel, out_shape=(jax.ShapeDtypeStruct((1024, 128), B...  1 us
    ppermute x1, starting transfers between devices, on_device(): other = lax.ppermute(four, 'kern', [(i, i ^ 1) for i in range(8)])  0.67 us
  transfers between devices with their start and end apart: 6, of which 1 were waited for; matrix products, arithmetic and copies ran while one was open for 1% of the time, Pallas kernels for 9%

profile of v4, /device:TPU:0, one launch (start us, length us, event | category | flops | bytes accessed | tf_op | source)
XLA Modules:
  0.0 29.0 jit_solution(1215909036663173745)
XLA Ops:
  0.6 0.9 %copy.10 = bf16[9,2,33,33]{3,2,1,0:T(8,128)(2,1)S(1)} copy(bf16[9,2,33,33]{3,1,2,0:T(2,128)(2,1)} %param.8) | data formatting | bytes 78408 | tf_op args[1]
  1.6 0.1 slice.9
  1.7 0.3 copy.12
  2.0 0.2 reshape.23
  2.1 0.0 copy-start.4
  2.1 0.1 concatenate.19
  2.2 2.0 %collective-permute-start.2 = (bf16[18,1152]{1,0:T(8,128)(2,1)S(1)}, bf16[18,1152]{1,0:T(8,128)(2,1)S(1)}, u32[]{:S(2)}, u32[]{:S(2)}) collective-permute-start(bf16[18,1152]{1,0:T(8,128)(2,1)S(1)} %concatenate.19), channel_id=1, source_target_pairs={{0,32},{16,48},{32,0},{48,16},{64,96},{80,112},{96,64},{112,80},{1... | collective-permute-start | bytes 124424 | tf_op jit(solution)/shard_map/ppermute | solution.py:499
  4.3 3.6 %collective-permute-start.3 = (bf16[18,1152]{1,0:T(8,128)(2,1)S(1)}, bf16[18,1152]{1,0:T(8,128)(2,1)S(1)}, u32[]{:S(2)}, u32[]{:S(2)}) collective-permute-start(bf16[18,1152]{1,0:T(8,128)(2,1)S(1)} %concatenate.19), channel_id=1, source_target_pairs={{0,64},{16,80},{32,96},{48,112},{64,0},{80,16},{96,32},{112,48},{1... | collective-permute-start | bytes 124424 | tf_op jit(solution)/shard_map/ppermute | solution.py:499
  7.9 0.0 collective-permute-start.4
  7.9 0.0 copy-done.4
  7.9 0.0 copy-start.5
  7.9 0.0 copy-start.3
  7.9 0.8 %copy-done.5 = bf16[32,1024]{1,0:T(8,128)(2,1)S(1)} copy-done((bf16[32,1024]{1,0:T(8,128)(2,1)S(1)}, bf16[32,1024]{1,0:T(8,128)(2,1)}, u32[]{:S(2)}) %copy-start.5) | copy-done | bytes 65560
  8.7 0.1 fusion.mask_ref
  8.8 0.0 copy-done.3
  8.8 0.1 pad_dynamic-slice_fusion
  8.9 0.1 pad_maximum_fusion.1
  9.0 0.1 collective-permute-start
  9.1 5.6 %collective-permute-start.1 = (f32[32,352]{1,0:T(8,128)S(1)}, f32[32,352]{1,0:T(8,128)S(1)}, u32[]{:S(2)}, u32[]{:S(2)}) collective-permute-start(f32[32,352]{1,0:T(8,128)S(1)} %get-tuple-element.24), channel_id=1, source_target_pairs={{1,2},{2,1},{3,4},{4,3},{5,6},{6,5},{7,8},{8,7},{9,10},{10,9},{11,... | collective-permute-start | bytes 135176 | tf_op jit(solution)/shard_map/ppermute | solution.py:494
  14.7 0.0 collective-permute-done.2
  14.7 0.0 collective-permute-done.3
  14.7 0.0 collective-permute-done.4
  14.7 0.1 pad_maximum_fusion.four_ref
  14.7 0.7 %collective-permute-start.5 = (bf16[4,18,1152]{2,1,0:T(8,128)(2,1)S(1)}, bf16[4,18,1152]{2,1,0:T(8,128)(2,1)S(1)}, u32[]{:S(2)}, u32[]{:S(2)}) collective-permute-start(bf16[4,18,1152]{2,1,0:T(8,128)(2,1)S(1)} %pad_maximum_fusion.four_ref), channel_id=1, source_target_pairs={{0,16},{16,0},{32,48},{48,32},{64,80},{80,64},{96,112},{112,96},{1... | collective-permute-start | bytes 497672 | tf_op jit(solution)/shard_map/ppermute | solution.py:501
  15.4 0.0 copy-start
  15.4 0.0 copy-start.1
  15.4 0.0 copy-start.2
  15.4 0.6 %copy-done = f32[3]{0:T(128)S(1)} copy-done((f32[3]{0:T(128)S(1)}, f32[3]{0:T(128)}, u32[]{:S(2)}) %copy-start) | copy-done | bytes 36
  16.1 0.0 copy-done.1
  16.1 0.0 copy-done.2
  16.1 1.0 %shard_map.86 = (bf16[1024,128]{1,0:T(8,128)(2,1)S(1)}, bf16[256,256]{1,0:T(8,128)(2,1)S(1)}, f32[144,128]{1,0:T(8,128)S(1)}, f32[12,256]{1,0:T(8,128)S(1)}) custom-call(f32[1,3]{1,0:T(1,128)S(1)} %bitcast.10, s32[1,72]{1,0:T(1,128)S(1)} %bitcast.11, f32[1,72]{1,0:T(1,128)S(1)} %bitcast.12, f32[32,192]{1,0:T(8,128)S(1)} %fusion.mask_ref), custom_call_target="tpu_custom_call" | custom-call | flops 2147483648 | bytes 262144 | tf_op jit(solution)/shard_map/pallas_call | solution.py:387
  17.1 0.1 pad_dynamic-slice_fusion.2
  17.2 0.0 collective-permute-done.near_ref
  17.2 0.0 collective-permute-done.1.far_ref
  17.2 1.7 %shard_map.87 = (bf16[2048,256]{1,0:T(8,128)(2,1)S(1)}, bf16[1280,256]{1,0:T(8,128)(2,1)S(1)}, bf16[480,256]{1,0:T(8,128)(2,1)S(1)}, f32[2,64,128]{2,1,0:T(8,128)S(1)}, f32[2,8,256]{2,1,0:T(8,128)S(1)}) custom-call(bf16[1024,128]{1,0:T(8,128)(2,1)S(1)} %get-tuple-element.11.center, f32[32,192]{1,0:T(8,128)S(1)} %fusion.mask_ref, ...), custom_call_target="tpu_custom_call" | custom-call | flops 536870912 | bytes 2097152 | tf_op jit(solution)/shard_map/pallas_call | solution.py:411
  18.9 1.9 %collective-permute-done.5.other_ref = bf16[4,18,1152]{2,1,0:T(8,128)(2,1)S(1)} collective-permute-done((bf16[4,18,1152]{2,1,0:T(8,128)(2,1)S(1)}, bf16[4,18,1152]{2,1,0:T(8,128)(2,1)S(1)}, u32[]{:S(2)}, u32[]{:S(2)}) %collective-permute-start.5) | collective-permute-done | bytes 165920 | tf_op jit(solution)/shard_map/ppermute | solution.py:501
  20.7 8.2 %shard_map.88 = (f32[32,128]{1,0:T(8,128)}, f32[3,32,128]{2,1,0:T(8,128)}) custom-call(bf16[2048,256]{1,0:T(8,128)(2,1)S(1)} %get-tuple-element.12.main_t, bf16[1280,256]{1,0:T(8,128)(2,1)S(1)} %get-tuple-element.13.side_t, bf16[480,256]{1,0:T(8,128)(2,1)S(1)} %get-tuple-element.14.e_ref, f32[2,64,128]{2,1,0:T(8,128)S(1)} %get-tuple-element.15.tgt_main, ...), custom_call_target="tpu_custom_call" | custom-call | tf_op jit(solution)/shard_map/pallas_call | solution.py:435
  (2 shorter events, 0.0 us)
Async XLA Ops:
  2.1 5.7 %copy-start.4 = (s32[32,1024]{1,0:T(8,128)S(1)}, s32[32,1024]{1,0:T(8,128)}, u32[]{:S(2)}) copy-start(s32[32,1024]{1,0:T(8,128)} %param.11) | copy-start | bytes 393220
  2.2 12.4 %collective-permute-start.2 = (bf16[18,1152]{1,0:T(8,128)(2,1)S(1)}, bf16[18,1152]{1,0:T(8,128)(2,1)S(1)}, u32[]{:S(2)}, u32[]{:S(2)}) collective-permute-start(bf16[18,1152]{1,0:T(8,128)(2,1)S(1)} %concatenate.19), channel_id=1, source_target_pairs={{0,32},{16,48},{32,0},{48,16},{64,96},{80,112},{96,64},{112,80},{1... | collective-permute-start | bytes 124424 | tf_op jit(solution)/shard_map/ppermute | solution.py:499
  4.3 10.4 %collective-permute-start.3 = (bf16[18,1152]{1,0:T(8,128)(2,1)S(1)}, bf16[18,1152]{1,0:T(8,128)(2,1)S(1)}, u32[]{:S(2)}, u32[]{:S(2)}) collective-permute-start(bf16[18,1152]{1,0:T(8,128)(2,1)S(1)} %concatenate.19), channel_id=1, source_target_pairs={{0,64},{16,80},{32,96},{48,112},{64,0},{80,16},{96,32},{112,48},{1... | collective-permute-start | bytes 124424 | tf_op jit(solution)/shard_map/ppermute | solution.py:499
  7.9 6.8 %collective-permute-start.4 = (bf16[18,1152]{1,0:T(8,128)(2,1)S(1)}, bf16[18,1152]{1,0:T(8,128)(2,1)S(1)}, u32[]{:S(2)}, u32[]{:S(2)}) collective-permute-start(bf16[18,1152]{1,0:T(8,128)(2,1)S(1)} %concatenate.19), channel_id=1, source_target_pairs={{0,96},{16,112},{32,64},{48,80},{64,32},{80,48},{96,0},{112,16},{1... | collective-permute-start | bytes 124424 | tf_op jit(solution)/shard_map/ppermute | solution.py:499
  7.9 0.8 %copy-start.5 = (bf16[32,1024]{1,0:T(8,128)(2,1)S(1)}, bf16[32,1024]{1,0:T(8,128)(2,1)}, u32[]{:S(2)}) copy-start(bf16[32,1024]{1,0:T(8,128)(2,1)} %param.7) | copy-start | bytes 196612
  7.9 0.9 %copy-start.3 = (f32[32,1024]{1,0:T(8,128)S(1)}, f32[32,1024]{1,0:T(8,128)}, u32[]{:S(2)}) copy-start(f32[32,1024]{1,0:T(8,128)} %param.12) | copy-start | bytes 393220
  9.0 8.2 %collective-permute-start = (f32[32,352]{1,0:T(8,128)S(1)}, f32[32,352]{1,0:T(8,128)S(1)}, u32[]{:S(2)}, u32[]{:S(2)}) collective-permute-start(f32[32,352]{1,0:T(8,128)S(1)} %get-tuple-element.25), channel_id=1, source_target_pairs={{0,1},{1,0},{2,3},{3,2},{4,5},{5,4},{6,7},{7,6},{8,9},{9,8},{10,11... | collective-permute-start | bytes 135176 | tf_op jit(solution)/shard_map/ppermute | solution.py:493
  9.1 8.1 %collective-permute-start.1 = (f32[32,352]{1,0:T(8,128)S(1)}, f32[32,352]{1,0:T(8,128)S(1)}, u32[]{:S(2)}, u32[]{:S(2)}) collective-permute-start(f32[32,352]{1,0:T(8,128)S(1)} %get-tuple-element.24), channel_id=1, source_target_pairs={{1,2},{2,1},{3,4},{4,3},{5,6},{6,5},{7,8},{8,7},{9,10},{10,9},{11,... | collective-permute-start | bytes 135176 | tf_op jit(solution)/shard_map/ppermute | solution.py:494
  14.7 6.0 %collective-permute-start.5 = (bf16[4,18,1152]{2,1,0:T(8,128)(2,1)S(1)}, bf16[4,18,1152]{2,1,0:T(8,128)(2,1)S(1)}, u32[]{:S(2)}, u32[]{:S(2)}) collective-permute-start(bf16[4,18,1152]{2,1,0:T(8,128)(2,1)S(1)} %pad_maximum_fusion.four_ref), channel_id=1, source_target_pairs={{0,16},{16,0},{32,48},{48,32},{64,80},{80,64},{96,112},{112,96},{1... | collective-permute-start | bytes 497672 | tf_op jit(solution)/shard_map/ppermute | solution.py:501
  15.4 0.7 %copy-start = (f32[3]{0:T(128)S(1)}, f32[3]{0:T(128)}, u32[]{:S(2)}) copy-start(f32[3]{0:T(128)} %param.13) | copy-start | bytes 40
  15.4 0.7 %copy-start.1 = (s32[72]{0:T(128)S(1)}, s32[72]{0:T(128)}, u32[]{:S(2)}) copy-start(s32[72]{0:T(128)} %param.10) | copy-start | bytes 868
  15.4 0.7 %copy-start.2 = (f32[72]{0:T(128)S(1)}, f32[72]{0:T(128)}, u32[]{:S(2)}) copy-start(f32[72]{0:T(128)} %param.9) | copy-start | bytes 868

commit v5 on v4

--- a/solution.py
+++ b/solution.py
@@ -57,10 +57,11 @@
     both_ref[1:2, 0:72] = eigen_vm[...]
     listed = jnp.transpose(both_ref[...])
     slot = iota((1, 256), 1)
-    block = slot >> 5
-    holder = me ^ (2 * (block & 3) + (block >> 2))
-    inside = (slot & 31) < 18
-    system = jnp.where(inside, 9 * holder + ((slot & 31) >> 1), -1)
+    place = slot & 127
+    block = (place >= 18).astype(jnp.int32) + (place >= 36) + (place >= 54)
+    holder = me ^ (2 * block + (slot >> 7))
+    inside = place < 72
+    system = jnp.where(inside, 9 * holder + ((place - 18 * block) >> 1), -1)
     here = iota((128, 256), 0) == system
     frow = jnp.sum(jnp.where(here, listed[:, 0:1], 0.0), axis=0, keepdims=True)
     frow = jnp.where(inside, frow, -1.0)
@@ -168,9 +169,8 @@
     eig = eig_ref[:, 0:1]
 
     raw_ref[...] = jnp.zeros_like(raw_ref)
-    for s in range(4):
-        raw_ref[32 * s : 32 * s + 18, :] = four_ref[s]
-        raw_ref[32 * s + 128 : 32 * s + 146, :] = other_ref[s]
+    raw_ref[0:72, :] = four_ref[...]
+    raw_ref[128:200, :] = other_ref[...]
     taps_f = jnp.dot(pick_ref[...], raw_ref[...], preferred_element_type=F32)
     taps_t = jnp.transpose(taps_f)
     blank = jnp.zeros((32, 128), BF16)
@@ -489,16 +489,27 @@
         return jnp.concatenate([columns(mask, 32), jnp.concatenate(edges, axis=0)], axis=1)
 
     near_pairs = [(i, i ^ 1) for i in range(strips)]
-    far_pairs = [((i + 1) % strips, ((i ^ 1) + 1) % strips) for i in range(strips)]
+    far_pairs = []
+    for k in range(8):
+        for i in range(strips):
+            if i in (0, strips - 1):
+                far_pairs.append((k * strips + i, (k ^ 1) * strips + i))
+            else:
+                far_pairs.append((k * strips + i, k * strips + ((i - 1) ^ 1) + 1))
     near = lax.ppermute(rim_rows(16 - 16 * odd), "strip", near_pairs)
-    far = lax.ppermute(rim_rows(16 * odd), "strip", far_pairs)
+    far = lax.ppermute(rim_rows(16 * odd), ("kern", "strip"), far_pairs)
 
     taps = flat_taps(kernels)
-    four = jnp.stack(
+    four = jnp.concatenate(
         [taps]
         + [lax.ppermute(taps, "kern", [(i, i ^ (2 * s)) for i in range(8)]) for s in range(1, 4)]
     )
-    other = lax.ppermute(four, "kern", [(i, i ^ 1) for i in range(8)])
+    beside = [
+        (k * strips + s, (k ^ 1) * strips + (s ^ (strips // 2) if s % 2 else s))
+        for k in range(8)
+        for s in range(strips)
+    ]
+    other = lax.ppermute(four, ("kern", "strip"), beside)
 
     own_mask = columns(mask, 32)
     center, *order = own_call(

time: 29.1 us -> 27.1 us (0.931)
  starting transfers between devices: 12 us -> 8.85 us
  waiting for transfers between devices: 1.89 us -> 2.96 us
    ppermute x2, starting transfers between devices: 6.25 us -> 3.14 us  [the longest x1 1.57 us: on_device(): far = lax.ppermute(rim_rows(16 * odd), ('kern', 'strip'), far_pairs)]
    ppermute x3, waiting for transfers between devices: 0.01 us -> 2.57 us  [on_device(): lax.ppermute(taps, 'kern', [(i, i ^ 2 * s) for i in range(8)])]
    ppermute x2, waiting for transfers between devices: 1.88 us -> 0.39 us  [the longest x1 0.39 us: on_device(): other = lax.ppermute(four, ('kern', 'strip'), beside)]
  transfers between devices with their start and end apart: 6 -> 6, of which waited for: 1 -> 2; matrix products, arithmetic and copies ran while one was open for 1% -> 2% of each run, Pallas kernels for 9% -> 10%
where the time goes in v5:
time: 27.1 us; the launch traced here: 26.9 us
  Pallas kernels  10.8 us (40%)
  starting transfers between devices  8.85 us (33%)
  local copies, waits for them, and re-layouts  3.26 us (12%)
  waiting for transfers between devices  2.96 us (11%)
  between operations  0.75 us (3%)
    pallas_call x1, Pallas kernels, step_call(): pl.pallas_call(step_kernel, out_shape=(jax.ShapeDtypeStruct((32, 128), F3...  8.19 us
    ppermute x3, starting transfers between devices, on_device(): lax.ppermute(taps, 'kern', [(i, i ^ 2 * s) for i in range(8)])  5.62 us
    unnamed x14, local copies, waits for them, and re-layouts  2.72 us
    ppermute x3, waiting for transfers between devices, on_device(): lax.ppermute(taps, 'kern', [(i, i ^ 2 * s) for i in range(8)])  2.57 us
    pallas_call x1, Pallas kernels, spread_call(): pl.pallas_call(spread_kernel, out_shape=(jax.ShapeDtypeStruct((2048, 256)...  1.65 us
    ppermute x1, starting transfers between devices, on_device(): far = lax.ppermute(rim_rows(16 * odd), ('kern', 'strip'), far_pairs)  1.57 us
    ppermute x1, starting transfers between devices, on_device(): other = lax.ppermute(four, ('kern', 'strip'), beside)  1.57 us
    pallas_call x1, Pallas kernels, own_call(): pl.pallas_call(own_kernel, out_shape=(jax.ShapeDtypeStruct((1024, 128), B...  1 us
  transfers between devices with their start and end apart: 6, of which 2 were waited for; matrix products, arithmetic and copies ran while one was open for 2% of the time, Pallas kernels for 10%

profile of v5, /device:TPU:0, one launch (start us, length us, event | category | flops | bytes accessed | tf_op | source)
XLA Modules:
  0.0 26.9 jit_solution(17842474935893269053)
XLA Ops:
  0.6 0.9 %copy.10 = bf16[9,2,33,33]{3,2,1,0:T(8,128)(2,1)S(1)} copy(bf16[9,2,33,33]{3,1,2,0:T(2,128)(2,1)} %param.8) | data formatting | bytes 78408 | tf_op args[1]
  1.6 0.1 slice.9
  1.7 0.3 copy.12
  2.0 0.2 reshape.23
  2.1 0.0 copy-start.4
  2.1 0.1 concatenate.22
  2.2 2.0 %collective-permute-start.2 = (bf16[18,1152]{1,0:T(8,128)(2,1)S(1)}, bf16[18,1152]{1,0:T(8,128)(2,1)S(1)}, u32[]{:S(2)}, u32[]{:S(2)}) collective-permute-start(bf16[18,1152]{1,0:T(8,128)(2,1)S(1)} %concatenate.22), channel_id=1, source_target_pairs={{0,32},{16,48},{32,0},{48,16},{64,96},{80,112},{96,64},{112,80},{1... | collective-permute-start | bytes 124424 | tf_op jit(solution)/shard_map/ppermute | solution.py:505
  4.3 3.6 %collective-permute-start.3 = (bf16[18,1152]{1,0:T(8,128)(2,1)S(1)}, bf16[18,1152]{1,0:T(8,128)(2,1)S(1)}, u32[]{:S(2)}, u32[]{:S(2)}) collective-permute-start(bf16[18,1152]{1,0:T(8,128)(2,1)S(1)} %concatenate.22), channel_id=1, source_target_pairs={{0,64},{16,80},{32,96},{48,112},{64,0},{80,16},{96,32},{112,48},{1... | collective-permute-start | bytes 124424 | tf_op jit(solution)/shard_map/ppermute | solution.py:505
  7.9 0.0 collective-permute-start.4
  7.9 0.0 copy-done.4
  7.9 0.0 copy-start.5
  7.9 0.0 copy-start.3
  7.9 0.8 %copy-done.5 = bf16[32,1024]{1,0:T(8,128)(2,1)S(1)} copy-done((bf16[32,1024]{1,0:T(8,128)(2,1)S(1)}, bf16[32,1024]{1,0:T(8,128)(2,1)}, u32[]{:S(2)}) %copy-start.5) | copy-done | bytes 65560
  8.7 0.1 fusion.mask_ref
  8.8 0.0 copy-done.3
  8.8 0.1 pad_dynamic-slice_fusion
  8.9 0.1 pad_maximum_fusion.1
  9.0 0.1 collective-permute-start
  9.1 1.6 %collective-permute-start.1 = (f32[32,352]{1,0:T(8,128)S(1)}, f32[32,352]{1,0:T(8,128)S(1)}, u32[]{:S(2)}, u32[]{:S(2)}) collective-permute-start(f32[32,352]{1,0:T(8,128)S(1)} %get-tuple-element.24), channel_id=1, source_target_pairs={{0,16},{1,2},{2,1},{3,4},{4,3},{5,6},{6,5},{7,8},{8,7},{9,10},{10,... | collective-permute-start | bytes 135176 | tf_op jit(solution)/shard_map/ppermute | solution.py:500
  10.7 0.0 collective-permute-done.2
  10.7 0.0 collective-permute-done.3
  10.7 2.6 %collective-permute-done.4 = bf16[18,1152]{1,0:T(8,128)(2,1)S(1)} collective-permute-done((bf16[18,1152]{1,0:T(8,128)(2,1)S(1)}, bf16[18,1152]{1,0:T(8,128)(2,1)S(1)}, u32[]{:S(2)}, u32[]{:S(2)}) %collective-permute-start.4) | collective-permute-done | bytes 41504 | tf_op jit(solution)/shard_map/ppermute | solution.py:505
  13.2 0.1 pad_maximum_fusion.four_ref
  13.3 1.6 %collective-permute-start.5 = (bf16[72,1152]{1,0:T(8,128)(2,1)S(1)}, bf16[72,1152]{1,0:T(8,128)(2,1)S(1)}, u32[]{:S(2)}, u32[]{:S(2)}) collective-permute-start(bf16[72,1152]{1,0:T(8,128)(2,1)S(1)} %pad_maximum_fusion.four_ref), channel_id=1, source_target_pairs={{0,16},{1,25},{2,18},{3,27},{4,20},{5,29},{6,22},{7,31},{8,24},{9,... | collective-permute-start | bytes 497672 | tf_op jit(solution)/shard_map/ppermute | solution.py:512
  14.9 0.0 copy-start
  14.9 0.0 copy-start.1
  14.9 0.0 copy-start.2
  14.9 0.6 %copy-done = f32[3]{0:T(128)S(1)} copy-done((f32[3]{0:T(128)S(1)}, f32[3]{0:T(128)}, u32[]{:S(2)}) %copy-start) | copy-done | bytes 36
  15.5 0.0 copy-done.1
  15.5 0.0 copy-done.2
  15.5 1.0 %shard_map.86 = (bf16[1024,128]{1,0:T(8,128)(2,1)S(1)}, bf16[256,256]{1,0:T(8,128)(2,1)S(1)}, f32[144,128]{1,0:T(8,128)S(1)}, f32[12,256]{1,0:T(8,128)S(1)}) custom-call(f32[1,3]{1,0:T(1,128)S(1)} %bitcast.6, s32[1,72]{1,0:T(1,128)S(1)} %bitcast.7, f32[1,72]{1,0:T(1,128)S(1)} %bitcast.8, f32[32,192]{1,0:T(8,128)S(1)} %fusion.mask_ref), custom_call_target="tpu_custom_call" | custom-call | flops 2147483648 | bytes 262144 | tf_op jit(solution)/shard_map/pallas_call | solution.py:387
  16.6 0.1 pad_dynamic-slice_fusion.2
  16.6 0.0 collective-permute-done.near_ref
  16.7 0.0 collective-permute-done.1.far_ref
  16.7 1.7 %shard_map.87 = (bf16[2048,256]{1,0:T(8,128)(2,1)S(1)}, bf16[1280,256]{1,0:T(8,128)(2,1)S(1)}, bf16[480,256]{1,0:T(8,128)(2,1)S(1)}, f32[2,64,128]{2,1,0:T(8,128)S(1)}, f32[2,8,256]{2,1,0:T(8,128)S(1)}) custom-call(bf16[1024,128]{1,0:T(8,128)(2,1)S(1)} %get-tuple-element.11.center, f32[32,192]{1,0:T(8,128)S(1)} %fusion.mask_ref, ...), custom_call_target="tpu_custom_call" | custom-call | flops 536870912 | bytes 2097152 | tf_op jit(solution)/shard_map/pallas_call | solution.py:411
  18.3 0.4 %collective-permute-done.5.other_ref = bf16[72,1152]{1,0:T(8,128)(2,1)S(1)} collective-permute-done((bf16[72,1152]{1,0:T(8,128)(2,1)S(1)}, bf16[72,1152]{1,0:T(8,128)(2,1)S(1)}, u32[]{:S(2)}, u32[]{:S(2)}) %collective-permute-start.5) | collective-permute-done | bytes 165920 | tf_op jit(solution)/shard_map/ppermute | solution.py:512
  18.7 8.2 %shard_map.88 = (f32[32,128]{1,0:T(8,128)}, f32[3,32,128]{2,1,0:T(8,128)}) custom-call(bf16[2048,256]{1,0:T(8,128)(2,1)S(1)} %get-tuple-element.12.main_t, bf16[1280,256]{1,0:T(8,128)(2,1)S(1)} %get-tuple-element.13.side_t, bf16[480,256]{1,0:T(8,128)(2,1)S(1)} %get-tuple-element.14.e_ref, f32[2,64,128]{2,1,0:T(8,128)S(1)} %get-tuple-element.15.tgt_main, ...), custom_call_target="tpu_custom_call" | custom-call | tf_op jit(solution)/shard_map/pallas_call | solution.py:435
  (2 shorter events, 0.0 us)
Async XLA Ops:
  2.1 5.7 %copy-start.4 = (s32[32,1024]{1,0:T(8,128)S(1)}, s32[32,1024]{1,0:T(8,128)}, u32[]{:S(2)}) copy-start(s32[32,1024]{1,0:T(8,128)} %param.11) | copy-start | bytes 393220
  2.2 8.4 %collective-permute-start.2 = (bf16[18,1152]{1,0:T(8,128)(2,1)S(1)}, bf16[18,1152]{1,0:T(8,128)(2,1)S(1)}, u32[]{:S(2)}, u32[]{:S(2)}) collective-permute-start(bf16[18,1152]{1,0:T(8,128)(2,1)S(1)} %concatenate.22), channel_id=1, source_target_pairs={{0,32},{16,48},{32,0},{48,16},{64,96},{80,112},{96,64},{112,80},{1... | collective-permute-start | bytes 124424 | tf_op jit(solution)/shard_map/ppermute | solution.py:505
  4.3 6.4 %collective-permute-start.3 = (bf16[18,1152]{1,0:T(8,128)(2,1)S(1)}, bf16[18,1152]{1,0:T(8,128)(2,1)S(1)}, u32[]{:S(2)}, u32[]{:S(2)}) collective-permute-start(bf16[18,1152]{1,0:T(8,128)(2,1)S(1)} %concatenate.22), channel_id=1, source_target_pairs={{0,64},{16,80},{32,96},{48,112},{64,0},{80,16},{96,32},{112,48},{1... | collective-permute-start | bytes 124424 | tf_op jit(solution)/shard_map/ppermute | solution.py:505
  7.9 5.4 %collective-permute-start.4 = (bf16[18,1152]{1,0:T(8,128)(2,1)S(1)}, bf16[18,1152]{1,0:T(8,128)(2,1)S(1)}, u32[]{:S(2)}, u32[]{:S(2)}) collective-permute-start(bf16[18,1152]{1,0:T(8,128)(2,1)S(1)} %concatenate.22), channel_id=1, source_target_pairs={{0,96},{16,112},{32,64},{48,80},{64,32},{80,48},{96,0},{112,16},{1... | collective-permute-start | bytes 124424 | tf_op jit(solution)/shard_map/ppermute | solution.py:505
  7.9 0.8 %copy-start.5 = (bf16[32,1024]{1,0:T(8,128)(2,1)S(1)}, bf16[32,1024]{1,0:T(8,128)(2,1)}, u32[]{:S(2)}) copy-start(bf16[32,1024]{1,0:T(8,128)(2,1)} %param.7) | copy-start | bytes 196612
  7.9 0.9 %copy-start.3 = (f32[32,1024]{1,0:T(8,128)S(1)}, f32[32,1024]{1,0:T(8,128)}, u32[]{:S(2)}) copy-start(f32[32,1024]{1,0:T(8,128)} %param.12) | copy-start | bytes 393220
  9.0 7.7 %collective-permute-start = (f32[32,352]{1,0:T(8,128)S(1)}, f32[32,352]{1,0:T(8,128)S(1)}, u32[]{:S(2)}, u32[]{:S(2)}) collective-permute-start(f32[32,352]{1,0:T(8,128)S(1)} %get-tuple-element.25), channel_id=1, source_target_pairs={{0,1},{1,0},{2,3},{3,2},{4,5},{5,4},{6,7},{7,6},{8,9},{9,8},{10,11... | collective-permute-start | bytes 135176 | tf_op jit(solution)/shard_map/ppermute | solution.py:499
  9.1 7.6 %collective-permute-start.1 = (f32[32,352]{1,0:T(8,128)S(1)}, f32[32,352]{1,0:T(8,128)S(1)}, u32[]{:S(2)}, u32[]{:S(2)}) collective-permute-start(f32[32,352]{1,0:T(8,128)S(1)} %get-tuple-element.24), channel_id=1, source_target_pairs={{0,16},{1,2},{2,1},{3,4},{4,3},{5,6},{6,5},{7,8},{8,7},{9,10},{10,... | collective-permute-start | bytes 135176 | tf_op jit(solution)/shard_map/ppermute | solution.py:500
  13.3 5.4 %collective-permute-start.5 = (bf16[72,1152]{1,0:T(8,128)(2,1)S(1)}, bf16[72,1152]{1,0:T(8,128)(2,1)S(1)}, u32[]{:S(2)}, u32[]{:S(2)}) collective-permute-start(bf16[72,1152]{1,0:T(8,128)(2,1)S(1)} %pad_maximum_fusion.four_ref), channel_id=1, source_target_pairs={{0,16},{1,25},{2,18},{3,27},{4,20},{5,29},{6,22},{7,31},{8,24},{9,... | collective-permute-start | bytes 497672 | tf_op jit(solution)/shard_map/ppermute | solution.py:512
  14.9 0.7 %copy-start = (f32[3]{0:T(128)S(1)}, f32[3]{0:T(128)}, u32[]{:S(2)}) copy-start(f32[3]{0:T(128)} %param.13) | copy-start | bytes 40
  14.9 0.7 %copy-start.1 = (s32[72]{0:T(128)S(1)}, s32[72]{0:T(128)}, u32[]{:S(2)}) copy-start(s32[72]{0:T(128)} %param.10) | copy-start | bytes 868
  14.9 0.7 %copy-start.2 = (f32[72]{0:T(128)S(1)}, f32[72]{0:T(128)}, u32[]{:S(2)}) copy-start(f32[72]{0:T(128)} %param.9) | copy-start | bytes 868

commit v6 on v5

--- a/solution.py
+++ b/solution.py
@@ -17,9 +17,8 @@
 def skewed(eight, j, tap, lane):
     left = jnp.broadcast_to(eight[j : j + 1, 0:128], (32, 128))
     right = jnp.broadcast_to(eight[j : j + 1, 128:256], (32, 128))
-    left = pltpu.roll(left, 97, 1, stride=1, stride_axis=0)
-    right = pltpu.roll(right, 97, 1, stride=1, stride_axis=0)
-    return jnp.where(lane + 31 - tap < 128, left, right).astype(BF16)
+    both = jnp.where(lane < 31 - tap, right, left)
+    return pltpu.roll(both, 97, 1, stride=1, stride_axis=0).astype(BF16)
 
 
 def own_kernel(
@@ -136,14 +135,14 @@
     def spread_side(block, _):
         start = pl.multiple_of(block * 8, 8)
         lows, highs = lo_ref[pl.ds(start, 8), :], hi_ref[pl.ds(start, 8), :]
+        turned = [pltpu.roll(highs[:, 128 * h : 128 * h + 128], 32, 1) for h in range(2)]
         for j in range(8):
             for half in range(2):
                 cols = slice(128 * half, 128 * half + 128)
                 low = jnp.broadcast_to(lows[j : j + 1, cols], (32, 128))
-                high = jnp.broadcast_to(highs[j : j + 1, cols], (32, 128))
-                low = pltpu.roll(low, 97, 1, stride=1, stride_axis=0)
-                high = pltpu.roll(high, 1, 1, stride=1, stride_axis=0)
-                both = jnp.where((lane & 31) <= tap, low, high).astype(BF16)
+                high = jnp.broadcast_to(turned[half][j : j + 1], (32, 128))
+                both = jnp.where((lane & 31) >= 31 - tap, low, high)
+                both = pltpu.roll(both, 97, 1, stride=1, stride_axis=0).astype(BF16)
                 side_t[pl.ds(pl.multiple_of((block * 8 + j) * 32, 32), 32), cols] = both
         return 0
 
@@ -368,9 +367,8 @@
             edge = chosen if edge is None else edge + chosen
         edge = edge + pltpu.roll(edge, 64, 1)
         edge = edge + pltpu.roll(edge, 32, 1)
-        body = pltpu.roll(body, 96, 1, stride=1, stride_axis=0)
-        edge = pltpu.roll(edge, 96, 1, stride=1, stride_axis=0)
-        both = jnp.where(lane + 32 - tap < 128, body, edge)
+        both = jnp.where(lane < 32 - tap, edge, body)
+        both = pltpu.roll(both, 96, 1, stride=1, stride_axis=0)
         grad_ref[r : r + 1, :] = (
             jnp.sum(both, axis=0, keepdims=True)
             + d_ref[r + 32 : r + 33, 0:128]

time: 27.1 us -> 27.1 us (level)
  no operation moved by 1% of the time
where the time goes in v6:
time: 27.1 us; the launch traced here: 26.9 us
  Pallas kernels  10.9 us (40%)
  starting transfers between devices  8.85 us (33%)
  local copies, waits for them, and re-layouts  3.26 us (12%)
  waiting for transfers between devices  2.96 us (11%)
  between operations  0.75 us (3%)
    pallas_call x1, Pallas kernels, step_call(): pl.pallas_call(step_kernel, out_shape=(jax.ShapeDtypeStruct((32, 128), F3...  8.23 us
    ppermute x3, starting transfers between devices, on_device(): lax.ppermute(taps, 'kern', [(i, i ^ 2 * s) for i in range(8)])  5.62 us
    unnamed x14, local copies, waits for them, and re-layouts  2.72 us
    ppermute x3, waiting for transfers between devices, on_device(): lax.ppermute(taps, 'kern', [(i, i ^ 2 * s) for i in range(8)])  2.57 us
    pallas_call x1, Pallas kernels, spread_call(): pl.pallas_call(spread_kernel, out_shape=(jax.ShapeDtypeStruct((2048, 256)...  1.71 us
    ppermute x1, starting transfers between devices, on_device(): other = lax.ppermute(four, ('kern', 'strip'), beside)  1.57 us
    ppermute x1, starting transfers between devices, on_device(): far = lax.ppermute(rim_rows(16 * odd), ('kern', 'strip'), far_pairs)  1.57 us
    pallas_call x1, Pallas kernels, own_call(): pl.pallas_call(own_kernel, out_shape=(jax.ShapeDtypeStruct((1024, 128), B...  0.93 us
  transfers between devices with their start and end apart: 6, of which 2 were waited for; matrix products, arithmetic and copies ran while one was open for 2% of the time, Pallas kernels for 10%

profile of v6, /device:TPU:0, one launch (start us, length us, event | category | flops | bytes accessed | tf_op | source)
XLA Modules:
  0.0 26.9 jit_solution(11852145342362317159)
XLA Ops:
  0.6 0.9 %copy.10 = bf16[9,2,33,33]{3,2,1,0:T(8,128)(2,1)S(1)} copy(bf16[9,2,33,33]{3,1,2,0:T(2,128)(2,1)} %param.8) | data formatting | bytes 78408 | tf_op args[1]
  1.6 0.1 slice.9
  1.7 0.3 copy.12
  2.0 0.2 reshape.23
  2.1 0.0 copy-start.4
  2.1 0.1 concatenate.22
  2.2 2.0 %collective-permute-start.2 = (bf16[18,1152]{1,0:T(8,128)(2,1)S(1)}, bf16[18,1152]{1,0:T(8,128)(2,1)S(1)}, u32[]{:S(2)}, u32[]{:S(2)}) collective-permute-start(bf16[18,1152]{1,0:T(8,128)(2,1)S(1)} %concatenate.22), channel_id=1, source_target_pairs={{0,32},{16,48},{32,0},{48,16},{64,96},{80,112},{96,64},{112,80},{1... | collective-permute-start | bytes 124424 | tf_op jit(solution)/shard_map/ppermute | solution.py:503
  4.3 3.6 %collective-permute-start.3 = (bf16[18,1152]{1,0:T(8,128)(2,1)S(1)}, bf16[18,1152]{1,0:T(8,128)(2,1)S(1)}, u32[]{:S(2)}, u32[]{:S(2)}) collective-permute-start(bf16[18,1152]{1,0:T(8,128)(2,1)S(1)} %concatenate.22), channel_id=1, source_target_pairs={{0,64},{16,80},{32,96},{48,112},{64,0},{80,16},{96,32},{112,48},{1... | collective-permute-start | bytes 124424 | tf_op jit(solution)/shard_map/ppermute | solution.py:503
  7.9 0.0 collective-permute-start.4
  7.9 0.0 copy-done.4
  7.9 0.0 copy-start.5
  7.9 0.0 copy-start.3
  7.9 0.8 %copy-done.5 = bf16[32,1024]{1,0:T(8,128)(2,1)S(1)} copy-done((bf16[32,1024]{1,0:T(8,128)(2,1)S(1)}, bf16[32,1024]{1,0:T(8,128)(2,1)}, u32[]{:S(2)}) %copy-start.5) | copy-done | bytes 65560
  8.7 0.1 fusion.mask_ref
  8.8 0.0 copy-done.3
  8.8 0.1 pad_dynamic-slice_fusion
  8.9 0.1 pad_maximum_fusion.1
  9.0 0.1 collective-permute-start
  9.1 1.6 %collective-permute-start.1 = (f32[32,352]{1,0:T(8,128)S(1)}, f32[32,352]{1,0:T(8,128)S(1)}, u32[]{:S(2)}, u32[]{:S(2)}) collective-permute-start(f32[32,352]{1,0:T(8,128)S(1)} %get-tuple-element.24), channel_id=1, source_target_pairs={{0,16},{1,2},{2,1},{3,4},{4,3},{5,6},{6,5},{7,8},{8,7},{9,10},{10,... | collective-permute-start | bytes 135176 | tf_op jit(solution)/shard_map/ppermute | solution.py:498
  10.7 0.0 collective-permute-done.2
  10.7 0.0 collective-permute-done.3
  10.7 2.6 %collective-permute-done.4 = bf16[18,1152]{1,0:T(8,128)(2,1)S(1)} collective-permute-done((bf16[18,1152]{1,0:T(8,128)(2,1)S(1)}, bf16[18,1152]{1,0:T(8,128)(2,1)S(1)}, u32[]{:S(2)}, u32[]{:S(2)}) %collective-permute-start.4) | collective-permute-done | bytes 41504 | tf_op jit(solution)/shard_map/ppermute | solution.py:503
  13.2 0.1 pad_maximum_fusion.four_ref
  13.3 1.6 %collective-permute-start.5 = (bf16[72,1152]{1,0:T(8,128)(2,1)S(1)}, bf16[72,1152]{1,0:T(8,128)(2,1)S(1)}, u32[]{:S(2)}, u32[]{:S(2)}) collective-permute-start(bf16[72,1152]{1,0:T(8,128)(2,1)S(1)} %pad_maximum_fusion.four_ref), channel_id=1, source_target_pairs={{0,16},{1,25},{2,18},{3,27},{4,20},{5,29},{6,22},{7,31},{8,24},{9,... | collective-permute-start | bytes 497672 | tf_op jit(solution)/shard_map/ppermute | solution.py:510
  14.9 0.0 copy-start
  14.9 0.0 copy-start.1
  14.9 0.0 copy-start.2
  14.9 0.6 %copy-done = f32[3]{0:T(128)S(1)} copy-done((f32[3]{0:T(128)S(1)}, f32[3]{0:T(128)}, u32[]{:S(2)}) %copy-start) | copy-done | bytes 36
  15.5 0.0 copy-done.1
  15.5 0.0 copy-done.2
  15.5 0.9 %shard_map.86 = (bf16[1024,128]{1,0:T(8,128)(2,1)S(1)}, bf16[256,256]{1,0:T(8,128)(2,1)S(1)}, f32[144,128]{1,0:T(8,128)S(1)}, f32[12,256]{1,0:T(8,128)S(1)}) custom-call(f32[1,3]{1,0:T(1,128)S(1)} %bitcast.6, s32[1,72]{1,0:T(1,128)S(1)} %bitcast.7, f32[1,72]{1,0:T(1,128)S(1)} %bitcast.8, f32[32,192]{1,0:T(8,128)S(1)} %fusion.mask_ref), custom_call_target="tpu_custom_call" | custom-call | flops 2147483648 | bytes 262144 | tf_op jit(solution)/shard_map/pallas_call | solution.py:385
  16.5 0.1 pad_dynamic-slice_fusion.2
  16.6 0.0 collective-permute-done.near_ref
  16.6 0.0 collective-permute-done.1.far_ref
  16.6 1.7 %shard_map.87 = (bf16[2048,256]{1,0:T(8,128)(2,1)S(1)}, bf16[1280,256]{1,0:T(8,128)(2,1)S(1)}, bf16[480,256]{1,0:T(8,128)(2,1)S(1)}, f32[2,64,128]{2,1,0:T(8,128)S(1)}, f32[2,8,256]{2,1,0:T(8,128)S(1)}) custom-call(bf16[1024,128]{1,0:T(8,128)(2,1)S(1)} %get-tuple-element.11.center, f32[32,192]{1,0:T(8,128)S(1)} %fusion.mask_ref, ...), custom_call_target="tpu_custom_call" | custom-call | flops 536870912 | bytes 2097152 | tf_op jit(solution)/shard_map/pallas_call | solution.py:409
  18.3 0.4 %collective-permute-done.5.other_ref = bf16[72,1152]{1,0:T(8,128)(2,1)S(1)} collective-permute-done((bf16[72,1152]{1,0:T(8,128)(2,1)S(1)}, bf16[72,1152]{1,0:T(8,128)(2,1)S(1)}, u32[]{:S(2)}, u32[]{:S(2)}) %collective-permute-start.5) | collective-permute-done | bytes 165920 | tf_op jit(solution)/shard_map/ppermute | solution.py:510
  18.7 8.2 %shard_map.88 = (f32[32,128]{1,0:T(8,128)}, f32[3,32,128]{2,1,0:T(8,128)}) custom-call(bf16[2048,256]{1,0:T(8,128)(2,1)S(1)} %get-tuple-element.12.main_t, bf16[1280,256]{1,0:T(8,128)(2,1)S(1)} %get-tuple-element.13.side_t, bf16[480,256]{1,0:T(8,128)(2,1)S(1)} %get-tuple-element.14.e_ref, f32[2,64,128]{2,1,0:T(8,128)S(1)} %get-tuple-element.15.tgt_main, ...), custom_call_target="tpu_custom_call" | custom-call | tf_op jit(solution)/shard_map/pallas_call | solution.py:433
  (2 shorter events, 0.0 us)
Async XLA Ops:
  2.1 5.7 %copy-start.4 = (s32[32,1024]{1,0:T(8,128)S(1)}, s32[32,1024]{1,0:T(8,128)}, u32[]{:S(2)}) copy-start(s32[32,1024]{1,0:T(8,128)} %param.11) | copy-start | bytes 393220
  2.2 8.4 %collective-permute-start.2 = (bf16[18,1152]{1,0:T(8,128)(2,1)S(1)}, bf16[18,1152]{1,0:T(8,128)(2,1)S(1)}, u32[]{:S(2)}, u32[]{:S(2)}) collective-permute-start(bf16[18,1152]{1,0:T(8,128)(2,1)S(1)} %concatenate.22), channel_id=1, source_target_pairs={{0,32},{16,48},{32,0},{48,16},{64,96},{80,112},{96,64},{112,80},{1... | collective-permute-start | bytes 124424 | tf_op jit(solution)/shard_map/ppermute | solution.py:503
  4.3 6.4 %collective-permute-start.3 = (bf16[18,1152]{1,0:T(8,128)(2,1)S(1)}, bf16[18,1152]{1,0:T(8,128)(2,1)S(1)}, u32[]{:S(2)}, u32[]{:S(2)}) collective-permute-start(bf16[18,1152]{1,0:T(8,128)(2,1)S(1)} %concatenate.22), channel_id=1, source_target_pairs={{0,64},{16,80},{32,96},{48,112},{64,0},{80,16},{96,32},{112,48},{1... | collective-permute-start | bytes 124424 | tf_op jit(solution)/shard_map/ppermute | solution.py:503
  7.9 5.4 %collective-permute-start.4 = (bf16[18,1152]{1,0:T(8,128)(2,1)S(1)}, bf16[18,1152]{1,0:T(8,128)(2,1)S(1)}, u32[]{:S(2)}, u32[]{:S(2)}) collective-permute-start(bf16[18,1152]{1,0:T(8,128)(2,1)S(1)} %concatenate.22), channel_id=1, source_target_pairs={{0,96},{16,112},{32,64},{48,80},{64,32},{80,48},{96,0},{112,16},{1... | collective-permute-start | bytes 124424 | tf_op jit(solution)/shard_map/ppermute | solution.py:503
  7.9 0.8 %copy-start.5 = (bf16[32,1024]{1,0:T(8,128)(2,1)S(1)}, bf16[32,1024]{1,0:T(8,128)(2,1)}, u32[]{:S(2)}) copy-start(bf16[32,1024]{1,0:T(8,128)(2,1)} %param.7) | copy-start | bytes 196612
  7.9 0.9 %copy-start.3 = (f32[32,1024]{1,0:T(8,128)S(1)}, f32[32,1024]{1,0:T(8,128)}, u32[]{:S(2)}) copy-start(f32[32,1024]{1,0:T(8,128)} %param.12) | copy-start | bytes 393220
  9.0 7.6 %collective-permute-start = (f32[32,352]{1,0:T(8,128)S(1)}, f32[32,352]{1,0:T(8,128)S(1)}, u32[]{:S(2)}, u32[]{:S(2)}) collective-permute-start(f32[32,352]{1,0:T(8,128)S(1)} %get-tuple-element.25), channel_id=1, source_target_pairs={{0,1},{1,0},{2,3},{3,2},{4,5},{5,4},{6,7},{7,6},{8,9},{9,8},{10,11... | collective-permute-start | bytes 135176 | tf_op jit(solution)/shard_map/ppermute | solution.py:497
  9.1 7.5 %collective-permute-start.1 = (f32[32,352]{1,0:T(8,128)S(1)}, f32[32,352]{1,0:T(8,128)S(1)}, u32[]{:S(2)}, u32[]{:S(2)}) collective-permute-start(f32[32,352]{1,0:T(8,128)S(1)} %get-tuple-element.24), channel_id=1, source_target_pairs={{0,16},{1,2},{2,1},{3,4},{4,3},{5,6},{6,5},{7,8},{8,7},{9,10},{10,... | collective-permute-start | bytes 135176 | tf_op jit(solution)/shard_map/ppermute | solution.py:498
  13.3 5.4 %collective-permute-start.5 = (bf16[72,1152]{1,0:T(8,128)(2,1)S(1)}, bf16[72,1152]{1,0:T(8,128)(2,1)S(1)}, u32[]{:S(2)}, u32[]{:S(2)}) collective-permute-start(bf16[72,1152]{1,0:T(8,128)(2,1)S(1)} %pad_maximum_fusion.four_ref), channel_id=1, source_target_pairs={{0,16},{1,25},{2,18},{3,27},{4,20},{5,29},{6,22},{7,31},{8,24},{9,... | collective-permute-start | bytes 497672 | tf_op jit(solution)/shard_map/ppermute | solution.py:510
  14.9 0.7 %copy-start = (f32[3]{0:T(128)S(1)}, f32[3]{0:T(128)}, u32[]{:S(2)}) copy-start(f32[3]{0:T(128)} %param.13) | copy-start | bytes 40
  14.9 0.7 %copy-start.1 = (s32[72]{0:T(128)S(1)}, s32[72]{0:T(128)}, u32[]{:S(2)}) copy-start(s32[72]{0:T(128)} %param.10) | copy-start | bytes 868
  14.9 0.7 %copy-start.2 = (f32[72]{0:T(128)S(1)}, f32[72]{0:T(128)}, u32[]{:S(2)}) copy-start(f32[72]{0:T(128)} %param.9) | copy-start | bytes 868

commit v7 on v5

--- a/solution.py
+++ b/solution.py
@@ -230,11 +230,8 @@
     scales = 2.0 * eigs * norm_scale
 
     def imaged(source, start, ones, tgt, wgt):
-        field = jnp.dot(
-            wf_ref[:, 0:1024], source[start : start + 1024, :], preferred_element_type=F32
-        )
-        tail = jnp.concatenate([source[start + 1024 : start + 1152, :], ones], axis=0)
-        field += jnp.dot(wf_ref[:, 1024:1200], tail, preferred_element_type=F32)
+        window = jnp.concatenate([source[start : start + 1152, :], ones], axis=0)
+        field = jnp.dot(wf_ref[:, 0:1200], window, preferred_element_type=F32)
         power = eigs * (field * field)
         planes = jnp.sum(power.reshape(12, 48, 256), axis=1)
         printed = 1.0 / (1.0 + jnp.exp(-STEEP * (norm_scale * planes - thr)))

time: 27.1 us -> 26.9 us (level)
  no operation moved by 1% of the time
where the time goes in v7:
time: 26.9 us; the launch traced here: 26.8 us
  Pallas kernels  10.7 us (40%)
  starting transfers between devices  8.85 us (33%)
  local copies, waits for them, and re-layouts  3.26 us (12%)
  waiting for transfers between devices  2.96 us (11%)
  between operations  0.75 us (3%)
    pallas_call x1, Pallas kernels, step_call(): pl.pallas_call(step_kernel, out_shape=(jax.ShapeDtypeStruct((32, 128), F3...  8.05 us
    ppermute x3, starting transfers between devices, on_device(): lax.ppermute(taps, 'kern', [(i, i ^ 2 * s) for i in range(8)])  5.62 us
    unnamed x14, local copies, waits for them, and re-layouts  2.72 us
    ppermute x3, waiting for transfers between devices, on_device(): lax.ppermute(taps, 'kern', [(i, i ^ 2 * s) for i in range(8)])  2.57 us
    pallas_call x1, Pallas kernels, spread_call(): pl.pallas_call(spread_kernel, out_shape=(jax.ShapeDtypeStruct((2048, 256)...  1.65 us
    ppermute x1, starting transfers between devices, on_device(): far = lax.ppermute(rim_rows(16 * odd), ('kern', 'strip'), far_pairs)  1.57 us
    ppermute x1, starting transfers between devices, on_device(): other = lax.ppermute(four, ('kern', 'strip'), beside)  1.57 us
    pallas_call x1, Pallas kernels, own_call(): pl.pallas_call(own_kernel, out_shape=(jax.ShapeDtypeStruct((1024, 128), B...  1 us
  transfers between devices with their start and end apart: 6, of which 2 were waited for; matrix products, arithmetic and copies ran while one was open for 2% of the time, Pallas kernels for 10%

profile of v7, /device:TPU:0, one launch (start us, length us, event | category | flops | bytes accessed | tf_op | source)
XLA Modules:
  0.0 26.8 jit_solution(8109488980551195788)
XLA Ops:
  0.6 0.9 %copy.10 = bf16[9,2,33,33]{3,2,1,0:T(8,128)(2,1)S(1)} copy(bf16[9,2,33,33]{3,1,2,0:T(2,128)(2,1)} %param.8) | data formatting | bytes 78408 | tf_op args[1]
  1.6 0.1 slice.9
  1.7 0.3 copy.12
  2.0 0.2 reshape.23
  2.1 0.0 copy-start.4
  2.1 0.1 concatenate.22
  2.2 2.0 %collective-permute-start.2 = (bf16[18,1152]{1,0:T(8,128)(2,1)S(1)}, bf16[18,1152]{1,0:T(8,128)(2,1)S(1)}, u32[]{:S(2)}, u32[]{:S(2)}) collective-permute-start(bf16[18,1152]{1,0:T(8,128)(2,1)S(1)} %concatenate.22), channel_id=1, source_target_pairs={{0,32},{16,48},{32,0},{48,16},{64,96},{80,112},{96,64},{112,80},{1... | collective-permute-start | bytes 124424 | tf_op jit(solution)/shard_map/ppermute | solution.py:502
  4.3 3.6 %collective-permute-start.3 = (bf16[18,1152]{1,0:T(8,128)(2,1)S(1)}, bf16[18,1152]{1,0:T(8,128)(2,1)S(1)}, u32[]{:S(2)}, u32[]{:S(2)}) collective-permute-start(bf16[18,1152]{1,0:T(8,128)(2,1)S(1)} %concatenate.22), channel_id=1, source_target_pairs={{0,64},{16,80},{32,96},{48,112},{64,0},{80,16},{96,32},{112,48},{1... | collective-permute-start | bytes 124424 | tf_op jit(solution)/shard_map/ppermute | solution.py:502
  7.9 0.0 collective-permute-start.4
  7.9 0.0 copy-done.4
  7.9 0.0 copy-start.5
  7.9 0.0 copy-start.3
  7.9 0.8 %copy-done.5 = bf16[32,1024]{1,0:T(8,128)(2,1)S(1)} copy-done((bf16[32,1024]{1,0:T(8,128)(2,1)S(1)}, bf16[32,1024]{1,0:T(8,128)(2,1)}, u32[]{:S(2)}) %copy-start.5) | copy-done | bytes 65560
  8.7 0.1 fusion.mask_ref
  8.8 0.0 copy-done.3
  8.8 0.1 pad_dynamic-slice_fusion
  8.9 0.1 pad_maximum_fusion.1
  9.0 0.1 collective-permute-start
  9.1 1.6 %collective-permute-start.1 = (f32[32,352]{1,0:T(8,128)S(1)}, f32[32,352]{1,0:T(8,128)S(1)}, u32[]{:S(2)}, u32[]{:S(2)}) collective-permute-start(f32[32,352]{1,0:T(8,128)S(1)} %get-tuple-element.24), channel_id=1, source_target_pairs={{0,16},{1,2},{2,1},{3,4},{4,3},{5,6},{6,5},{7,8},{8,7},{9,10},{10,... | collective-permute-start | bytes 135176 | tf_op jit(solution)/shard_map/ppermute | solution.py:497
  10.7 0.0 collective-permute-done.2
  10.7 0.0 collective-permute-done.3
  10.7 2.6 %collective-permute-done.4 = bf16[18,1152]{1,0:T(8,128)(2,1)S(1)} collective-permute-done((bf16[18,1152]{1,0:T(8,128)(2,1)S(1)}, bf16[18,1152]{1,0:T(8,128)(2,1)S(1)}, u32[]{:S(2)}, u32[]{:S(2)}) %collective-permute-start.4) | collective-permute-done | bytes 41504 | tf_op jit(solution)/shard_map/ppermute | solution.py:502
  13.2 0.1 pad_maximum_fusion.four_ref
  13.3 1.6 %collective-permute-start.5 = (bf16[72,1152]{1,0:T(8,128)(2,1)S(1)}, bf16[72,1152]{1,0:T(8,128)(2,1)S(1)}, u32[]{:S(2)}, u32[]{:S(2)}) collective-permute-start(bf16[72,1152]{1,0:T(8,128)(2,1)S(1)} %pad_maximum_fusion.four_ref), channel_id=1, source_target_pairs={{0,16},{1,25},{2,18},{3,27},{4,20},{5,29},{6,22},{7,31},{8,24},{9,... | collective-permute-start | bytes 497672 | tf_op jit(solution)/shard_map/ppermute | solution.py:509
  14.9 0.0 copy-start
  14.9 0.0 copy-start.1
  14.9 0.0 copy-start.2
  14.9 0.6 %copy-done = f32[3]{0:T(128)S(1)} copy-done((f32[3]{0:T(128)S(1)}, f32[3]{0:T(128)}, u32[]{:S(2)}) %copy-start) | copy-done | bytes 36
  15.5 0.0 copy-done.1
  15.5 0.0 copy-done.2
  15.5 1.0 %shard_map.86 = (bf16[1024,128]{1,0:T(8,128)(2,1)S(1)}, bf16[256,256]{1,0:T(8,128)(2,1)S(1)}, f32[144,128]{1,0:T(8,128)S(1)}, f32[12,256]{1,0:T(8,128)S(1)}) custom-call(f32[1,3]{1,0:T(1,128)S(1)} %bitcast.6, s32[1,72]{1,0:T(1,128)S(1)} %bitcast.7, f32[1,72]{1,0:T(1,128)S(1)} %bitcast.8, f32[32,192]{1,0:T(8,128)S(1)} %fusion.mask_ref), custom_call_target="tpu_custom_call" | custom-call | flops 2147483648 | bytes 262144 | tf_op jit(solution)/shard_map/pallas_call | solution.py:384
  16.6 0.1 pad_dynamic-slice_fusion.2
  16.6 0.0 collective-permute-done.near_ref
  16.7 0.0 collective-permute-done.1.far_ref
  16.7 1.7 %shard_map.87 = (bf16[2048,256]{1,0:T(8,128)(2,1)S(1)}, bf16[1280,256]{1,0:T(8,128)(2,1)S(1)}, bf16[480,256]{1,0:T(8,128)(2,1)S(1)}, f32[2,64,128]{2,1,0:T(8,128)S(1)}, f32[2,8,256]{2,1,0:T(8,128)S(1)}) custom-call(bf16[1024,128]{1,0:T(8,128)(2,1)S(1)} %get-tuple-element.11.center, f32[32,192]{1,0:T(8,128)S(1)} %fusion.mask_ref, ...), custom_call_target="tpu_custom_call" | custom-call | flops 536870912 | bytes 2097152 | tf_op jit(solution)/shard_map/pallas_call | solution.py:408
  18.3 0.4 %collective-permute-done.5.other_ref = bf16[72,1152]{1,0:T(8,128)(2,1)S(1)} collective-permute-done((bf16[72,1152]{1,0:T(8,128)(2,1)S(1)}, bf16[72,1152]{1,0:T(8,128)(2,1)S(1)}, u32[]{:S(2)}, u32[]{:S(2)}) %collective-permute-start.5) | collective-permute-done | bytes 165920 | tf_op jit(solution)/shard_map/ppermute | solution.py:509
  18.7 8.0 %shard_map.88 = (f32[32,128]{1,0:T(8,128)}, f32[3,32,128]{2,1,0:T(8,128)}) custom-call(bf16[2048,256]{1,0:T(8,128)(2,1)S(1)} %get-tuple-element.12.main_t, bf16[1280,256]{1,0:T(8,128)(2,1)S(1)} %get-tuple-element.13.side_t, bf16[480,256]{1,0:T(8,128)(2,1)S(1)} %get-tuple-element.14.e_ref, f32[2,64,128]{2,1,0:T(8,128)S(1)} %get-tuple-element.15.tgt_main, ...), custom_call_target="tpu_custom_call" | custom-call | tf_op jit(solution)/shard_map/pallas_call | solution.py:432
  (2 shorter events, 0.0 us)
Async XLA Ops:
  2.1 5.7 %copy-start.4 = (s32[32,1024]{1,0:T(8,128)S(1)}, s32[32,1024]{1,0:T(8,128)}, u32[]{:S(2)}) copy-start(s32[32,1024]{1,0:T(8,128)} %param.11) | copy-start | bytes 393220
  2.2 8.4 %collective-permute-start.2 = (bf16[18,1152]{1,0:T(8,128)(2,1)S(1)}, bf16[18,1152]{1,0:T(8,128)(2,1)S(1)}, u32[]{:S(2)}, u32[]{:S(2)}) collective-permute-start(bf16[18,1152]{1,0:T(8,128)(2,1)S(1)} %concatenate.22), channel_id=1, source_target_pairs={{0,32},{16,48},{32,0},{48,16},{64,96},{80,112},{96,64},{112,80},{1... | collective-permute-start | bytes 124424 | tf_op jit(solution)/shard_map/ppermute | solution.py:502
  4.3 6.4 %collective-permute-start.3 = (bf16[18,1152]{1,0:T(8,128)(2,1)S(1)}, bf16[18,1152]{1,0:T(8,128)(2,1)S(1)}, u32[]{:S(2)}, u32[]{:S(2)}) collective-permute-start(bf16[18,1152]{1,0:T(8,128)(2,1)S(1)} %concatenate.22), channel_id=1, source_target_pairs={{0,64},{16,80},{32,96},{48,112},{64,0},{80,16},{96,32},{112,48},{1... | collective-permute-start | bytes 124424 | tf_op jit(solution)/shard_map/ppermute | solution.py:502
  7.9 5.4 %collective-permute-start.4 = (bf16[18,1152]{1,0:T(8,128)(2,1)S(1)}, bf16[18,1152]{1,0:T(8,128)(2,1)S(1)}, u32[]{:S(2)}, u32[]{:S(2)}) collective-permute-start(bf16[18,1152]{1,0:T(8,128)(2,1)S(1)} %concatenate.22), channel_id=1, source_target_pairs={{0,96},{16,112},{32,64},{48,80},{64,32},{80,48},{96,0},{112,16},{1... | collective-permute-start | bytes 124424 | tf_op jit(solution)/shard_map/ppermute | solution.py:502
  7.9 0.8 %copy-start.5 = (bf16[32,1024]{1,0:T(8,128)(2,1)S(1)}, bf16[32,1024]{1,0:T(8,128)(2,1)}, u32[]{:S(2)}) copy-start(bf16[32,1024]{1,0:T(8,128)(2,1)} %param.7) | copy-start | bytes 196612
  7.9 0.9 %copy-start.3 = (f32[32,1024]{1,0:T(8,128)S(1)}, f32[32,1024]{1,0:T(8,128)}, u32[]{:S(2)}) copy-start(f32[32,1024]{1,0:T(8,128)} %param.12) | copy-start | bytes 393220
  9.0 7.7 %collective-permute-start = (f32[32,352]{1,0:T(8,128)S(1)}, f32[32,352]{1,0:T(8,128)S(1)}, u32[]{:S(2)}, u32[]{:S(2)}) collective-permute-start(f32[32,352]{1,0:T(8,128)S(1)} %get-tuple-element.25), channel_id=1, source_target_pairs={{0,1},{1,0},{2,3},{3,2},{4,5},{5,4},{6,7},{7,6},{8,9},{9,8},{10,11... | collective-permute-start | bytes 135176 | tf_op jit(solution)/shard_map/ppermute | solution.py:496
  9.1 7.6 %collective-permute-start.1 = (f32[32,352]{1,0:T(8,128)S(1)}, f32[32,352]{1,0:T(8,128)S(1)}, u32[]{:S(2)}, u32[]{:S(2)}) collective-permute-start(f32[32,352]{1,0:T(8,128)S(1)} %get-tuple-element.24), channel_id=1, source_target_pairs={{0,16},{1,2},{2,1},{3,4},{4,3},{5,6},{6,5},{7,8},{8,7},{9,10},{10,... | collective-permute-start | bytes 135176 | tf_op jit(solution)/shard_map/ppermute | solution.py:497
  13.3 5.4 %collective-permute-start.5 = (bf16[72,1152]{1,0:T(8,128)(2,1)S(1)}, bf16[72,1152]{1,0:T(8,128)(2,1)S(1)}, u32[]{:S(2)}, u32[]{:S(2)}) collective-permute-start(bf16[72,1152]{1,0:T(8,128)(2,1)S(1)} %pad_maximum_fusion.four_ref), channel_id=1, source_target_pairs={{0,16},{1,25},{2,18},{3,27},{4,20},{5,29},{6,22},{7,31},{8,24},{9,... | collective-permute-start | bytes 497672 | tf_op jit(solution)/shard_map/ppermute | solution.py:509
  14.9 0.7 %copy-start = (f32[3]{0:T(128)S(1)}, f32[3]{0:T(128)}, u32[]{:S(2)}) copy-start(f32[3]{0:T(128)} %param.13) | copy-start | bytes 40
  14.9 0.7 %copy-start.1 = (s32[72]{0:T(128)S(1)}, s32[72]{0:T(128)}, u32[]{:S(2)}) copy-start(s32[72]{0:T(128)} %param.10) | copy-start | bytes 868
  14.9 0.7 %copy-start.2 = (f32[72]{0:T(128)S(1)}, f32[72]{0:T(128)}, u32[]{:S(2)}) copy-start(f32[72]{0:T(128)} %param.9) | copy-start | bytes 868
